TPU v7x, 32 devices: a whole 2x2x4 slice. The times are simulated.
32 devices in a mesh: grp: 2 (over y), tp: 4 (over z), kv: 4 (over x, core).
Axes of the slice: x: 2, y: 2, z: 4, core: 2. Of those that a mesh axis runs over, the one named last changes fastest.
Arguments:
- queries: bfloat16 [64, 4, 16384], P('grp', None, 'kv'), parts along dimension 0, may hold values from -6 to 6
- fresh_keys: bfloat16 [64, 4, 1024], P(('grp', 'tp'), None, 'kv'), parts along dimension 0, may hold values from -6 to 6
- fresh_values: bfloat16 [64, 4, 1024], P(('grp', 'tp'), None, 'kv'), parts along dimension 0, may hold values from -6 to 6
- cache_keys: bfloat16 [16, 128, 4096], P(('grp', 'kv'), 'tp'), parts along dimension 0, may hold values from -6 to 6
- cache_values: bfloat16 [16, 128, 4096], P(('grp', 'kv'), 'tp'), parts along dimension 0, may hold values from -6 to 6
- page_counts: int32 [64], P('grp'), parts along dimension 0, may hold values from 1 to 64, 128 in all
- page_owner: int32 [16, 128], P(('grp', 'kv'), 'tp'), parts along dimension 0, may hold values from 0 to 3, as said below
- out_weight: bfloat16 [16384, 16384], P('kv', 'tp'), may hold values from -0.046875 to 0.046875
Outputs:
- attention_out: bfloat16 [64, 4, 16384], P(('grp', 'kv'), None, 'tp'), parts along dimension 0
- handed_keys: bfloat16 [16, 256, 4096], P(('grp', 'kv'), 'tp'), parts along dimension 0
- handed_values: bfloat16 [16, 256, 4096], P(('grp', 'kv'), 'tp'), parts along dimension 0
- slot_rows: int32 [16, 256], P(('grp', 'kv'), 'tp'), parts along dimension 0
There are 2 independent parts, one for each index of `grp`. A program takes and returns all parts, laid end to end along the dimension named above; an argument that names none is the same for every part. Nothing has to cross between parts.
Inputs may be any that keep to these rules, and one draw needn't show every extreme that they name: `page_owner`: for each KV head and each prefill owner's block of 32 consecutive pages, no decode owner is listed more than 16 times; for each KV head one decode owner is listed exactly 16 times in every block. `page_counts`: the counts sum to 128; the pages of request r follow those of the requests before it in prefill order; the largest count is 64.
All inputs are finite; a program needn't handle non-finite values.
Results may differ from a plain program's by a relative error of at most 0.007.
Values may be sent and summed in bfloat16 or wider, within the bound.
No kernel may reach another device: no remote copies, remote signals or barrier semaphores. Data moves between devices by JAX's collectives and lax.ppermute only.
A program may use at most 128 MiB of HBM per device.

v0:
```python
import jax
import jax.numpy as jnp
from jax import lax
from jax.sharding import PartitionSpec as P

HD = 128


NEGATIVE = -1e30


def combine_parts(earlier, later):
    max_first, total_first, numer_first = earlier
    max_second, total_second, numer_second = later
    largest = jnp.maximum(max_first, max_second)
    scale_first = jnp.exp(max_first - largest)
    scale_second = jnp.exp(max_second - largest)
    widened = (
        numer_first.reshape(max_first.shape + (-1,)) * scale_first[..., None]
        + numer_second.reshape(max_second.shape + (-1,)) * scale_second[..., None]
    )
    return (
        largest,
        total_first * scale_first + total_second * scale_second,
        widened.reshape(numer_first.shape),
    )


def page_partials(key_pages, value_pages, page_rows, queries, head_dim):
    highest = lax.Precision.HIGHEST
    head_count, page_total, page_width = key_pages.shape
    page_len = page_width // head_dim
    row_count, step_count, query_width = queries.shape
    group_size = query_width // (head_count * head_dim)
    score_scale = head_dim ** (-0.5)
    query_heads = queries.reshape(row_count, step_count, head_count, group_size, head_dim)
    row_ids = jnp.arange(row_count, dtype=jnp.int32)
    maxima, totals, numers = ([], [], [])
    for head_index in range(head_count):
        owned = page_rows[head_index]
        is_valid = owned >= 0
        safe_rows = jnp.maximum(owned, 0)
        chosen = query_heads[:, :, head_index].reshape(
            row_count, step_count * group_size, head_dim
        )[safe_rows]
        key_block = key_pages[head_index].reshape(page_total, page_len, head_dim)
        value_block = value_pages[head_index].reshape(page_total, page_len, head_dim)
        scores = (
            jnp.einsum("pqd,ptd->pqt", chosen, key_block, preferred_element_type=jnp.float32)
            * score_scale
        )
        page_max = jnp.max(scores, axis=2)
        weights = jnp.exp(scores - page_max[:, :, None]).astype(jnp.bfloat16)
        page_sum = jnp.sum(weights.astype(jnp.float32), axis=2)
        page_numer = jnp.einsum(
            "pqt,ptd->pqd", weights, value_block, preferred_element_type=jnp.float32
        )
        page_max = jnp.where(is_valid[:, None], page_max, NEGATIVE)
        member = (safe_rows[None, :] == row_ids[:, None]) & is_valid[None, :]
        row_max = jnp.max(jnp.where(member[:, :, None], page_max[None, :, :], NEGATIVE), axis=1)
        factor = jnp.exp(page_max - row_max[safe_rows])
        member_weight = member.astype(jnp.float32)
        row_sum = jnp.dot(member_weight, page_sum * factor, precision=highest)
        row_numer = jnp.einsum(
            "rp,pqd->rqd", member_weight, page_numer * factor[:, :, None], precision=highest
        )
        maxima.append(row_max.reshape(row_count, step_count, group_size))
        totals.append(row_sum.reshape(row_count, step_count, group_size))
        numers.append(row_numer.reshape(row_count, step_count, group_size, head_dim))
    return (
        jnp.stack(maxima, axis=2),
        jnp.stack(totals, axis=2),
        jnp.stack(numers, axis=2).reshape(row_count, step_count, -1),
    )


def fresh_partials(queries_own, fresh_keys, fresh_values, head_dim):
    row_count, step_count, query_width = queries_own.shape
    head_count = fresh_keys.shape[2] // head_dim
    group_size = query_width // (head_count * head_dim)
    query_heads = queries_own.reshape(row_count, step_count, head_count, group_size, head_dim)
    key_heads = fresh_keys.reshape(row_count, step_count, head_count, head_dim)
    value_heads = fresh_values.reshape(row_count, step_count, head_count, head_dim)
    scores = jnp.einsum(
        "rshgd,ruhd->rshgu", query_heads, key_heads, preferred_element_type=jnp.float32
    ) * head_dim ** (-0.5)
    steps_seen = jnp.arange(step_count)
    causal = steps_seen[:, None] >= steps_seen[None, :]
    scores = jnp.where(causal[None, :, None, None, :], scores, NEGATIVE)
    fresh_max = jnp.max(scores, axis=4)
    weights = jnp.exp(scores - fresh_max[..., None]).astype(jnp.bfloat16)
    fresh_sum = jnp.sum(weights.astype(jnp.float32), axis=4)
    fresh_numer = jnp.einsum(
        "rshgu,ruhd->rshgd", weights, value_heads, preferred_element_type=jnp.float32
    )
    return (fresh_max, fresh_sum, fresh_numer.reshape(row_count, step_count, -1))


def place_slots(buffer, slot_index, entries):
    return buffer.at[slot_index].set(entries)


def pick_rows(table, index_list):
    return table[index_list]


def body(
    queries, fresh_keys, fresh_values, cache_keys, cache_values, page_counts, page_owner, out_weight
):
    tp_size = lax.axis_size("tp")
    tp_index = lax.axis_index("tp")
    head_count, pages_here, page_width = cache_keys.shape
    slot_cap = max(2, (2 * pages_here + tp_size - 1) // tp_size)
    slot_count = tp_size * slot_cap
    row_ends = jnp.cumsum(page_counts)
    global_pages = tp_index * pages_here + jnp.arange(pages_here, dtype=jnp.int32)
    page_row = jnp.sum((row_ends[None, :] <= global_pages[:, None]).astype(jnp.int32), axis=1)
    page_rows = jnp.broadcast_to(page_row, (head_count, pages_here))
    owner_ids = jnp.arange(tp_size, dtype=jnp.int32)
    onehot = (page_owner[:, :, None] == owner_ids[None, None, :]).astype(jnp.int32)
    page_rank = jnp.sum((jnp.cumsum(onehot, axis=1) - onehot) * onehot, axis=2)
    slot_index = page_owner * slot_cap + page_rank
    empty_slots = jnp.full((head_count, slot_count), pages_here, jnp.int32)
    local_ids = jnp.broadcast_to(jnp.arange(pages_here, dtype=jnp.int32), (head_count, pages_here))
    sources = jax.vmap(place_slots)(empty_slots, slot_index, local_ids)
    blank_page = jnp.zeros((head_count, 1, page_width), jnp.bfloat16)
    send_keys = jax.vmap(pick_rows)(jnp.concatenate([cache_keys, blank_page], axis=1), sources)
    send_values = jax.vmap(pick_rows)(jnp.concatenate([cache_values, blank_page], axis=1), sources)
    row_table = jnp.concatenate([page_rows, jnp.full((head_count, 1), -1, jnp.int32)], axis=1)
    send_rows = jax.vmap(pick_rows)(row_table, sources).astype(jnp.bfloat16)
    got_keys, got_values, got_rows = (
        lax.all_to_all(
            send_keys.reshape(head_count, tp_size, slot_cap, page_width),
            "tp",
            split_axis=1,
            concat_axis=1,
            tiled=True,
        ),
        lax.all_to_all(
            send_values.reshape(head_count, tp_size, slot_cap, page_width),
            "tp",
            split_axis=1,
            concat_axis=1,
            tiled=True,
        ),
        lax.all_to_all(
            send_rows.reshape(head_count, tp_size, slot_cap),
            "tp",
            split_axis=1,
            concat_axis=1,
            tiled=True,
        ),
    )
    slot_keys = got_keys.reshape(head_count, slot_count, page_width)
    slot_values = got_values.reshape(head_count, slot_count, page_width)
    slot_rows = got_rows.reshape(head_count, slot_count).astype(jnp.int32)
    partial_value = page_partials(cache_keys, cache_values, page_rows, queries, HD)
    own_count = fresh_keys.shape[0]
    own_start = tp_index * own_count
    queries_own = lax.dynamic_slice_in_dim(queries, own_start, own_count, 0)
    fresh_parts = fresh_partials(queries_own, fresh_keys, fresh_values, HD)
    padded_parts = (
        lax.dynamic_update_slice_in_dim(
            jnp.full(partial_value[0].shape, NEGATIVE, jnp.float32), fresh_parts[0], own_start, 0
        ),
        lax.dynamic_update_slice_in_dim(
            jnp.zeros(partial_value[1].shape, jnp.float32), fresh_parts[1], own_start, 0
        ),
        lax.dynamic_update_slice_in_dim(
            jnp.zeros(partial_value[2].shape, jnp.float32), fresh_parts[2], own_start, 0
        ),
    )
    partial_value = combine_parts(partial_value, padded_parts)
    row_count, step_count = (queries.shape[0], queries.shape[1])
    largest = lax.pmax(partial_value[0], "tp")
    factor = jnp.exp(partial_value[0] - largest)
    scaled_numer = (partial_value[2].reshape(factor.shape + (-1,)) * factor[..., None]).reshape(
        partial_value[2].shape
    )
    share_sum, share_numer = (
        lax.psum_scatter(partial_value[1] * factor, "tp", scatter_dimension=0, tiled=True),
        lax.psum_scatter(scaled_numer, "tp", scatter_dimension=0, tiled=True),
    )
    share_rows = (share_numer.reshape(share_sum.shape + (-1,)) / share_sum[..., None]).astype(
        jnp.bfloat16
    )
    attended = lax.all_gather(
        share_rows.reshape(share_sum.shape[0], step_count, -1), "tp", axis=0, tiled=True
    )
    block_rows = row_count // lax.axis_size("kv") * lax.axis_size("kv")
    flat_rows = attended.reshape(block_rows * step_count, -1)
    product = jnp.dot(flat_rows, out_weight, preferred_element_type=jnp.float32)
    attention_out = lax.psum_scatter(
        product.reshape(block_rows, step_count, -1), "kv", scatter_dimension=0, tiled=True
    ).astype(jnp.bfloat16)
    return (attention_out, slot_keys, slot_values, slot_rows)


def solution(mesh):
    return jax.shard_map(
        body,
        mesh=mesh,
        in_specs=(
            P("grp", None, "kv"),
            P(("grp", "tp"), None, "kv"),
            P(("grp", "tp"), None, "kv"),
            P(("grp", "kv"), "tp", None),
            P(("grp", "kv"), "tp", None),
            P("grp"),
            P(("grp", "kv"), "tp"),
            P("kv", "tp"),
        ),
        out_specs=(
            P(("grp", "kv"), None, "tp"),
            P(("grp", "kv"), "tp", None),
            P(("grp", "kv"), "tp", None),
            P(("grp", "kv"), "tp"),
        ),
        check_vma=False,
    )
```

profile of v0, /device:TPU:0, one launch (start us, length us, event | category | flops | bytes accessed | tf_op | source)
XLA Modules:
  0.0 243.4 jit_solution(13687530942337816964)
XLA Ops:
  7.2 0.7 copy.128
  8.4 2.2 reshape.222
  10.6 0.3 fusion.33
  11.1 0.6 gather_fusion.2
  11.7 0.6 gather_fusion
  12.5 0.4 fusion.34
  12.9 0.4 fusion.35
  13.4 0.3 select_reduce_fusion.1
  13.7 0.6 gather_fusion.3
  14.4 0.6 gather_fusion.1
  15.3 1.0 constant_dynamic-slice_fusion.1
  16.3 0.3 reshape.305
  16.6 0.8 fusion.36
  17.7 0.3 dynamic_update_slice.9
  18.0 22.5 %pmax.7 = f32[32,4,2,16]{0,3,1,2:T(8,128)S(1)} all-reduce(f32[32,4,2,16]{0,3,1,2:T(8,128)S(1)} %fusion.11), channel_id=1, replica_groups=mesh['grp'=2,'tp'=4,'kv'=4] {'tp'}, use_global_device_ids=true, to_apply=%region_7.8 | all-reduce | flops 4096 | bytes 32768 | tf_op jit(solution)/shard_map/pmax | solution.py:175
  40.6 0.2 fusion.15
  40.8 0.2 fusion.17
  41.1 0.3 dynamic_update_slice.11
  41.6 2.0 mul.109
  43.5 1.7 mul.110
  45.3 1.1 slice_bitcast_fusion.2
  46.4 1.2 convolution_multiply_fusion
  47.7 1.3 fusion.4
  49.0 0.5 convolution_multiply_fusion.1
  49.6 1.3 fusion.6
  50.8 0.7 maximum_multiply_fusion
  51.6 2.5 %copy.137 = f32[32,4,2,16,128]{4,3,2,0,1:T(8,128)} copy(f32[32,4,2,16,128]{4,0,3,1,2:T(8,128)S(1)} %maximum_multiply_fusion) | data formatting | bytes 4194304 | tf_op jit(solution)/shard_map/mul | solution.py:19
  54.1 2.8 %mul.105 = f32[32,4,4096]{2,0,1:T(8,128)} reshape(f32[32,4,2,16,128]{4,3,2,0,1:T(8,128)} %copy.137) | data formatting | bytes 4194304 | tf_op jit(solution)/shard_map/mul | solution.py:19
  56.8 0.3 convolution_bitcast_fusion
  57.4 1.9 mul.106
  59.3 2.7 %mul.107 = f32[32,4,4096]{2,0,1:T(8,128)} reshape(f32[32,4,2,16,128]{4,3,2,0,1:T(8,128)} %mul.106) | data formatting | bytes 4194304 | tf_op jit(solution)/shard_map/mul | solution.py:20
  62.3 1.3 copy-done.2
  63.7 3.6 %add_multiply_fusion = f32[32,4,4096]{2,0,1:T(8,128)} fusion(f32[32,4,4096]{2,0,1:T(8,128)S(1)} %mul.110, f32[32,4,4096]{2,0,1:T(8,128)S(1)} %copy-done.2, f32[32,4,4096]{2,0,1:T(8,128)S(1)} %constant_dynamic-update-slice_fusion, f32[32,4,4096]{2,0,1:T(8,128)} %mul.107), kind=kLoop, calls=%fused_computation.11 | loop fusion | flops 1572864 | bytes 10485760 | tf_op jit(solution)/shard_map/mul | solution.py:177
  67.5 0.4 copy-done.19
  67.9 0.6 dynamic-slice
  69.1 22.5 %all-reduce.3 = f32[32,4,2,16]{3,1,2,0:T(4,128)S(1)} all-reduce(f32[32,4,2,16]{3,1,2,0:T(4,128)S(1)} %copy.145), channel_id=3, replica_groups=mesh['grp'=2,'tp'=4,'kv'=4] {'tp'}, use_global_device_ids=true, to_apply=%region_12.13.clone | all-reduce | flops 4096 | bytes 32768
  91.7 20.9 %reduce-scatter.3.cloned.1.call-done = f32[8,4,4096]{2,0,1:T(8,128)} async-done(((f32[32,4,4096]{2,0,1:T(8,128)}), f32[8,4,4096]{2,0,1:T(8,128)}) %reduce-scatter.3.cloned.1.call-update) | async-done | bytes 524304 | tf_op jit(solution)/shard_map/reduce_scatter | solution.py:182
  112.8 1.9 divide_convert_fusion
  114.7 0.3 reduce-scatter.5.cloned.1.call-start
  115.0 28.2 %all-gather.2.cloned.1.call-done = bf16[32,4,4096]{2,0,1:T(8,128)(2,1)} async-done(((bf16[8,4,4096]{2,0,1:T(8,128)(2,1)}), bf16[32,4,4096]{2,0,1:T(8,128)(2,1)}) %all-gather.2.cloned.1.call-update) | async-done | bytes 1048592 | tf_op jit(solution)/shard_map/all_gather | solution.py:187
  143.2 16.7 %fusion = f32[32,4,4096]{2,0,1:T(8,128)} fusion(bf16[32,4,4096]{2,0,1:T(8,128)(2,1)} %all-gather.2.cloned.1.call-done, bf16[4096,4096]{1,0:T(8,128)(2,1)} %param.15), kind=kOutput, calls=%fused_computation.8 | convolution fusion | flops 4294967296 | bytes 36700160 | tf_op jit(solution)/shard_map/dot_general | solution.py:192
  159.9 0.7 copy-done.15
  161.1 3.5 %scatter_fusion = s32[2,64]{1,0:T(2,128)S(1)} fusion(s32[2,64]{1,0:T(2,128)S(1)} %broadcast_in_dim.125, s32[64]{0:T(128)S(1)} %reshape.282, s32[64]{0:T(128)S(1)} %reshape.284), kind=kCustom, calls=%fused_computation.7 | custom fusion | bytes 1280 | tf_op jit(solution)/shard_map/vmap()/scatter | solution.py:100
  164.7 1.5 gather_fusion.6
  166.3 0.6 copy.153
  166.9 3.2 %all-to-all-start.2 = ((bf16[2,4,16]{2,0,1:T(2,128)(2,1)}), bf16[2,4,16]{2,0,1:T(2,128)(2,1)S(1)}, u32[]{:S(2)}, u32[]{:S(2)}) async-start(bf16[2,4,16]{2,0,1:T(2,128)(2,1)} %copy.153), calls=%async_computation.4 | async-start | bytes 4096 | tf_op jit(solution)/shard_map/all_to_all | solution.py:146
  170.1 0.5 copy.147
  170.7 0.5 concatenate.11
  171.2 2.5 %gather_fusion.4 = bf16[128,4096]{1,0:T(8,128)(2,1)S(1)} fusion(bf16[2,33,4096]{2,0,1:T(2,128)(2,1)S(1)} %concatenate.11, s32[128]{0:T(128)S(1)} %reshape.264), kind=kCustom, calls=%fused_computation.4 | custom fusion | bytes 2098176 | tf_op jit(solution)/shard_map/vmap()/gather | solution.py:104
  173.8 1.1 copy.148
  174.8 0.7 all-to-all-done.2
  175.5 4.3 %all-to-all-start = ((bf16[2,4,16,4096]{3,2,0,1:T(8,128)(2,1)}), bf16[2,4,16,4096]{3,2,0,1:T(8,128)(2,1)S(1)}, u32[]{:S(2)}, u32[]{:S(2)}) async-start(bf16[2,4,16,4096]{3,2,0,1:T(8,128)(2,1)} %copy.148), calls=%async_computation.2 | async-start | bytes 2097152 | tf_op jit(solution)/shard_map/all_to_all | solution.py:132
  179.9 0.5 copy.150
  180.4 0.6 concatenate.12
  181.0 2.5 %gather_fusion.5 = bf16[128,4096]{1,0:T(8,128)(2,1)S(1)} fusion(bf16[2,33,4096]{2,0,1:T(2,128)(2,1)S(1)} %concatenate.12, s32[128]{0:T(128)S(1)} %reshape.264), kind=kCustom, calls=%fused_computation.5 | custom fusion | bytes 2098176 | tf_op jit(solution)/shard_map/vmap()/gather | solution.py:104
  183.5 1.1 copy.151
  184.6 20.6 %all-to-all-done = bf16[2,4,16,4096]{3,2,0,1:T(8,128)(2,1)S(1)} async-done(((bf16[2,4,16,4096]{3,2,0,1:T(8,128)(2,1)}), bf16[2,4,16,4096]{3,2,0,1:T(8,128)(2,1)S(1)}, u32[]{:S(2)}, u32[]{:S(2)}) %all-to-all-start) | async-done | bytes 1048608 | tf_op jit(solution)/shard_map/all_to_all | solution.py:132
  205.2 3.5 %all-to-all-start.1 = ((bf16[2,4,16,4096]{3,2,0,1:T(8,128)(2,1)}), bf16[2,4,16,4096]{3,2,0,1:T(8,128)(2,1)S(1)}, u32[]{:S(2)}, u32[]{:S(2)}) async-start(bf16[2,4,16,4096]{3,2,0,1:T(8,128)(2,1)} %copy.151), calls=%async_computation.3 | async-start | bytes 2097152 | tf_op jit(solution)/shard_map/all_to_all | solution.py:139
  208.7 0.6 reshape.231
  209.4 1.1 copy.149
  210.4 23.5 %all-to-all-done.1 = bf16[2,4,16,4096]{3,2,0,1:T(8,128)(2,1)S(1)} async-done(((bf16[2,4,16,4096]{3,2,0,1:T(8,128)(2,1)}), bf16[2,4,16,4096]{3,2,0,1:T(8,128)(2,1)S(1)}, u32[]{:S(2)}, u32[]{:S(2)}) %all-to-all-start.1) | async-done | bytes 1048608 | tf_op jit(solution)/shard_map/all_to_all | solution.py:139
  233.9 1.0 copy.152
  234.9 1.1 convert_element_type.54
  236.0 0.9 copy.155
  (95 shorter events, 3.4 us)
Async XLA Ops:
  7.2 49.7 %copy-start = (bf16[8,4,256]{2,1,0:T(4,128)(2,1)S(1)}, bf16[8,4,256]{2,1,0:T(4,128)(2,1)}, u32[]{:S(2)}) copy-start(bf16[8,4,256]{2,1,0:T(4,128)(2,1)} %param.10) | copy-start | bytes 49156
  7.2 105.4 %reduce-scatter.3.cloned.1.call-start = ((), (), s32[]{:S(2)}) async-start(), calls=%async_computation.5 | async-start | bytes 2621440 | tf_op jit(solution)/shard_map/reduce_scatter | solution.py:182
  8.3 2.6 %copy-start.17 = (s32[32]{0:T(128)}, s32[32]{0:T(128)S(1)}, u32[]{:S(2)}) copy-start(s32[32]{0:T(128)S(1)} %convert_reduce_fusion.3) | copy-start | bytes 388
  8.3 4.1 %copy-start.12 = (s32[32]{0:T(128)}, s32[32]{0:T(128)S(1)}, u32[]{:S(2)}) copy-start(s32[32]{0:T(128)S(1)} %broadcast_maximum_fusion) | copy-start | bytes 388
  8.4 4.9 %copy-start.9 = (pred[32]{0:T(512)(128)(4,1)}, pred[32]{0:T(512)(128)(4,1)S(1)}, u32[]{:S(2)}) copy-start(pred[32]{0:T(512)(128)(4,1)S(1)} %broadcast_compare_fusion) | copy-start | bytes 100
  8.4 2.6 %copy-start.3 = (bf16[2,32,4096]{2,1,0:T(8,128)(2,1)S(1)}, bf16[2,32,4096]{2,1,0:T(8,128)(2,1)}, u32[]{:S(2)}) copy-start(bf16[2,32,4096]{2,1,0:T(8,128)(2,1)} %param.11) | copy-start | bytes 1572868
  12.9 3.8 %copy-start.16 = (bf16[8,4,256]{2,1,0:T(4,128)(2,1)S(1)}, bf16[8,4,256]{2,1,0:T(4,128)(2,1)}, u32[]{:S(2)}) copy-start(bf16[8,4,256]{2,1,0:T(4,128)(2,1)} %param.9) | copy-start | bytes 49156
  13.7 26.9 %copy-start.10 = (pred[32]{0:T(512)(128)(4,1)S(1)}, pred[32]{0:T(512)(128)(4,1)}, u32[]{:S(2)}) copy-start(pred[32]{0:T(512)(128)(4,1)} %copy-done.9) | copy-start | bytes 100
  13.7 26.9 %copy-start.13 = (s32[32]{0:T(128)S(1)}, s32[32]{0:T(128)}, u32[]{:S(2)}) copy-start(s32[32]{0:T(128)} %copy-done.12) | copy-start | bytes 388
  40.6 0.8 copy-start.6
  40.6 0.8 copy-start.8
  45.3 2.4 copy-start.11
  45.3 2.4 copy-start.14
  46.4 2.6 %copy-start.7 = (f32[32,64]{1,0:T(8,128)S(1)}, f32[32,64]{1,0:T(8,128)}, u32[]{:S(2)}) copy-start(f32[32,64]{1,0:T(8,128)} %copy-done.6) | copy-start | bytes 24580
  62.1 1.6 copy-start.2
  67.2 0.7 copy-start.19
  67.3 75.9 %all-gather.2.cloned.1.call-start = ((), (), s32[]{:S(2)}) async-start(), calls=%async_computation.6 | async-start | bytes 1310720 | tf_op jit(solution)/shard_map/all_gather | solution.py:187
  114.7 120.2 %reduce-scatter.5.cloned.1.call-start = ((), (), s32[]{:S(2)}) async-start(), calls=%async_computation.7 | async-start | bytes 2621440 | tf_op jit(solution)/shard_map/reduce_scatter | solution.py:193
  159.9 0.7 copy-start.15
  159.9 4.8 %copy-start.18 = (s32[32]{0:T(128)S(1)}, s32[32]{0:T(128)}, u32[]{:S(2)}) copy-start(s32[32]{0:T(128)} %copy-done.17) | copy-start | bytes 388
  160.6 9.5 %copy-start.4 = (bf16[2,32,4096]{2,1,0:T(8,128)(2,1)S(1)}, bf16[2,32,4096]{2,1,0:T(8,128)(2,1)}, u32[]{:S(2)}) copy-start(bf16[2,32,4096]{2,1,0:T(8,128)(2,1)} %param.11) | copy-start | bytes 1572868
  166.9 8.7 %all-to-all-start.2 = ((bf16[2,4,16]{2,0,1:T(2,128)(2,1)}), bf16[2,4,16]{2,0,1:T(2,128)(2,1)S(1)}, u32[]{:S(2)}, u32[]{:S(2)}) async-start(bf16[2,4,16]{2,0,1:T(2,128)(2,1)} %copy.153), calls=%async_computation.4 | async-start | bytes 4096 | tf_op jit(solution)/shard_map/all_to_all | solution.py:146
  173.7 6.1 %copy-start.5 = (bf16[2,32,4096]{2,1,0:T(8,128)(2,1)S(1)}, bf16[2,32,4096]{2,1,0:T(8,128)(2,1)}, u32[]{:S(2)}) copy-start(bf16[2,32,4096]{2,1,0:T(8,128)(2,1)} %param.12) | copy-start | bytes 1572868
  175.5 29.6 %all-to-all-start = ((bf16[2,4,16,4096]{3,2,0,1:T(8,128)(2,1)}), bf16[2,4,16,4096]{3,2,0,1:T(8,128)(2,1)S(1)}, u32[]{:S(2)}, u32[]{:S(2)}) async-start(bf16[2,4,16,4096]{3,2,0,1:T(8,128)(2,1)} %copy.148), calls=%async_computation.2 | async-start | bytes 2097152 | tf_op jit(solution)/shard_map/all_to_all | solution.py:132
  205.2 28.7 %all-to-all-start.1 = ((bf16[2,4,16,4096]{3,2,0,1:T(8,128)(2,1)}), bf16[2,4,16,4096]{3,2,0,1:T(8,128)(2,1)S(1)}, u32[]{:S(2)}, u32[]{:S(2)}) async-start(bf16[2,4,16,4096]{3,2,0,1:T(8,128)(2,1)} %copy.151), calls=%async_computation.3 | async-start | bytes 2097152 | tf_op jit(solution)/shard_map/all_to_all | solution.py:139
  209.4 27.6 %copy-start.1 = (bf16[8,4,256]{2,1,0:T(4,128)(2,1)S(1)}, bf16[8,4,256]{2,1,0:T(4,128)(2,1)}, u32[]{:S(2)}) copy-start(bf16[8,4,256]{2,1,0:T(4,128)(2,1)} %param.10) | copy-start | bytes 49156
Sparse Core Ops, SparseCore 0:
  67.4 45.1 reduce-scatter.2
  114.8 28.2 all-gather.1
  160.0 30.9 reduce-scatter.4
where the time goes:
time: 244 us; the launch traced here: 243 us
  waiting for transfers between devices  93.9 us (38%)
  local copies, waits for them, and re-layouts  46 us (19%)
  blocking collectives  45 us (18%)
  matrix products  23.3 us (10%)
  between operations  15.1 us (6%)
  starting transfers between devices  11.4 us (5%)
  other arithmetic  8.8 us (4%)
    all_gather x1, waiting for transfers between devices, body(): lax.all_gather(share_rows.reshape(share_sum.shape[0], step_count, -1), 't...  28.2 us
    all_to_all x1, waiting for transfers between devices, body(): lax.all_to_all(send_values.reshape(head_count, tp_size, slot_cap, page_wi...  23.5 us
    pmax x1, blocking collectives, body(): largest = lax.pmax(partial_value[0], 'tp')  22.5 us
    unnamed x1, blocking collectives  22.5 us
    reduce_scatter x1, waiting for transfers between devices, body(): lax.psum_scatter(scaled_numer, 'tp', scatter_dimension=0, tiled=True)  20.9 us
    all_to_all x1, waiting for transfers between devices, body(): lax.all_to_all(send_keys.reshape(head_count, tp_size, slot_cap, page_widt...  20.6 us
    dot_general x1, matrix products, body(): product = jnp.dot(flat_rows, out_weight, preferred_element_type=jnp.float32)  16.7 us
    gather x4, local copies, waits for them, and re-layouts, pick_rows(): return table[index_list]  6.63 us
  transfers between devices with their start and end apart: 6, of which 5 were waited for; matrix products, arithmetic and copies ran while one was open for 8% of the time, Pallas kernels for 0%

commit v1 on v0

v1 whole, which is shorter than its diff:
```python
import functools

import jax
import jax.numpy as jnp
from jax import lax
from jax.experimental import pallas as pl
from jax.experimental.pallas import tpu as pltpu
from jax.sharding import PartitionSpec as P

HD = 128
LANES = 128
NEGATIVE = -1e30
HIGHEST = lax.Precision.HIGHEST
VMEM_BYTES = 24 * 1024 * 1024


def round_up(value, step):
    return -(-value // step) * step


def flip(size, bit):
    return [(i, i ^ bit) for i in range(size)]


def params():
    return pltpu.CompilerParams(vmem_limit_bytes=VMEM_BYTES)


def hand_kernel(cap, owner_ref, key_ref, value_ref, send_key_ref, send_value_ref):
    dest_count, head_count = send_key_ref.shape[0], send_key_ref.shape[1]
    page_count, width = key_ref.shape[1], key_ref.shape[2]
    dest_rows = max(8, dest_count)
    step = min(width, 1024)
    earlier = (
        lax.broadcasted_iota(jnp.int32, (page_count, page_count), 0)
        < lax.broadcasted_iota(jnp.int32, (page_count, page_count), 1)
    ).astype(jnp.bfloat16)
    for head in range(head_count):
        owner = owner_ref[head : head + 1, :]
        listed = (
            lax.broadcasted_iota(jnp.int32, (dest_rows, page_count), 0) == owner
        ).astype(jnp.float32)
        before = jnp.dot(
            listed.astype(jnp.bfloat16), earlier, preferred_element_type=jnp.float32
        )
        rank = jnp.sum(before * listed, axis=0, keepdims=True).astype(jnp.int32)
        slot = owner * cap + rank
        pick = (
            lax.broadcasted_iota(jnp.int32, (dest_count * cap, page_count), 0) == slot
        ).astype(jnp.bfloat16)
        for source, target in ((key_ref, send_key_ref), (value_ref, send_value_ref)):
            for start in range(0, width, step):
                placed = jnp.dot(
                    pick,
                    source[head, :, start : start + step],
                    preferred_element_type=jnp.float32,
                ).astype(jnp.bfloat16)
                for dest in range(dest_count):
                    target[dest, head, :, start : start + step] = placed[
                        dest * cap : (dest + 1) * cap
                    ]


def place_pages(page_owner, cache_keys, cache_values, dest_count, cap):
    head_count, _, width = cache_keys.shape
    shape = jax.ShapeDtypeStruct((dest_count, head_count, cap, width), jnp.bfloat16)
    return pl.pallas_call(
        functools.partial(hand_kernel, cap),
        out_shape=(shape, shape),
        compiler_params=params(),
        name="place_pages",
    )(page_owner, cache_keys, cache_values)


def list_slot_rows(page_owner, row_ends, tp_index, tp_size, cap):
    head_count, pages_here = page_owner.shape
    owners = lax.all_gather(page_owner, "tp", axis=1, tiled=False)
    ids = jnp.arange(pages_here, dtype=jnp.int32)
    same = (owners[..., :, None] == owners[..., None, :]) & (ids[:, None] < ids[None, :])
    rank = jnp.sum(same.astype(jnp.int32), axis=2)
    page_ids = jnp.arange(tp_size * pages_here, dtype=jnp.int32)
    page_row = jnp.sum((row_ends[None, :] <= page_ids[:, None]).astype(jnp.int32), axis=1)
    here = (owners == tp_index)[..., None, :] & (
        rank[..., None, :] == jnp.arange(cap, dtype=jnp.int32)[:, None]
    )
    marks = jnp.where(here, page_row.reshape(tp_size, 1, pages_here) + 1, 0)
    return (jnp.sum(marks, axis=3) - 1).reshape(head_count, tp_size * cap)


def attend_kernel(
    steps, has_earlier, last, chunks, *refs
):
    query_ref, tokens_ref, member_ref, member_t_ref = refs[:4]
    refs = refs[4:]
    if has_earlier:
        early_max_ref, early_total_ref, early_numer_ref = refs[:3]
        refs = refs[3:]
    if last:
        payload_refs, refs = refs[:chunks], refs[chunks:]
    else:
        out_max_ref, out_total_ref, out_numer_ref = refs[:3]
        refs = refs[3:]
    chosen, numers, high, low = refs

    row_lines, query_width = query_ref.shape
    group = query_width // HD
    member_lines = member_ref.shape[0]
    held, page_len = tokens_ref.shape[0] // 2, tokens_ref.shape[1]
    pages = held - 1
    page_lines = pages * steps
    used_lines = page_lines + page_len
    scale = HD ** (-0.5)
    lane = lax.broadcasted_iota(jnp.int32, (1, LANES), 1)

    chosen[...] = jnp.dot(
        member_ref[...], query_ref[...], preferred_element_type=jnp.float32
    ).astype(jnp.bfloat16)

    maxima, totals = [], []

    def one_block(first_line, lines, keys, values, mask):
        queries = jnp.concatenate(
            [
                chosen[first_line : first_line + lines, g * HD : (g + 1) * HD]
                for g in range(group)
            ],
            axis=0,
        )
        scores = (
            lax.dot_general(
                queries, keys, (((1,), (1,)), ((), ())), preferred_element_type=jnp.float32
            )
            * scale
        )
        scores = jnp.where(mask, scores, NEGATIVE)
        largest = jnp.max(scores, axis=1, keepdims=True)
        weights = jnp.exp(scores - largest).astype(jnp.bfloat16)
        total = jnp.sum(weights.astype(jnp.float32), axis=1, keepdims=True)
        numer = jnp.dot(weights, values, preferred_element_type=jnp.float32)
        block_max = jnp.zeros((lines, LANES), jnp.float32)
        block_total = jnp.zeros((lines, LANES), jnp.float32)
        for g in range(group):
            part = slice(g * lines, (g + 1) * lines)
            block_max = jnp.where(lane == g, largest[part], block_max)
            block_total = jnp.where(lane == g, total[part], block_total)
            numers[first_line : first_line + lines, g * HD : (g + 1) * HD] = numer[part]
        maxima.append(block_max)
        totals.append(block_total)

    batch = min(pages, max(1, 128 // page_len))
    lines = batch * steps
    line = lax.broadcasted_iota(jnp.int32, (group * lines, batch * page_len), 0)
    token = lax.broadcasted_iota(jnp.int32, (group * lines, batch * page_len), 1)
    mask = (line % lines) // steps == token // page_len
    for first in range(0, pages, batch):
        one_block(
            first * steps,
            lines,
            tokens_ref[first : first + batch].reshape(batch * page_len, HD),
            tokens_ref[held + first : held + first + batch].reshape(batch * page_len, HD),
            mask,
        )
    line = lax.broadcasted_iota(jnp.int32, (group * page_len, page_len), 0) % page_len
    token = lax.broadcasted_iota(jnp.int32, (group * page_len, page_len), 1)
    mask = (line // steps == token // steps) & (token % steps <= line % steps)
    one_block(page_lines, page_len, tokens_ref[pages], tokens_ref[held + pages], mask)

    spare = member_lines - used_lines
    if spare:
        maxima.append(jnp.zeros((spare, LANES), jnp.float32))
        totals.append(jnp.zeros((spare, LANES), jnp.float32))
    line_max = jnp.concatenate(maxima, axis=0)
    line_total = jnp.concatenate(totals, axis=0)

    member_t = member_t_ref[...]
    is_member = member_t > 0
    line_max_t = jnp.transpose(line_max)
    row_max = jnp.full((row_lines, LANES), NEGATIVE, jnp.float32)
    for g in range(group):
        best = jnp.max(
            jnp.where(is_member, line_max_t[g : g + 1, :], NEGATIVE), axis=1, keepdims=True
        )
        row_max = jnp.where(lane == g, best, row_max)
    spread = jnp.dot(
        member_ref[...].astype(jnp.float32),
        row_max,
        precision=HIGHEST,
        preferred_element_type=jnp.float32,
    )
    factor = jnp.exp(jnp.minimum(line_max - spread, 0.0))
    row_total = jnp.dot(
        member_t.astype(jnp.float32),
        line_total * factor,
        precision=HIGHEST,
        preferred_element_type=jnp.float32,
    )
    if spare:
        high[used_lines:, :] = jnp.zeros((spare, query_width), jnp.bfloat16)
        low[used_lines:, :] = jnp.zeros((spare, query_width), jnp.bfloat16)
    for g in range(group):
        columns = slice(g * HD, (g + 1) * HD)
        scaled = numers[:, columns] * factor[:used_lines, g : g + 1]
        rounded = scaled.astype(jnp.bfloat16)
        high[:used_lines, columns] = rounded
        low[:used_lines, columns] = (scaled - rounded.astype(jnp.float32)).astype(jnp.bfloat16)

    if has_earlier:
        early_max = early_max_ref[...]
        largest = jnp.maximum(row_max, early_max)
        scale_now = jnp.exp(row_max - largest)
        scale_early = jnp.exp(early_max - largest)
        row_total = row_total * scale_now + early_total_ref[...] * scale_early
        row_max = largest
    if last:
        present = row_total > 0
        inverse = jnp.where(present, 1.0 / jnp.where(present, row_total, 1.0), 0.0)
        log_sum = jnp.where(
            present & (lane < group),
            row_max + jnp.log(jnp.where(present, row_total, 1.0)),
            jnp.where(lane < group, NEGATIVE, 0.0),
        )
        if has_earlier:
            scale_now = scale_now * inverse
            scale_early = scale_early * inverse
        else:
            scale_now = inverse
        part = group // chunks
        for chunk in range(chunks):
            if chunk == 0:
                payload_refs[0][:, part * HD :] = split_sums(log_sum, group)
    for g in range(group):
        columns = slice(g * HD, (g + 1) * HD)
        numer = jnp.dot(
            member_t, high[:, columns], preferred_element_type=jnp.float32
        ) + jnp.dot(member_t, low[:, columns], preferred_element_type=jnp.float32)
        if has_earlier:
            numer = (
                numer * scale_now[:, g : g + 1]
                + early_numer_ref[:, columns] * scale_early[:, g : g + 1]
            )
        elif last:
            numer = numer * scale_now[:, g : g + 1]
        if last:
            place = g % part
            payload_refs[g // part][:, place * HD : (place + 1) * HD] = numer.astype(jnp.bfloat16)
        else:
            out_numer_ref[:, columns] = numer
    if not last:
        out_max_ref[...] = row_max
        out_total_ref[...] = row_total


def split_sums(value, group):
    first = value.astype(jnp.bfloat16).astype(jnp.float32)
    rest = value - first
    second = rest.astype(jnp.bfloat16).astype(jnp.float32)
    third = rest - second
    return (
        first + pltpu.roll(second, group, axis=1) + pltpu.roll(third, 2 * group, axis=1)
    ).astype(jnp.bfloat16)


def join_sums(parts, group):
    parts = parts.astype(jnp.float32)
    return (
        parts
        + pltpu.roll(parts, LANES - group, axis=1)
        + pltpu.roll(parts, LANES - 2 * group, axis=1)
    )


def attend(query, tokens, member, member_t, earlier, last, steps, chunks):
    row_lines, query_width = query.shape
    group = query_width // HD
    held, page_len = tokens.shape[0] // 2, tokens.shape[1]
    member_lines = member.shape[0]
    used_lines = (held - 1) * steps + page_len
    stat = jax.ShapeDtypeStruct((row_lines, LANES), jnp.float32)
    if last:
        part = group // chunks * HD
        out_shape = tuple(
            jax.ShapeDtypeStruct((row_lines, part + (LANES if c == 0 else 0)), jnp.bfloat16)
            for c in range(chunks)
        )
    else:
        out_shape = (stat, stat, jax.ShapeDtypeStruct((row_lines, query_width), jnp.float32))
    return pl.pallas_call(
        functools.partial(attend_kernel, steps, earlier is not None, last, chunks),
        out_shape=out_shape,
        scratch_shapes=[
            pltpu.VMEM((member_lines, query_width), jnp.bfloat16),
            pltpu.VMEM((used_lines, query_width), jnp.float32),
            pltpu.VMEM((member_lines, query_width), jnp.bfloat16),
            pltpu.VMEM((member_lines, query_width), jnp.bfloat16),
        ],
        compiler_params=params(),
        cost_estimate=pl.CostEstimate(
            flops=4 * 1024 * 1024 * 1024, bytes_accessed=4 * 1024 * 1024, transcendentals=0
        ),
        name="attend",
    )(query, tokens, member, member_t, *(earlier or ()))


def combine_kernel(group, first_group, sums_ref, their_sums_ref, mine_ref, theirs_ref, out_ref):
    wide = out_ref.shape[1]
    sums = join_sums(sums_ref[...], group)
    their_sums = join_sums(their_sums_ref[...], group)
    largest = jnp.maximum(sums, their_sums)
    weight = jnp.exp(sums - largest)
    their_weight = jnp.exp(their_sums - largest)
    inverse = 1.0 / (weight + their_weight)
    weight = weight * inverse
    their_weight = their_weight * inverse
    for place in range(wide // HD):
        g = first_group + place
        columns = slice(place * HD, (place + 1) * HD)
        out_ref[:, columns] = (
            mine_ref[:, columns].astype(jnp.float32) * weight[:, g : g + 1]
            + theirs_ref[:, columns].astype(jnp.float32) * their_weight[:, g : g + 1]
        ).astype(jnp.bfloat16)


def combine(group, first_group, sums, their_sums, mine, theirs, wide):
    row_lines = mine.shape[0]
    return pl.pallas_call(
        functools.partial(combine_kernel, group, first_group),
        out_shape=jax.ShapeDtypeStruct((row_lines, wide), jnp.bfloat16),
        compiler_params=params(),
        name="combine",
    )(sums, their_sums, mine, theirs)


def project_kernel(has_total, chunk_lines, place_ref, *refs):
    input_ref, weight_ref = refs[:2]
    refs = refs[2:]
    product = jnp.dot(input_ref[...], weight_ref[...], preferred_element_type=jnp.float32)
    if has_total:
        product = product + refs[0][...]
        refs = refs[1:]
    if chunk_lines is None:
        refs[0][...] = product
        return
    keep_ref, send_ref = refs
    core = place_ref[1]
    for pair in range(keep_ref.shape[0]):
        first = product[2 * pair * chunk_lines : (2 * pair + 1) * chunk_lines]
        second = product[(2 * pair + 1) * chunk_lines : (2 * pair + 2) * chunk_lines]
        keep_ref[pair] = jnp.where(core == 0, first, second)
        send_ref[pair] = jnp.where(core == 0, second, first).astype(send_ref.dtype)


def project(place, inputs, weight, total, columns, chunk_lines):
    row_lines, depth = inputs.shape
    first, width = columns
    block = min(width, 512)
    offset = first // block
    in_specs = [
        pl.BlockSpec((row_lines, depth), lambda n, place: (0, 0)),
        pl.BlockSpec((depth, block), lambda n, place: (place[0], n + offset)),
    ]
    operands = [inputs, weight]
    if total is not None:
        in_specs.append(pl.BlockSpec((row_lines, block), lambda n, place: (0, n + offset)))
        operands.append(total)
    if chunk_lines is None:
        out_shape = jax.ShapeDtypeStruct((row_lines, width), jnp.float32)
        out_specs = pl.BlockSpec((row_lines, block), lambda n, place: (0, n))
    else:
        pairs = row_lines // (2 * chunk_lines)
        shape = (pairs, chunk_lines, width)
        out_shape = (
            jax.ShapeDtypeStruct(shape, jnp.float32),
            jax.ShapeDtypeStruct(shape, jnp.bfloat16),
        )
        spec = pl.BlockSpec((pairs, chunk_lines, block), lambda n, place: (0, 0, n))
        out_specs = (spec, spec)
    return pl.pallas_call(
        functools.partial(project_kernel, total is not None, chunk_lines),
        grid_spec=pltpu.PrefetchScalarGridSpec(
            num_scalar_prefetch=1,
            grid=(width // block,),
            in_specs=in_specs,
            out_specs=out_specs,
        ),
        out_shape=out_shape,
        compiler_params=params(),
        cost_estimate=pl.CostEstimate(
            flops=2 * row_lines * depth * width,
            bytes_accessed=2 * depth * width,
            transcendentals=0,
        ),
        name="project",
    )(place, *operands)


def sum_heads(keep, send, kv_index, kv_size):
    total = keep + lax.ppermute(send, "kv", flip(kv_size, 1)).astype(jnp.float32)
    half = kv_index // 2
    result = lax.dynamic_index_in_dim(total, half, 0, keepdims=False)
    for step in range(1, kv_size // 2):
        part = lax.dynamic_index_in_dim(total, half ^ step, 0, keepdims=False)
        got = lax.ppermute(part.astype(jnp.bfloat16), "kv", flip(kv_size, 2 * step))
        result = result + got.astype(jnp.float32)
    return result.astype(jnp.bfloat16)


def body(
    queries, fresh_keys, fresh_values, cache_keys, cache_values, page_counts, page_owner, out_weight
):
    tp_size, kv_size = lax.axis_size("tp"), lax.axis_size("kv")
    tp_index, kv_index = lax.axis_index("tp"), lax.axis_index("kv")
    head_count, pages_here, page_width = cache_keys.shape
    row_count, step_count, query_width = queries.shape
    own_rows = fresh_keys.shape[0]
    page_len = page_width // HD
    row_lines = row_count * step_count
    head_width = query_width // head_count
    group = head_width // HD
    cap = max(2, (2 * pages_here + tp_size - 1) // tp_size)
    rows = jnp.arange(row_count, dtype=jnp.int32)

    own_head = tp_index % head_count
    spare = page_len - own_rows * step_count

    def by_head(fresh):
        split = fresh.reshape(own_rows * step_count, head_count, HD).transpose(1, 0, 2)
        return jnp.pad(split, ((0, 0), (0, spare), (0, 0)))[:, None]

    def paged(cache):
        return cache.reshape(head_count, pages_here, page_len, HD)

    tokens = jnp.concatenate(
        [paged(cache_keys), by_head(fresh_keys), paged(cache_values), by_head(fresh_values)], axis=1
    )
    own_tokens = lax.dynamic_index_in_dim(tokens, own_head, 0, keepdims=False)
    if head_count == 2:
        other_tokens = lax.dynamic_index_in_dim(tokens, 1 - own_head, 0, keepdims=False)
        near_tokens = lax.ppermute(other_tokens, "tp", flip(tp_size, 1))

    row_ends = jnp.sum(jnp.where(rows[None, :] <= rows[:, None], page_counts[None, :], 0), axis=1)
    send_keys, send_values = place_pages(page_owner, cache_keys, cache_values, tp_size, cap)

    def hand_over(pages):
        got = lax.all_to_all(pages, "tp", split_axis=0, concat_axis=0, tiled=True)
        return got.transpose(1, 0, 2, 3).reshape(head_count, tp_size * cap, page_width)

    slot_keys = hand_over(send_keys)
    slot_values = hand_over(send_values)
    slot_rows = list_slot_rows(page_owner, row_ends, tp_index, tp_size, cap)

    page_lines = pages_here * step_count
    member_lines = round_up(page_lines + page_len, LANES)
    line = jnp.arange(member_lines, dtype=jnp.int32)
    query_line = jnp.arange(row_lines, dtype=jnp.int32)
    query_row = query_line // step_count
    ends = jnp.sum(jnp.where(rows[None, :] <= query_row[:, None], page_counts[None, :], 0), axis=1)
    counts = jnp.sum(jnp.where(rows[None, :] == query_row[:, None], page_counts[None, :], 0), axis=1)

    def membership(owner, line, query_line, ends, starts):
        page = owner * pages_here + line // step_count
        in_row = (starts <= page) & (page < ends) & (line % step_count == query_line % step_count)
        own_line = line - page_lines
        is_own = (
            (own_line >= 0)
            & (own_line < own_rows * step_count)
            & (query_line == owner * own_rows * step_count + own_line)
        )
        return (((line < page_lines) & in_row) | is_own).astype(jnp.bfloat16)

    def members(owner):
        starts = ends - counts
        return (
            membership(owner, line[:, None], query_line[None, :], ends[None, :], starts[None, :]),
            membership(owner, line[None, :], query_line[:, None], ends[:, None], starts[:, None]),
        )

    own_query = lax.dynamic_slice_in_dim(
        queries.reshape(row_lines, query_width), own_head * head_width, head_width, 1
    )
    outer = tp_size // head_count
    chunks = 2 if outer == 2 and group % 2 == 0 else 1
    if head_count == 2:
        earlier = attend(own_query, own_tokens, *members(tp_index), None, False, step_count, chunks)
        payload = attend(
            own_query, near_tokens, *members(tp_index ^ 1), earlier, True, step_count, chunks
        )
    else:
        payload = attend(own_query, own_tokens, *members(tp_index), None, True, step_count, chunks)

    part = head_width // chunks
    own_parts, near_parts = [], []
    if outer == 2:
        far = [lax.ppermute(p, "tp", flip(tp_size, head_count)) for p in payload]
        for c in range(chunks):
            own_parts.append(
                combine(
                    group,
                    c * (group // chunks),
                    payload[0][:, part:],
                    far[0][:, part:],
                    payload[c][:, :part],
                    far[c][:, :part],
                    part,
                )
            )
    else:
        raw = payload[0][:, part:].astype(jnp.float32)
        sums = raw[:, :group] + raw[:, group : 2 * group] + raw[:, 2 * group : 3 * group]
        weight = jnp.exp(sums - lax.pmax(sums, "tp"))
        numer = payload[0][:, :part].astype(jnp.float32).reshape(row_lines, group, HD)
        numer = lax.psum(numer * weight[..., None], "tp")
        joined = numer / lax.psum(weight, "tp")[..., None]
        own_parts.append(joined.reshape(row_lines, head_width).astype(jnp.bfloat16))
    if head_count == 2:
        near_parts = [lax.ppermute(p, "tp", flip(tp_size, 1)) for p in own_parts]

    core = kv_index % 2
    chunk_lines = row_lines // kv_size
    out_width = out_weight.shape[1]
    own_place = jnp.stack([own_head, core]).astype(jnp.int32)
    own_input = jnp.concatenate(own_parts, axis=1)
    results = []
    if head_count == 2:
        total = project(own_place, own_input, out_weight, None, (0, out_width), None)
        near_place = jnp.stack([1 - own_head, core]).astype(jnp.int32)
        near_input = jnp.concatenate(near_parts, axis=1)
        for first in (0, out_width // 2):
            keep, send = project(
                near_place, near_input, out_weight, total, (first, out_width // 2), chunk_lines
            )
            results.append(sum_heads(keep, send, kv_index, kv_size))
    else:
        keep, send = project(own_place, own_input, out_weight, None, (0, out_width), chunk_lines)
        results.append(sum_heads(keep, send, kv_index, kv_size))
    attention_out = jnp.concatenate(results, axis=1).reshape(-1, step_count, out_width)
    return (attention_out, slot_keys, slot_values, slot_rows)


def solution(mesh):
    return jax.shard_map(
        body,
        mesh=mesh,
        in_specs=(
            P("grp", None, "kv"),
            P(("grp", "tp"), None, "kv"),
            P(("grp", "tp"), None, "kv"),
            P(("grp", "kv"), "tp", None),
            P(("grp", "kv"), "tp", None),
            P("grp"),
            P(("grp", "kv"), "tp"),
            P("kv", "tp"),
        ),
        out_specs=(
            P(("grp", "kv"), None, "tp"),
            P(("grp", "kv"), "tp", None),
            P(("grp", "kv"), "tp", None),
            P(("grp", "kv"), "tp"),
        ),
        check_vma=False,
    )
```

time: 244 us -> 130 us (0.53)
  waiting for transfers between devices: 93.9 us -> 43.8 us
  local copies, waits for them, and re-layouts: 46 us -> 9.52 us
  Pallas kernels: 0 us -> 30.3 us
  matrix products: 23.3 us -> 0 us
  blocking collectives: 45 us -> 25.7 us
  between operations: 15.1 us -> 1.04 us
  other arithmetic: 8.8 us -> 2.63 us
  starting transfers between devices: 11.4 us -> 16.9 us
    pallas_call x0 -> x8, Pallas kernels: none -> 30.3 us  [the longest x3 21.1 us: project(): pl.pallas_call(functools.partial(project_kernel, total is not None, chunk...]
    all_gather x1 -> x0, waiting for transfers between devices: 28.2 us -> none  [body(): lax.all_gather(share_rows.reshape(share_sum.shape[0], step_count, -1), 't...]
    all_to_all x3 -> x2, waiting for transfers between devices: 44.8 us -> 17.5 us  [hand_over(): got = lax.all_to_all(pages, 'tp', split_axis=0, concat_axis=0, tiled=True)]
    ppermute x0 -> x9, waiting for transfers between devices: none -> 26.3 us  [the longest x2 21.2 us: body(): far = [lax.ppermute(p, 'tp', flip(tp_size, head_count)) for p in payload]]
    all_gather x0 -> x1, blocking collectives: none -> 25.7 us  [list_slot_rows(): owners = lax.all_gather(page_owner, 'tp', axis=1, tiled=False)]
    dot_general x11 -> x0, matrix products: 23.3 us -> none  [the longest x1 16.7 us: body(): product = jnp.dot(flat_rows, out_weight, preferred_element_type=jnp.float32)]
    pmax x1 -> x0, blocking collectives: 22.5 us -> none  [body(): largest = lax.pmax(partial_value[0], 'tp')]
    unnamed x1 -> x0, blocking collectives: 22.5 us -> none
  transfers between devices with their start and end apart: 6 -> 11, of which waited for: 5 -> 5; matrix products, arithmetic and copies ran while one was open for 8% -> 6% of each run, Pallas kernels for 0% -> 23%
where the time goes in v1:
time: 130 us
  waiting for transfers between devices  43.8 us (34%)
  Pallas kernels  30.3 us (23%)
  blocking collectives  25.7 us (20%)
  starting transfers between devices  16.9 us (13%)
  local copies, waits for them, and re-layouts  9.52 us (7%)
  other arithmetic  2.63 us (2%)
    all_gather x1, blocking collectives, list_slot_rows(): owners = lax.all_gather(page_owner, 'tp', axis=1, tiled=False)  25.7 us
    ppermute x2, waiting for transfers between devices, body(): far = [lax.ppermute(p, 'tp', flip(tp_size, head_count)) for p in payload]  21.2 us
    pallas_call x3, Pallas kernels, project(): pl.pallas_call(functools.partial(project_kernel, total is not None, chunk...  21.1 us
    all_to_all x2, waiting for transfers between devices, hand_over(): got = lax.all_to_all(pages, 'tp', split_axis=0, concat_axis=0, tiled=True)  17.5 us
    all_to_all x2, starting transfers between devices, hand_over(): got = lax.all_to_all(pages, 'tp', split_axis=0, concat_axis=0, tiled=True)  7.92 us
    pallas_call x2, Pallas kernels, attend(): pl.pallas_call(functools.partial(attend_kernel, steps, earlier is not Non...  6.16 us
    ppermute x2, waiting for transfers between devices, sum_heads(): got = lax.ppermute(part.astype(jnp.bfloat16), 'kv', flip(kv_size, 2 * step))  4.58 us
    transpose x2, local copies, waits for them, and re-layouts, hand_over(): got.transpose(1, 0, 2, 3).reshape(head_count, tp_size * cap, page_width)  3.33 us
  transfers between devices with their start and end apart: 11, of which 5 were waited for; matrix products, arithmetic and copies ran while one was open for 6% of the time, Pallas kernels for 23%

profile of v1, /device:TPU:0, one launch (start us, length us, event | category | flops | bytes accessed | tf_op | source)
XLA Modules:
  0.0 129.9 jit_solution(11507949689948553877)
XLA Ops:
  0.6 0.0 copy-start
  0.7 0.8 reshape.279
  1.4 0.7 reshape.281
  2.2 1.1 copy.32
  3.3 0.0 copy-done
  3.3 0.1 copy.33
  3.5 0.1 pad_maximum_fusion
  3.6 0.0 copy-start.1
  3.6 0.0 copy-start.2
  3.6 0.2 dynamic-slice_bitcast_fusion
  3.8 3.1 %collective-permute-start = (bf16[66,32,128]{2,1,0:T(8,128)(2,1)S(1)}, bf16[66,32,128]{2,1,0:T(8,128)(2,1)S(1)}, u32[]{:S(2)}, u32[]{:S(2)}) collective-permute-start(bf16[66,32,128]{2,1,0:T(8,128)(2,1)S(1)} %get-tuple-element.29), channel_id=1, source_target_pairs={{0,4},{4,0},{8,12},{12,8},{1,5},{5,1},{9,13},{13,9},{2,6},{6,2},{1... | collective-permute-start | bytes 1622024 | tf_op jit(solution)/shard_map/ppermute | solution.py:438
  6.9 0.0 copy-done.1
  6.9 0.0 copy-done.2
  6.9 2.1 %place_pages.1 = (bf16[4,2,16,4096]{3,2,1,0:T(8,128)(2,1)}, bf16[4,2,16,4096]{3,2,1,0:T(8,128)(2,1)}) custom-call(s32[2,32]{1,0:T(2,128)S(1)} %copy-done.2, bf16[2,32,4096]{2,1,0:T(8,128)(2,1)S(1)} %copy-done.1, bf16[2,32,4096]{2,1,0:T(8,128)(2,1)S(1)} %copy-done), custom_call_target="tpu_custom_call" | custom-call | tf_op jit(solution)/shard_map/place_pages/pallas_call | solution.py:67
  9.1 0.0 copy-start.3
  9.1 4.4 %all-to-all-start = ((bf16[4,2,16,4096]{3,2,1,0:T(8,128)(2,1)}), bf16[4,2,16,4096]{3,2,1,0:T(8,128)(2,1)}, u32[]{:S(2)}, u32[]{:S(2)}) async-start(bf16[4,2,16,4096]{3,2,1,0:T(8,128)(2,1)} %get-tuple-element.24), calls=%async_computation | async-start | bytes 2097152 | tf_op jit(solution)/shard_map/all_to_all | solution.py:444
  13.5 0.0 copy-done.3
  13.5 0.1 select_reduce_fusion.2
  13.6 0.2 fusion.15
  13.8 0.3 fusion.12
  14.1 0.1 select_reduce_fusion.1
  14.3 1.3 %reshape.277 = bf16[128,4096]{1,0:T(8,128)(2,1)S(1)} reshape(bf16[32,4,4096]{2,1,0:T(4,128)(2,1)} %param.8) | data formatting | bytes 2097152 | tf_op jit(solution)/shard_map/reshape | solution.py:478
  15.6 25.7 %all-gather.1 = s32[4,32,2]{1,2,0:T(2,128)S(1)} all-gather(s32[1,32,2]{1,2,0:T(2,128)S(1)} %bitcast.49), channel_id=2, replica_groups=mesh['grp'=2,'tp'=4,'kv'=4] {'tp'}, dimensions={0}, use_global_device_ids=true | all-gather | bytes 1280 | tf_op jit(solution)/shard_map/all_gather | solution.py:77
  41.3 0.1 reshape.287
  41.3 0.1 reshape.285
  41.4 0.1 convert_reduce_fusion.1
  41.6 0.1 pad_add_fusion.1.place_ref
  41.7 2.8 %attend.2 = (f32[128,128]{1,0:T(8,128)S(1)}, f32[128,128]{1,0:T(8,128)S(1)}, f32[128,2048]{1,0:T(8,128)S(1)}) custom-call(bf16[128,2048]{1,0:T(8,128)(2,1)S(1)} %constant_dynamic-slice_fusion.refs_0_, bf16[66,32,128]{2,1,0:T(8,128)(2,1)S(1)} %get-tuple-element.28.refs_1_, bf16[256,128]{1,0:T(8,128)(2,1)S(1)} %get-tuple-element.32.refs_2_, ...), custom_call_target="tpu_custom_call" | custom-call | flops 4294967296 | bytes 4194304 | tf_op jit(solution)/shard_map/attend/pallas_call | solution.py:287
  44.5 0.0 collective-permute-done.refs_1_
  44.5 3.3 %attend.3 = (bf16[128,1152]{1,0:T(8,128)(2,1)S(1)}, bf16[128,1024]{1,0:T(8,128)(2,1)S(1)}) custom-call(bf16[128,2048]{1,0:T(8,128)(2,1)S(1)} %constant_dynamic-slice_fusion.refs_0_, bf16[66,32,128]{2,1,0:T(8,128)(2,1)S(1)} %collective-permute-done.refs_1_, bf16[256,128]{1,0:T(8,128)(2,1)S(1)} %get-tuple-element.33.refs_2_, ...), custom_call_target="tpu_custom_call" | custom-call | flops 4294967296 | bytes 4194304 | tf_op jit(solution)/shard_map/attend/pallas_call | solution.py:287
  47.9 1.6 %collective-permute-start.1 = (bf16[128,1152]{1,0:T(8,128)(2,1)S(1)}, bf16[128,1152]{1,0:T(8,128)(2,1)S(1)}, u32[]{:S(2)}, u32[]{:S(2)}) collective-permute-start(bf16[128,1152]{1,0:T(8,128)(2,1)S(1)} %get-tuple-element.18), channel_id=1, source_target_pairs={{0,8},{4,12},{8,0},{12,4},{1,9},{5,13},{9,1},{13,5},{2,10},{6,14},... | collective-permute-start | bytes 884744 | tf_op jit(solution)/shard_map/ppermute | solution.py:493
  49.4 1.4 %collective-permute-start.3 = (bf16[128,1024]{1,0:T(8,128)(2,1)S(1)}, bf16[128,1024]{1,0:T(8,128)(2,1)S(1)}, u32[]{:S(2)}, u32[]{:S(2)}) collective-permute-start(bf16[128,1024]{1,0:T(8,128)(2,1)S(1)} %get-tuple-element.19.mine_ref), channel_id=1, source_target_pairs={{0,8},{4,12},{8,0},{12,4},{1,9},{5,13},{9,1},{13,5},{2,10},{6,14},... | collective-permute-start | bytes 786440 | tf_op jit(solution)/shard_map/ppermute | solution.py:493
  50.9 0.1 pad_add_fusion.place_ref
  50.9 0.1 add.248
  51.0 0.1 convert_reduce_fusion
  51.1 0.2 select_reduce_fusion
  51.4 16.4 %collective-permute-done.1 = bf16[128,1152]{1,0:T(8,128)(2,1)S(1)} collective-permute-done((bf16[128,1152]{1,0:T(8,128)(2,1)S(1)}, bf16[128,1152]{1,0:T(8,128)(2,1)S(1)}, u32[]{:S(2)}, u32[]{:S(2)}) %collective-permute-start.1) | collective-permute-done | bytes 294944 | tf_op jit(solution)/shard_map/ppermute | solution.py:493
  67.9 0.5 combine.2
  68.3 0.1 collective-permute-start.2
  68.4 4.8 %collective-permute-done.3.theirs_ref = bf16[128,1024]{1,0:T(8,128)(2,1)S(1)} collective-permute-done((bf16[128,1024]{1,0:T(8,128)(2,1)S(1)}, bf16[128,1024]{1,0:T(8,128)(2,1)S(1)}, u32[]{:S(2)}, u32[]{:S(2)}) %collective-permute-start.3) | collective-permute-done | bytes 262176 | tf_op jit(solution)/shard_map/ppermute | solution.py:493
  73.2 0.5 combine.3
  73.7 0.1 collective-permute-start.4
  73.8 10.0 %project.3.refs_2_ = f32[128,4096]{1,0:T(8,128)S(1)} custom-call(s32[2]{0:T(128)S(1)} %pad_add_fusion.1.place_ref, bf16[128,2048]{1,0:T(8,128)(2,1)S(1)} %pad_maximum_fusion.1.refs_0_, bf16[4096,4096]{1,0:T(8,128)(2,1)} %refs_1_.5), custom_call_target="tpu_custom_call" | custom-call | flops 2147483648 | bytes 16777216 | tf_op jit(solution)/shard_map/project/pallas_call | solution.py:377
  83.9 0.0 collective-permute-done.2
  83.9 0.5 collective-permute-done.4
  84.4 5.5 %project.4 = (f32[2,32,2048]{2,1,0:T(8,128)S(1)}, bf16[2,32,2048]{2,1,0:T(8,128)(2,1)S(1)}) custom-call(s32[2]{0:T(128)S(1)} %pad_add_fusion.place_ref, bf16[128,2048]{1,0:T(8,128)(2,1)S(1)} %constant_dynamic-update-slice_fusion.refs_0_, bf16[4096,4096]{1,0:T(8,128)(2,1)} %refs_1_.5, f32[128,4096]{1,0:T(8,128)S(1)} %project.3.refs_2_), custom_call_target="tpu_custom_call" | custom-call | flops 1073741824 | bytes 8388608 | tf_op jit(solution)/shard_map/project/pallas_call | solution.py:377
  89.9 0.1 collective-permute-start.5
  90.0 0.6 sub.74
  90.6 5.5 %project.5 = (f32[2,32,2048]{2,1,0:T(8,128)S(1)}, bf16[2,32,2048]{2,1,0:T(8,128)(2,1)S(1)}) custom-call(s32[2]{0:T(128)S(1)} %pad_add_fusion.place_ref, bf16[128,2048]{1,0:T(8,128)(2,1)S(1)} %constant_dynamic-update-slice_fusion.refs_0_, bf16[4096,4096]{1,0:T(8,128)(2,1)} %refs_1_.5, f32[128,4096]{1,0:T(8,128)S(1)} %project.3.refs_2_), custom_call_target="tpu_custom_call" | custom-call | flops 1073741824 | bytes 8388608 | tf_op jit(solution)/shard_map/project/pallas_call | solution.py:377
  96.2 0.6 collective-permute-start.7
  96.7 0.0 collective-permute-done.5
  96.7 1.0 convert_add_fusion.1
  97.8 1.6 %collective-permute-start.6 = (bf16[32,2048]{1,0:T(8,128)(2,1)S(1)}, bf16[32,2048]{1,0:T(8,128)(2,1)S(1)}, u32[]{:S(2)}, u32[]{:S(2)}) collective-permute-start(bf16[32,2048]{1,0:T(8,128)(2,1)S(1)} %fusion.2), channel_id=1, source_target_pairs={{0,2},{1,3},{2,0},{3,1},{4,6},{5,7},{6,4},{7,5},{8,10},{9,11},{10,... | collective-permute-start | bytes 393224 | tf_op jit(solution)/shard_map/ppermute | solution.py:402
  99.3 0.0 collective-permute-done.7
  99.3 0.1 convert_add_fusion
  99.4 0.0 all-to-all-done
  99.4 3.5 %all-to-all-start.1 = ((bf16[4,2,16,4096]{3,2,1,0:T(8,128)(2,1)}), bf16[4,2,16,4096]{3,2,1,0:T(8,128)(2,1)S(1)}, u32[]{:S(2)}, u32[]{:S(2)}) async-start(bf16[4,2,16,4096]{3,2,1,0:T(8,128)(2,1)} %get-tuple-element.25), calls=%async_computation.1 | async-start | bytes 2097152 | tf_op jit(solution)/shard_map/all_to_all | solution.py:444
  103.0 0.6 collective-permute-start.8
  103.6 0.0 collective-permute-done.6
  103.6 4.6 %collective-permute-done.8 = bf16[32,2048]{1,0:T(8,128)(2,1)S(1)} collective-permute-done((bf16[32,2048]{1,0:T(8,128)(2,1)S(1)}, bf16[32,2048]{1,0:T(8,128)(2,1)S(1)}, u32[]{:S(2)}, u32[]{:S(2)}) %collective-permute-start.8) | collective-permute-done | bytes 131104 | tf_op jit(solution)/shard_map/ppermute | solution.py:402
  108.2 0.8 reshape.282
  109.0 2.3 %copy.29 = bf16[2,4,16,4096]{3,2,1,0:T(8,128)(2,1)} copy(bf16[2,4,16,4096]{3,2,0,1:T(8,128)(2,1)} %bitcast.13) | data formatting | bytes 2097152 | tf_op jit(solution)/shard_map/transpose | solution.py:445
  111.3 17.5 %all-to-all-done.1 = bf16[4,2,16,4096]{3,2,1,0:T(8,128)(2,1)S(1)} async-done(((bf16[4,2,16,4096]{3,2,1,0:T(8,128)(2,1)}), bf16[4,2,16,4096]{3,2,1,0:T(8,128)(2,1)S(1)}, u32[]{:S(2)}, u32[]{:S(2)}) %all-to-all-start.1) | async-done | bytes 1048608 | tf_op jit(solution)/shard_map/all_to_all | solution.py:444
  128.8 1.0 copy.30
  (25 shorter events, 0.3 us)
Async XLA Ops:
  0.6 2.7 %copy-start = (bf16[2,32,4096]{2,1,0:T(8,128)(2,1)S(1)}, bf16[2,32,4096]{2,1,0:T(8,128)(2,1)}, u32[]{:S(2)}) copy-start(bf16[2,32,4096]{2,1,0:T(8,128)(2,1)} %value_ref.1) | copy-start | bytes 1572868
  3.6 3.3 %copy-start.1 = (bf16[2,32,4096]{2,1,0:T(8,128)(2,1)S(1)}, bf16[2,32,4096]{2,1,0:T(8,128)(2,1)}, u32[]{:S(2)}) copy-start(bf16[2,32,4096]{2,1,0:T(8,128)(2,1)} %key_ref.1) | copy-start | bytes 1572868
  3.6 3.3 %copy-start.2 = (s32[2,32]{1,0:T(2,128)S(1)}, s32[2,32]{1,0:T(2,128)}, u32[]{:S(2)}) copy-start(s32[2,32]{1,0:T(2,128)} %owner_ref.1) | copy-start | bytes 772
  3.8 40.7 %collective-permute-start = (bf16[66,32,128]{2,1,0:T(8,128)(2,1)S(1)}, bf16[66,32,128]{2,1,0:T(8,128)(2,1)S(1)}, u32[]{:S(2)}, u32[]{:S(2)}) collective-permute-start(bf16[66,32,128]{2,1,0:T(8,128)(2,1)S(1)} %get-tuple-element.29), channel_id=1, source_target_pairs={{0,4},{4,0},{8,12},{12,8},{1,5},{5,1},{9,13},{13,9},{2,6},{6,2},{1... | collective-permute-start | bytes 1622024 | tf_op jit(solution)/shard_map/ppermute | solution.py:438
  9.1 4.5 %copy-start.3 = (s32[32]{0:T(128)S(1)}, s32[32]{0:T(128)}, u32[]{:S(2)}) copy-start(s32[32]{0:T(128)} %param.13) | copy-start | bytes 388
  9.1 90.3 %all-to-all-start = ((bf16[4,2,16,4096]{3,2,1,0:T(8,128)(2,1)}), bf16[4,2,16,4096]{3,2,1,0:T(8,128)(2,1)}, u32[]{:S(2)}, u32[]{:S(2)}) async-start(bf16[4,2,16,4096]{3,2,1,0:T(8,128)(2,1)} %get-tuple-element.24), calls=%async_computation | async-start | bytes 2097152 | tf_op jit(solution)/shard_map/all_to_all | solution.py:444
  47.9 20.0 %collective-permute-start.1 = (bf16[128,1152]{1,0:T(8,128)(2,1)S(1)}, bf16[128,1152]{1,0:T(8,128)(2,1)S(1)}, u32[]{:S(2)}, u32[]{:S(2)}) collective-permute-start(bf16[128,1152]{1,0:T(8,128)(2,1)S(1)} %get-tuple-element.18), channel_id=1, source_target_pairs={{0,8},{4,12},{8,0},{12,4},{1,9},{5,13},{9,1},{13,5},{2,10},{6,14},... | collective-permute-start | bytes 884744 | tf_op jit(solution)/shard_map/ppermute | solution.py:493
  49.4 23.8 %collective-permute-start.3 = (bf16[128,1024]{1,0:T(8,128)(2,1)S(1)}, bf16[128,1024]{1,0:T(8,128)(2,1)S(1)}, u32[]{:S(2)}, u32[]{:S(2)}) collective-permute-start(bf16[128,1024]{1,0:T(8,128)(2,1)S(1)} %get-tuple-element.19.mine_ref), channel_id=1, source_target_pairs={{0,8},{4,12},{8,0},{12,4},{1,9},{5,13},{9,1},{13,5},{2,10},{6,14},... | collective-permute-start | bytes 786440 | tf_op jit(solution)/shard_map/ppermute | solution.py:493
  68.3 15.5 %collective-permute-start.2 = (bf16[128,1024]{1,0:T(8,128)(2,1)S(1)}, bf16[128,1024]{1,0:T(8,128)(2,1)S(1)}, u32[]{:S(2)}, u32[]{:S(2)}) collective-permute-start(bf16[128,1024]{1,0:T(8,128)(2,1)S(1)} %combine.2), channel_id=1, source_target_pairs={{0,4},{4,0},{8,12},{12,8},{1,5},{5,1},{9,13},{13,9},{2,6},{6,2},{1... | collective-permute-start | bytes 786440 | tf_op jit(solution)/shard_map/ppermute | solution.py:515
  73.7 10.6 %collective-permute-start.4 = (bf16[128,1024]{1,0:T(8,128)(2,1)S(1)}, bf16[128,1024]{1,0:T(8,128)(2,1)S(1)}, u32[]{:S(2)}, u32[]{:S(2)}) collective-permute-start(bf16[128,1024]{1,0:T(8,128)(2,1)S(1)} %combine.3), channel_id=1, source_target_pairs={{0,4},{4,0},{8,12},{12,8},{1,5},{5,1},{9,13},{13,9},{2,6},{6,2},{1... | collective-permute-start | bytes 786440 | tf_op jit(solution)/shard_map/ppermute | solution.py:515
  89.9 6.8 %collective-permute-start.5 = (bf16[2,32,2048]{2,1,0:T(8,128)(2,1)S(1)}, bf16[2,32,2048]{2,1,0:T(8,128)(2,1)}, u32[]{:S(2)}, u32[]{:S(2)}) collective-permute-start(bf16[2,32,2048]{2,1,0:T(8,128)(2,1)S(1)} %get-tuple-element.21), channel_id=1, source_target_pairs={{0,1},{1,0},{2,3},{3,2},{4,5},{5,4},{6,7},{7,6},{8,9},{9,8},{10,11... | collective-permute-start | bytes 786440 | tf_op jit(solution)/shard_map/ppermute | solution.py:397
  96.2 3.1 %collective-permute-start.7 = (bf16[2,32,2048]{2,1,0:T(8,128)(2,1)S(1)}, bf16[2,32,2048]{2,1,0:T(8,128)(2,1)S(1)}, u32[]{:S(2)}, u32[]{:S(2)}) collective-permute-start(bf16[2,32,2048]{2,1,0:T(8,128)(2,1)S(1)} %get-tuple-element.23), channel_id=1, source_target_pairs={{0,1},{1,0},{2,3},{3,2},{4,5},{5,4},{6,7},{7,6},{8,9},{9,8},{10,11... | collective-permute-start | bytes 786440 | tf_op jit(solution)/shard_map/ppermute | solution.py:397
  97.8 5.8 %collective-permute-start.6 = (bf16[32,2048]{1,0:T(8,128)(2,1)S(1)}, bf16[32,2048]{1,0:T(8,128)(2,1)S(1)}, u32[]{:S(2)}, u32[]{:S(2)}) collective-permute-start(bf16[32,2048]{1,0:T(8,128)(2,1)S(1)} %fusion.2), channel_id=1, source_target_pairs={{0,2},{1,3},{2,0},{3,1},{4,6},{5,7},{6,4},{7,5},{8,10},{9,11},{10,... | collective-permute-start | bytes 393224 | tf_op jit(solution)/shard_map/ppermute | solution.py:402
  99.4 29.4 %all-to-all-start.1 = ((bf16[4,2,16,4096]{3,2,1,0:T(8,128)(2,1)}), bf16[4,2,16,4096]{3,2,1,0:T(8,128)(2,1)S(1)}, u32[]{:S(2)}, u32[]{:S(2)}) async-start(bf16[4,2,16,4096]{3,2,1,0:T(8,128)(2,1)} %get-tuple-element.25), calls=%async_computation.1 | async-start | bytes 2097152 | tf_op jit(solution)/shard_map/all_to_all | solution.py:444
  103.0 5.2 %collective-permute-start.8 = (bf16[32,2048]{1,0:T(8,128)(2,1)S(1)}, bf16[32,2048]{1,0:T(8,128)(2,1)S(1)}, u32[]{:S(2)}, u32[]{:S(2)}) collective-permute-start(bf16[32,2048]{1,0:T(8,128)(2,1)S(1)} %fusion.3), channel_id=1, source_target_pairs={{0,2},{1,3},{2,0},{3,1},{4,6},{5,7},{6,4},{7,5},{8,10},{9,11},{10,... | collective-permute-start | bytes 393224 | tf_op jit(solution)/shard_map/ppermute | solution.py:402

commit v2 on v1

v2 whole, which is shorter than its diff:
```python
import functools

import jax
import jax.numpy as jnp
from jax import lax
from jax.experimental import pallas as pl
from jax.experimental.pallas import tpu as pltpu
from jax.sharding import PartitionSpec as P

HD = 128
LANES = 128
NEGATIVE = -1e30
HIGHEST = lax.Precision.HIGHEST
MIB = 1024 * 1024


def round_up(value, step):
    return -(-value // step) * step


def flip(size, bit):
    return [(i, i ^ bit) for i in range(size)]


def params(mib):
    return pltpu.CompilerParams(vmem_limit_bytes=mib * MIB)


def in_hbm(*arrays):
    return [pltpu.with_memory_space_constraint(array, pltpu.HBM) for array in arrays]


def vmem():
    return pl.BlockSpec(memory_space=pltpu.VMEM)


def hbm():
    return pl.BlockSpec(memory_space=pltpu.HBM)


def anywhere():
    return pl.BlockSpec(memory_space=pl.ANY)


def call(kernel, operands, in_specs, follows=(), **rest):
    count, extra = len(operands), len(follows)

    def without_extra(*refs):
        kernel(*refs[:count], *refs[count + extra :])

    return pl.pallas_call(
        without_extra,
        in_specs=list(in_specs) + [anywhere()] * extra,
        cost_estimate=pl.CostEstimate(flops=0, bytes_accessed=0, transcendentals=0),
        **rest,
    )(*operands, *follows)


def tie(value, *follows):
    return call(
        lambda value_ref, out_ref: None,
        (value,),
        [anywhere()],
        follows,
        out_specs=anywhere(),
        out_shape=jax.ShapeDtypeStruct(value.shape, value.dtype),
        input_output_aliases={0: 0},
        compiler_params=params(1),
        name="tie",
    )


def earlier_pages(page_count):
    first = lax.broadcasted_iota(jnp.int32, (page_count, page_count), 0)
    second = lax.broadcasted_iota(jnp.int32, (page_count, page_count), 1)
    return (first < second).astype(jnp.bfloat16)


def rank_pages(away, earlier, dest_rows):
    ways = lax.broadcasted_iota(jnp.int32, (dest_rows, away.shape[1]), 0)
    listed = (ways == away).astype(jnp.float32)
    before = jnp.dot(listed.astype(jnp.bfloat16), earlier, preferred_element_type=jnp.float32)
    return jnp.sum(before * listed, axis=0, keepdims=True).astype(jnp.int32)


def slot_picks(owners, me, distances, cap, tp_size):
    head_count, page_count = owners.shape
    earlier = earlier_pages(page_count)
    row = lax.broadcasted_iota(jnp.int32, (cap, page_count), 0)
    picks = []
    for head in range(head_count):
        away = owners[head : head + 1, :] ^ me
        rank = rank_pages(away, earlier, round_up(tp_size, 8))
        picks.append([((away == d) & (rank == row)).astype(jnp.float32) for d in distances])
    return picks


def place_rows(pages_ref, pick, targets):
    width, cap = pages_ref.shape[1], pick[0].shape[0]
    step = min(width, 1024)
    for start in range(0, width, step):
        columns = slice(start, start + step)
        placed = jnp.dot(
            jnp.concatenate(pick).astype(jnp.bfloat16),
            pages_ref[:, columns],
            preferred_element_type=jnp.float32,
        ).astype(jnp.bfloat16)
        for which, target in enumerate(targets):
            target[:, columns] = placed[which * cap : (which + 1) * cap]


def place_kernel(cap, jobs, by_index, tp_size, owner_ref, *refs):
    count = (len(refs) - 2 - len(jobs)) // 2
    sources, targets = refs[:count], refs[count : count + len(jobs)]
    held, owners, arrived = refs[count + len(jobs) : -2], refs[-2], refs[-1]
    head_count = sources[0].shape[0]
    copies = [
        pltpu.make_async_copy(source, target, arrived.at[i])
        for i, (source, target) in enumerate(zip((owner_ref, *sources), (owners, *held)))
    ]
    for copy in copies:
        copy.start()
    copies[0].wait()
    me = 0 if by_index else lax.axis_index("tp")
    own_head = lax.rem(me, head_count)
    picks = slot_picks(owners, me, [d for d, _ in jobs], cap, tp_size)

    def place(index, head, pick, target_of):
        place_rows(held[index].at[head], pick, target_of)

    shared = [i for i, (_, every) in enumerate(jobs) if every]
    single = [i for i, (_, every) in enumerate(jobs) if not every]
    for index in range(count):
        copies[index + 1].wait()
        for head in range(head_count):
            if shared:
                pick = [picks[head][i] for i in shared]
                place(index, head, pick, [targets[i].at[index, head] for i in shared])
        if single:
            pick = []
            for i in single:
                chosen = picks[0][i]
                for head in range(1, head_count):
                    chosen = jnp.where(own_head == head, picks[head][i], chosen)
                pick.append(chosen)
            place(index, own_head, pick, [targets[i].at[index] for i in single])


def place_pages(page_owner, caches, jobs, cap, tp_size, by_index, follows=()):
    head_count, page_count, width = caches[0].shape
    return call(
        functools.partial(place_kernel, cap, jobs, by_index, tp_size),
        in_hbm(page_owner, *caches),
        [hbm()] * (1 + len(caches)),
        follows,
        out_specs=tuple(vmem() for _ in jobs),
        out_shape=tuple(
            jax.ShapeDtypeStruct(
                (len(caches),) + ((head_count,) if every else ()) + (cap, width), jnp.bfloat16
            )
            for _, every in jobs
        ),
        scratch_shapes=[pltpu.VMEM(cache.shape, cache.dtype) for cache in caches]
        + [
            pltpu.VMEM(page_owner.shape, jnp.int32),
            pltpu.SemaphoreType.DMA((1 + len(caches),)),
        ],
        compiler_params=params(8),
        name="place_pages",
    )


def place_near_kernel(tp_size, head_count, tokens_ref, out_ref):
    cap, width = out_ref.shape[1:]
    held, page_len = (tokens_ref.shape[0] - 1) // 2, tokens_ref.shape[1]
    pages = held - 1
    me = lax.axis_index("tp")
    head = lax.rem(me, head_count)
    lists = tokens_ref[2 * held].astype(jnp.float32)[:, :pages].astype(jnp.int32)
    owner = lists[0:1]
    for which in range(1, head_count):
        owner = jnp.where(head == which, lists[which : which + 1], owner)
    rank = rank_pages(owner, earlier_pages(pages), round_up(tp_size, 8))
    row = lax.broadcasted_iota(jnp.int32, (cap, pages), 0)
    pick = ((owner == me) & (rank == row)).astype(jnp.bfloat16)
    for index in range(2):
        paged = tokens_ref[index * held : index * held + pages].reshape(pages, page_len * HD)
        out_ref[index] = jnp.dot(pick, paged, preferred_element_type=jnp.float32).astype(
            jnp.bfloat16
        )


def place_near(tokens, head_count, cap, tp_size):
    pages, page_len = (tokens.shape[0] - 1) // 2 - 1, tokens.shape[1]
    return call(
        functools.partial(place_near_kernel, tp_size, head_count),
        (tokens,),
        [vmem()],
        out_specs=vmem(),
        out_shape=jax.ShapeDtypeStruct((2, cap, page_len * HD), jnp.bfloat16),
        compiler_params=params(8),
        name="place_near",
    )


def settle_kernel(plan, *refs):
    count = len(plan)
    parts, arrived = refs[:count], refs[-1]
    key_ref, value_ref, done_ref = refs[-4:-1]
    head_count, cap = key_ref.shape[0], parts[0].shape[-2]
    me = lax.axis_index("tp")

    def copies_of(place):
        distance, _, other = plan[place]
        first = pl.multiple_of((me ^ distance) * cap, cap)
        copies = []
        for index, target in enumerate((key_ref, value_ref)):
            for head in range(head_count if other is None else 1):
                source = parts[place].at[index]
                if other is None:
                    source = source.at[head]
                else:
                    head = lax.rem(me + other, head_count)
                copies.append(
                    pltpu.make_async_copy(
                        source,
                        target.at[head, pl.ds(first, cap)],
                        arrived.at[place * 2 * head_count + len(copies)],
                    )
                )
        return copies

    def move(place, action):
        holders = plan[place][1]
        if holders is None:
            for copy in copies_of(place):
                action(copy)
            return
        holds = functools.reduce(lambda a, b: a | b, [me == holder for holder in holders])

        @pl.when(holds)
        def _():
            for copy in copies_of(place):
                action(copy)

    for place in range(count):
        move(place, lambda copy: copy.start())
    done_ref[...] = jnp.zeros_like(done_ref)
    for place in range(count):
        move(place, lambda copy: copy.wait())


def settle(parts, plan, head_count, slots, settled=(), follows=()):
    width = parts[0].shape[-1]
    shape = jax.ShapeDtypeStruct((head_count, slots, width), jnp.bfloat16)
    count = len(parts)
    return call(
        functools.partial(settle_kernel, plan),
        (*parts, *settled),
        [vmem()] * count + [hbm()] * len(settled),
        follows,
        out_specs=(hbm(), hbm(), vmem()),
        out_shape=(shape, shape, jax.ShapeDtypeStruct((8, LANES), jnp.float32)),
        input_output_aliases={count: 0, count + 1: 1} if settled else {},
        scratch_shapes=[pltpu.SemaphoreType.DMA((2 * count * head_count,))],
        compiler_params=params(6),
        name="settle",
    )


def slot_rows_kernel(
    cap, pages, first_lane, page_len, steps, bounds_ref, own_ref, far_ref, out_ref
):
    head_count, slots = out_ref.shape
    tp_size = slots // cap
    me = lax.axis_index("tp")
    earlier = earlier_pages(pages)
    ends = bounds_ref[1:2, :]
    ids = lax.broadcasted_iota(jnp.int32, (pages, ends.shape[1]), 0)
    row = lax.broadcasted_iota(jnp.int32, (cap, pages), 0)
    ones = jnp.ones((8, ends.shape[1]), jnp.bfloat16)
    lines = [[] for _ in range(head_count)]
    for distance in range(tp_size):
        block = me ^ distance
        marks = lax.dot_general(
            ones,
            (ends <= block * pages + ids).astype(jnp.bfloat16),
            (((1,), (1,)), ((), ())),
            preferred_element_type=jnp.float32,
        )
        marks = marks / steps + 1
        source = own_ref if distance < 2 else far_ref
        line = (distance % 2) * page_len
        notes = source[line : line + page_len, -LANES:].astype(jnp.float32)
        notes = pltpu.roll(notes, LANES - first_lane, axis=1)
        for head in range(head_count):
            owner = notes[head : head + 1, :pages].astype(jnp.int32)
            rank = rank_pages(owner, earlier, round_up(tp_size, 8))
            pick = ((owner == me) & (rank == row)).astype(jnp.bfloat16)
            found = lax.dot_general(
                marks.astype(jnp.bfloat16),
                pick,
                (((1,), (1,)), ((), ())),
                preferred_element_type=jnp.float32,
            )
            found = jnp.concatenate([found, jnp.zeros((8, LANES - cap), jnp.float32)], axis=1)
            lines[head].append(pltpu.roll(found, block * cap, axis=1)[:1])
    for head in range(head_count):
        total = lines[head][0]
        for line in lines[head][1:]:
            total = total + line
        out_ref[head : head + 1, :] = total[:, :slots].astype(jnp.int32) - 1


def slot_rows_near(bounds, own, far, pages, first_lane, page_len, cap, shape, steps, follows):
    return call(
        functools.partial(slot_rows_kernel, cap, pages, first_lane, page_len, steps),
        (bounds, own, far),
        [vmem()] * 3,
        follows,
        out_specs=vmem(),
        out_shape=jax.ShapeDtypeStruct(shape, jnp.int32),
        compiler_params=params(2),
        name="slot_rows",
    )


def slot_rows_gathered(page_owner, page_counts, cap):
    owners = lax.all_gather(page_owner, "tp", axis=0, tiled=False)
    tp_size, head_count, pages_here = owners.shape
    rows = jnp.arange(page_counts.shape[0], dtype=jnp.int32)
    row_ends = jnp.sum(jnp.where(rows[None, :] <= rows[:, None], page_counts[None, :], 0), axis=1)
    ids = jnp.arange(pages_here, dtype=jnp.int32)
    same = (owners[..., :, None] == owners[..., None, :]) & (ids[:, None] < ids[None, :])
    rank = jnp.sum(same.astype(jnp.int32), axis=2)
    blocks = jnp.arange(tp_size, dtype=jnp.int32)
    page_ids = blocks[:, None] * pages_here + ids
    page_row = jnp.sum((row_ends <= page_ids[..., None]).astype(jnp.int32), axis=-1)
    slot = jnp.where(owners == lax.axis_index("tp"), blocks[:, None, None] * cap + rank, -1)
    slot_ids = jnp.arange(tp_size * cap, dtype=jnp.int32)
    marks = jnp.where(slot[..., None] == slot_ids, page_row[:, None, :, None] + 1, 0)
    return jnp.sum(marks, axis=(0, 2)) - 1


def gather_tokens_kernel(other, with_queries, handing, *refs):
    key_ref, value_ref, fresh_key_ref, fresh_value_ref, owner_ref = refs[:5]
    arrived = refs[-1]
    if with_queries:
        all_query_ref, count_ref, out_ref, query_ref, bounds_ref = refs[5:10]
        held, fresh, owners, queries, counts = refs[10:15]
    elif handing:
        out_ref, hand_ref, held, fresh, owners = refs[5:10]
    else:
        out_ref, held, fresh, owners = refs[5:9]
    pages, page_len = key_ref.shape[1], out_ref.shape[1]
    head_count, own_rows, steps = key_ref.shape[0], fresh.shape[1], fresh.shape[2]
    me = lax.axis_index("tp")
    head = lax.rem(me + other, head_count)
    pairs = [
        (owner_ref, owners),
        (fresh_key_ref, fresh.at[0]),
        (fresh_value_ref, fresh.at[1]),
    ]
    if handing:
        pairs += [(key_ref, held.at[0]), (value_ref, held.at[1])]
    else:
        pairs += [(key_ref.at[head], held.at[0, 0]), (value_ref.at[head], held.at[1, 0])]
    if with_queries:
        width = query_ref.shape[1]
        columns = pl.ds(pl.multiple_of(head * width, LANES), width)
        pairs += [(count_ref, counts), (all_query_ref.at[:, :, columns], queries)]
    copies = [
        pltpu.make_async_copy(source, target, arrived.at[i])
        for i, (source, target) in enumerate(pairs)
    ]
    for copy in copies:
        copy.start()
    copies[0].wait()
    out_ref[2 * pages + 2] = owner_page(owners[...], page_len).astype(jnp.bfloat16)
    if handing:
        cap = hand_ref.shape[2]
        picks = slot_picks(owners, me, [handing], cap, lax.axis_size("tp"))
    for i in range(2):
        copies[1 + i].wait()
        new = fresh[i]
        part = new[:, :, :HD]
        for which in range(1, head_count):
            part = jnp.where(head == which, new[:, :, which * HD : (which + 1) * HD], part)
        lines = part.reshape(own_rows * steps, HD)
        if own_rows * steps < page_len:
            spare = jnp.zeros((page_len - own_rows * steps, HD), jnp.bfloat16)
            lines = jnp.concatenate([lines, spare])
        out_ref[pages + i * (pages + 1)] = lines
    for i in range(2):
        copies[3 + i].wait()
        first = i * (pages + 1)
        paged = held[i, head] if handing else held[i, 0]
        out_ref[first : first + pages] = paged.reshape(pages, page_len, HD)
    if handing:
        for i in range(2):
            for which in range(head_count):
                place_rows(held.at[i, which], picks[which], [hand_ref.at[i, which]])
    if with_queries:
        copies[5].wait()
        row_lines = query_ref.shape[0]
        row = lax.broadcasted_iota(jnp.int32, (1, row_lines), 1) // steps
        starts = jnp.zeros((1, row_lines), jnp.int32)
        ends = jnp.zeros((1, row_lines), jnp.int32)
        for r in range(counts.shape[0]):
            starts = starts + jnp.where(row > r, counts[r], 0)
            ends = ends + jnp.where(row >= r, counts[r], 0)
        line = lax.broadcasted_iota(jnp.int32, (8, row_lines), 0)
        bounds_ref[...] = jnp.where(line == 0, starts, ends)
        copies[6].wait()
        query_ref[...] = queries[...].reshape(row_lines, query_ref.shape[1])


def owner_page(owners, lines):
    head_count, pages = owners.shape
    page = jnp.concatenate(
        [owners.astype(jnp.float32), jnp.zeros((head_count, LANES - pages), jnp.float32)], axis=1
    )
    return jnp.concatenate([page, jnp.zeros((lines - head_count, LANES), jnp.float32)])


def gather_tokens(
    other, caches, fresh, owner, queries=None, counts=None, handing=0, cap=0, follows=()
):
    head_count, pages, width = caches[0].shape
    page_len = width // HD
    with_queries = queries is not None
    operands = [*caches, *fresh, owner]
    out_shape = [jax.ShapeDtypeStruct((2 * pages + 3, page_len, HD), jnp.bfloat16)]
    scratch = [
        pltpu.VMEM((2, head_count if handing else 1, pages, width), jnp.bfloat16),
        pltpu.VMEM((2,) + fresh[0].shape, jnp.bfloat16),
        pltpu.VMEM(owner.shape, jnp.int32),
    ]
    if handing:
        out_shape.append(jax.ShapeDtypeStruct((2, head_count, cap, width), jnp.bfloat16))
    if with_queries:
        operands += [queries, counts]
        rows, steps, query_width = queries.shape
        query_width = query_width // head_count
        out_shape += [
            jax.ShapeDtypeStruct((rows * steps, query_width), jnp.bfloat16),
            jax.ShapeDtypeStruct((8, rows * steps), jnp.int32),
        ]
        scratch += [
            pltpu.VMEM((rows, steps, query_width), jnp.bfloat16),
            pltpu.SMEM(counts.shape, jnp.int32),
        ]
    return call(
        functools.partial(gather_tokens_kernel, other, with_queries, handing),
        in_hbm(*operands),
        [hbm()] * len(operands),
        follows,
        out_specs=[vmem()] * len(out_shape),
        out_shape=out_shape,
        scratch_shapes=scratch + [pltpu.SemaphoreType.DMA((len(operands),))],
        compiler_params=params(6),
        name="gather_tokens",
    )


def membership(bounds, owner, pages, own_lines, member_lines, row_lines, steps):
    query_line = lax.broadcasted_iota(jnp.int32, (1, row_lines), 1)
    starts, ends = bounds[0:1, :], bounds[1:2, :]
    page_lines = pages * steps
    line = lax.broadcasted_iota(jnp.int32, (member_lines, row_lines), 0)
    page = owner * pages + line // steps
    in_row = (starts <= page) & (page < ends) & (line % steps == query_line % steps)
    own_line = line - page_lines
    is_own = (
        (own_line >= 0) & (own_line < own_lines) & (query_line == owner * own_lines + own_line)
    )
    member = (((line < page_lines) & in_row) | is_own).astype(jnp.float32)
    return member, jnp.transpose(member)


def attend_kernel(steps, own_lines, neighbour, has_earlier, last, *refs):
    bounds_ref, query_ref, tokens_ref = refs[:3]
    refs = refs[3:]
    if has_earlier:
        early_max_ref, early_total_ref, early_numer_ref = refs[:3]
        refs = refs[3:]
    if last:
        if has_earlier:
            own_tokens_ref, refs = refs[0], refs[1:]
        payload_ref, refs = refs[0], refs[1:]
    else:
        out_max_ref, out_total_ref, out_numer_ref = refs[:3]
        refs = refs[3:]
    chosen, numers, high, low = refs

    row_lines, query_width = query_ref.shape
    group = query_width // HD
    held, page_len = (tokens_ref.shape[0] - 1) // 2, tokens_ref.shape[1]
    pages = held - 1
    page_lines = pages * steps
    used_lines = page_lines + page_len
    member_lines = chosen.shape[0]
    scale = HD ** (-0.5)
    lane = lax.broadcasted_iota(jnp.int32, (1, LANES), 1)
    me = lax.axis_index("tp")
    member, member_t = membership(
        bounds_ref[...], me ^ neighbour, pages, own_lines, member_lines, row_lines, steps
    )
    is_member = member_t > 0
    chosen[...] = jnp.dot(
        member.astype(jnp.bfloat16), query_ref[...], preferred_element_type=jnp.float32
    ).astype(jnp.bfloat16)

    maxima, totals = [], []

    def one_block(first_line, lines, keys, values, mask):
        queries = jnp.concatenate(
            [
                chosen[first_line : first_line + lines, g * HD : (g + 1) * HD]
                for g in range(group)
            ],
            axis=0,
        )
        scores = (
            lax.dot_general(
                queries, keys, (((1,), (1,)), ((), ())), preferred_element_type=jnp.float32
            )
            * scale
        )
        scores = jnp.where(mask, scores, NEGATIVE)
        largest = jnp.max(scores, axis=1, keepdims=True)
        weights = jnp.exp(scores - largest).astype(jnp.bfloat16)
        total = jnp.sum(weights.astype(jnp.float32), axis=1, keepdims=True)
        numer = jnp.dot(weights, values, preferred_element_type=jnp.float32)
        block_max = jnp.zeros((lines, LANES), jnp.float32)
        block_total = jnp.zeros((lines, LANES), jnp.float32)
        for g in range(group):
            part = slice(g * lines, (g + 1) * lines)
            block_max = jnp.where(lane == g, largest[part], block_max)
            block_total = jnp.where(lane == g, total[part], block_total)
            numers[first_line : first_line + lines, g * HD : (g + 1) * HD] = numer[part]
        maxima.append(block_max)
        totals.append(block_total)

    batch = min(pages, max(1, 128 // page_len))
    lines = batch * steps
    line = lax.broadcasted_iota(jnp.int32, (group * lines, batch * page_len), 0)
    token = lax.broadcasted_iota(jnp.int32, (group * lines, batch * page_len), 1)
    mask = (line % lines) // steps == token // page_len
    for first in range(0, pages, batch):
        one_block(
            first * steps,
            lines,
            tokens_ref[first : first + batch].reshape(batch * page_len, HD),
            tokens_ref[held + first : held + first + batch].reshape(batch * page_len, HD),
            mask,
        )
    line = lax.broadcasted_iota(jnp.int32, (group * page_len, page_len), 0) % page_len
    token = lax.broadcasted_iota(jnp.int32, (group * page_len, page_len), 1)
    mask = (line // steps == token // steps) & (token % steps <= line % steps)
    one_block(page_lines, page_len, tokens_ref[pages], tokens_ref[held + pages], mask)

    spare = member_lines - used_lines
    if spare:
        maxima.append(jnp.zeros((spare, LANES), jnp.float32))
        totals.append(jnp.zeros((spare, LANES), jnp.float32))
    line_max = jnp.concatenate(maxima, axis=0)
    line_total = jnp.concatenate(totals, axis=0)

    line_max_t = jnp.transpose(line_max)
    row_max = jnp.full((row_lines, LANES), NEGATIVE, jnp.float32)
    for g in range(group):
        best = jnp.max(
            jnp.where(is_member, line_max_t[g : g + 1, :], NEGATIVE), axis=1, keepdims=True
        )
        row_max = jnp.where(lane == g, best, row_max)
    spread = jnp.dot(
        member,
        row_max,
        precision=HIGHEST,
        preferred_element_type=jnp.float32,
    )
    factor = jnp.exp(jnp.minimum(line_max - spread, 0.0))
    row_total = jnp.dot(
        member_t,
        line_total * factor,
        precision=HIGHEST,
        preferred_element_type=jnp.float32,
    )
    turned = member_t.astype(jnp.bfloat16)
    if spare:
        high[used_lines:, :] = jnp.zeros((spare, query_width), jnp.bfloat16)
        low[used_lines:, :] = jnp.zeros((spare, query_width), jnp.bfloat16)
    for g in range(group):
        columns = slice(g * HD, (g + 1) * HD)
        scaled = numers[:, columns] * factor[:used_lines, g : g + 1]
        rounded = scaled.astype(jnp.bfloat16)
        high[:used_lines, columns] = rounded
        low[:used_lines, columns] = (scaled - rounded.astype(jnp.float32)).astype(jnp.bfloat16)

    if has_earlier:
        early_max = early_max_ref[...]
        largest = jnp.maximum(row_max, early_max)
        scale_now = jnp.exp(row_max - largest)
        scale_early = jnp.exp(early_max - largest)
        row_total = row_total * scale_now + early_total_ref[...] * scale_early
        row_max = largest
    if last:
        present = row_total > 0
        inverse = jnp.where(present, 1.0 / jnp.where(present, row_total, 1.0), 0.0)
        log_sum = jnp.where(
            present & (lane < group),
            row_max + jnp.log(jnp.where(present, row_total, 1.0)),
            jnp.where(lane < group, NEGATIVE, 0.0),
        )
        if has_earlier:
            scale_now = scale_now * inverse
            scale_early = scale_early * inverse
        else:
            scale_now = inverse
        lanes = split_sums(log_sum, group)
        if has_earlier:
            lanes = lanes + owner_notes(
                own_tokens_ref[2 * held], tokens_ref[2 * held], row_lines, 3 * group
            )
        payload_ref[:, query_width:] = lanes.astype(jnp.bfloat16)
    for g in range(group):
        columns = slice(g * HD, (g + 1) * HD)
        numer = jnp.dot(
            turned, high[:, columns], preferred_element_type=jnp.float32
        ) + jnp.dot(turned, low[:, columns], preferred_element_type=jnp.float32)
        if has_earlier:
            numer = (
                numer * scale_now[:, g : g + 1]
                + early_numer_ref[:, columns] * scale_early[:, g : g + 1]
            )
        elif last:
            numer = numer * scale_now[:, g : g + 1]
        if last:
            payload_ref[:, columns] = numer.astype(jnp.bfloat16)
        else:
            out_numer_ref[:, columns] = numer
    if not last:
        out_max_ref[...] = row_max
        out_total_ref[...] = row_total


def split_sums(value, group):
    first = value.astype(jnp.bfloat16).astype(jnp.float32)
    rest = value - first
    second = rest.astype(jnp.bfloat16).astype(jnp.float32)
    third = rest - second
    return first + pltpu.roll(second, group, axis=1) + pltpu.roll(third, 2 * group, axis=1)


def owner_notes(own, near_page, row_lines, first_lane):
    lines = near_page.shape[0]
    notes = jnp.concatenate(
        [
            own.astype(jnp.float32),
            near_page.astype(jnp.float32),
            jnp.zeros((row_lines - 2 * lines, LANES), jnp.float32),
        ]
    )
    return pltpu.roll(notes, first_lane, axis=1)


def join_sums(parts, group):
    parts = parts.astype(jnp.float32)
    return (
        parts
        + pltpu.roll(parts, LANES - group, axis=1)
        + pltpu.roll(parts, LANES - 2 * group, axis=1)
    )


def attend(
    bounds, query, tokens, neighbour, own_lines, steps, earlier, own_tokens, last, follows=()
):
    row_lines, query_width = query.shape
    group = query_width // HD
    held, page_len = (tokens.shape[0] - 1) // 2, tokens.shape[1]
    used_lines = (held - 1) * steps + page_len
    member_lines = round_up(used_lines, LANES)
    stat = jax.ShapeDtypeStruct((row_lines, LANES), jnp.float32)
    if last:
        out_shape = (jax.ShapeDtypeStruct((row_lines, query_width + LANES), jnp.bfloat16),)
    else:
        out_shape = (stat, stat, jax.ShapeDtypeStruct((row_lines, query_width), jnp.float32))
    operands = (bounds, query, tokens, *earlier, *own_tokens)
    return call(
        functools.partial(
            attend_kernel, steps, own_lines, neighbour, bool(earlier), last
        ),
        operands,
        [vmem()] * len(operands),
        follows,
        out_specs=tuple(vmem() for _ in out_shape),
        out_shape=out_shape,
        scratch_shapes=[
            pltpu.VMEM((member_lines, query_width), jnp.bfloat16),
            pltpu.VMEM((used_lines, query_width), jnp.float32),
            pltpu.VMEM((member_lines, query_width), jnp.bfloat16),
            pltpu.VMEM((member_lines, query_width), jnp.bfloat16),
        ],
        compiler_params=params(12),
        name="attend",
    )


def combine_kernel(group, mine_ref, theirs_ref, *out_refs):
    sums = join_sums(mine_ref[:, -LANES:], group)
    their_sums = join_sums(theirs_ref[:, -LANES:], group)
    largest = jnp.maximum(sums, their_sums)
    weight = jnp.exp(sums - largest)
    their_weight = jnp.exp(their_sums - largest)
    inverse = 1.0 / (weight + their_weight)
    weight = weight * inverse
    their_weight = their_weight * inverse
    part = group // len(out_refs)
    for g in range(group):
        columns = slice(g * HD, (g + 1) * HD)
        place = g % part
        out_refs[g // part][:, place * HD : (place + 1) * HD] = (
            mine_ref[:, columns].astype(jnp.float32) * weight[:, g : g + 1]
            + theirs_ref[:, columns].astype(jnp.float32) * their_weight[:, g : g + 1]
        ).astype(jnp.bfloat16)


def combine(mine, theirs, chunks, follows=()):
    row_lines, width = mine.shape
    group = (width - LANES) // HD
    shape = jax.ShapeDtypeStruct((row_lines, group // chunks * HD), jnp.bfloat16)
    return call(
        functools.partial(combine_kernel, group),
        (mine, theirs),
        [vmem()] * 2,
        follows,
        out_specs=[vmem()] * chunks,
        out_shape=[shape] * chunks,
        compiler_params=params(4),
        name="combine",
    )


def block_row(own, chunk, chunks, head_count, depth):
    head = lax.rem(lax.axis_index("tp") + (0 if own else 1), head_count)
    return pl.multiple_of((head * chunks + chunk) * depth, depth)


def fetch_kernel(blocks, chunks, head_count, weight_ref, held_ref, done_ref, arrived):
    depth = held_ref.shape[0] // len(blocks)
    pieces = arrived.shape[0] // len(blocks)
    size = depth // pieces
    copies = []
    for place, (own, chunk) in enumerate(blocks):
        base = block_row(own, chunk, chunks, head_count, depth)
        for piece in range(pieces):
            copies.append(
                pltpu.make_async_copy(
                    weight_ref.at[pl.ds(pl.multiple_of(base + piece * size, size), size)],
                    held_ref.at[pl.ds(place * depth + piece * size, size)],
                    arrived.at[place * pieces + piece],
                )
            )
    for copy in copies:
        copy.start()
    done_ref[...] = jnp.zeros_like(done_ref)
    for copy in copies:
        copy.wait()


def fetch(weight, blocks, chunks, head_count, depth, follows):
    pieces = 4
    return call(
        functools.partial(fetch_kernel, blocks, chunks, head_count),
        in_hbm(weight),
        [hbm()],
        follows,
        out_specs=(vmem(), vmem()),
        out_shape=(
            pltpu.VMEM((len(blocks) * depth, weight.shape[1]), weight.dtype),
            jax.ShapeDtypeStruct((8, LANES), jnp.float32),
        ),
        scratch_shapes=[pltpu.SemaphoreType.DMA((len(blocks) * pieces,))],
        compiler_params=params(1),
        name="fetch",
    )


def project_kernel(parts, has_total, chunk_lines, first, offsets, chunks, head_count, *refs):
    input_refs, weight_ref, refs = refs[:parts], refs[parts], refs[parts + 1 :]
    streamed = offsets is None
    if streamed:
        held, arrived = refs[-2:]
        refs = refs[:-2]
    outs = refs[1:] if has_total else refs
    depth, width = input_refs[0].shape[1], outs[0].shape[-1]
    block = min(width, 512)
    count = width // block

    def piece(index):
        return pltpu.make_async_copy(
            weight_ref.at[
                pl.ds(block_row(True, 0, chunks, head_count, depth), depth),
                pl.ds(first + index * block, block),
            ],
            held.at[:, pl.ds(index * block, block)],
            arrived.at[index],
        )

    if streamed:
        for index in range(count):
            piece(index).start()
    for index in range(count):
        start = index * block
        columns = slice(first + start, first + start + block)
        product = refs[0][:, columns] if has_total else 0.0
        if streamed:
            piece(index).wait()
            product = product + jnp.dot(
                input_refs[0][...],
                held[:, start : start + block],
                preferred_element_type=jnp.float32,
            )
        else:
            for input_ref, offset in zip(input_refs, offsets):
                product = product + jnp.dot(
                    input_ref[...],
                    weight_ref[offset * depth : (offset + 1) * depth, columns],
                    preferred_element_type=jnp.float32,
                )
        if chunk_lines is None:
            outs[0][:, start : start + block] = product
            continue
        core = lax.rem(lax.axis_index("kv"), 2)
        keep_ref, send_ref = outs
        for pair in range(keep_ref.shape[0]):
            even = product[2 * pair * chunk_lines : (2 * pair + 1) * chunk_lines]
            odd = product[(2 * pair + 1) * chunk_lines : (2 * pair + 2) * chunk_lines]
            keep_ref[pair, :, start : start + block] = jnp.where(core == 0, even, odd)
            send_ref[pair, :, start : start + block] = jnp.where(core == 0, odd, even).astype(
                send_ref.dtype
            )


def project(inputs, weight, offsets, chunks, head_count, total, columns, chunk_lines, follows=()):
    row_lines, depth = inputs[0].shape
    first, width = columns
    in_specs = [vmem()] * len(inputs) + [hbm() if offsets is None else vmem()]
    operands = [*inputs, *(in_hbm(weight) if offsets is None else [weight])]
    if total is not None:
        in_specs.append(vmem())
        operands.append(total)
    if chunk_lines is None:
        out_shape = jax.ShapeDtypeStruct((row_lines, width), jnp.float32)
        out_specs = vmem()
    else:
        pairs = row_lines // (2 * chunk_lines)
        shape = (pairs, chunk_lines, width)
        out_shape = (
            jax.ShapeDtypeStruct(shape, jnp.float32),
            jax.ShapeDtypeStruct(shape, jnp.bfloat16),
        )
        out_specs = (vmem(), vmem())
    scratch = []
    if offsets is None:
        scratch = [
            pltpu.VMEM((depth, width), weight.dtype),
            pltpu.SemaphoreType.DMA((max(1, width // 512),)),
        ]
    return call(
        functools.partial(
            project_kernel,
            len(inputs),
            total is not None,
            chunk_lines,
            first,
            offsets,
            chunks,
            head_count,
        ),
        operands,
        in_specs,
        follows,
        out_specs=out_specs,
        out_shape=out_shape,
        scratch_shapes=scratch,
        compiler_params=params(16 if offsets is None else 8),
        name="project",
    )


def add_core_kernel(keep_ref, got_ref, own_ref, *send_refs):
    half = lax.axis_index("kv") // 2
    own_ref[...] = keep_ref[half] + got_ref[half].astype(jnp.float32)
    for step, send_ref in enumerate(send_refs, 1):
        part = keep_ref[half ^ step] + got_ref[half ^ step].astype(jnp.float32)
        send_ref[...] = part.astype(send_ref.dtype)


def sum_heads(keep, send, kv_size):
    got = lax.ppermute(send, "kv", flip(kv_size, 1))
    shape = keep.shape[1:]
    own, *sends = call(
        add_core_kernel,
        (keep, got),
        [vmem(), vmem()],
        out_specs=[vmem()] * (kv_size // 2),
        out_shape=[jax.ShapeDtypeStruct(shape, jnp.float32)]
        + [jax.ShapeDtypeStruct(shape, jnp.bfloat16)] * (kv_size // 2 - 1),
        compiler_params=params(4),
        name="add_core",
    )
    return [own] + [
        lax.ppermute(part, "kv", flip(kv_size, 2 * step)) for step, part in enumerate(sends, 1)
    ]


def finish_kernel(pieces, *refs):
    parts, out_ref, done_ref = refs[:-2], refs[-2], refs[-1]
    done_ref[...] = jnp.zeros_like(done_ref)
    each = len(parts) // pieces
    steps, width = out_ref.shape[1], out_ref.shape[2] // pieces
    for piece in range(pieces):
        total = parts[piece * each][...]
        for part in parts[piece * each + 1 : (piece + 1) * each]:
            total = total + part[...].astype(jnp.float32)
        out_ref[:, :, piece * width : (piece + 1) * width] = total.astype(jnp.bfloat16).reshape(
            -1, steps, width
        )


def finish(results, steps):
    lines, width = results[0][0].shape
    parts = [part for pieces in results for part in pieces]
    return call(
        functools.partial(finish_kernel, len(results)),
        parts,
        [vmem()] * len(parts),
        out_specs=(vmem(), vmem()),
        out_shape=(
            jax.ShapeDtypeStruct((lines // steps, steps, width * len(results)), jnp.bfloat16),
            jax.ShapeDtypeStruct((8, LANES), jnp.float32),
        ),
        compiler_params=params(4),
        name="finish",
    )


def body(
    queries, fresh_keys, fresh_values, cache_keys, cache_values, page_counts, page_owner, out_weight
):
    tp_size, kv_size = lax.axis_size("tp"), lax.axis_size("kv")
    head_count, pages_here, page_width = cache_keys.shape
    row_count, step_count, query_width = queries.shape
    own_lines = fresh_keys.shape[0] * step_count
    page_len = page_width // HD
    row_lines = row_count * step_count
    head_width = query_width // head_count
    group = head_width // HD
    cap = max(2, (2 * pages_here + tp_size - 1) // tp_size)
    out_width = out_weight.shape[1]
    chunk_lines = row_lines // kv_size
    caches = (cache_keys, cache_values)
    fresh = (fresh_keys, fresh_values)

    paired = head_count == 2 and tp_size == 4 and group % 2 == 0 and cap % 16 == 0
    paired = paired and 3 * group + pages_here <= LANES and 2 * page_len <= row_lines
    chunks = 2 if paired else 1
    part = head_width // chunks
    everything = (0, out_width)

    if paired:
        tokens, send_last = gather_tokens(1, caches, fresh, page_owner, handing=3, cap=cap)
        near_tokens = lax.ppermute(tokens, "tp", flip(tp_size, 1))
        got_inner = lax.ppermute(send_last, "tp", [(1, 2), (2, 1)])
        own_tokens, query, bounds = gather_tokens(
            0, caches, fresh, page_owner, queries, page_counts, follows=(send_last,)
        )
        shapes = (own_lines, step_count)
        earlier = attend(bounds, query, own_tokens, 0, *shapes, (), (), False)
        jobs = ((2, True), (1, False), (0, True))
        send_far, send_near, kept = place_pages(
            page_owner, caches, jobs, cap, tp_size, False, (earlier[0],)
        )
        (payload,) = attend(
            bounds, query, near_tokens, 1, *shapes, earlier, (own_tokens,), True, (kept,)
        )
        payload = tie(payload, got_inner)
        theirs = lax.ppermute(payload, "tp", flip(tp_size, 2))
        blocks = ((True, 1), (False, 0), (False, 1))
        held, held_done = fetch(out_weight, blocks, chunks, head_count, part, (payload,))
        got_near = lax.ppermute(tie(send_near, held_done), "tp", flip(tp_size, 1))
        near_pages = place_near(near_tokens, head_count, cap, tp_size)
        own_parts = combine(payload, theirs, chunks, (got_near,))
        near_parts = [lax.ppermute(p, "tp", flip(tp_size, 1)) for p in own_parts]
        got_far = lax.ppermute(tie(send_far, own_parts[0]), "tp", flip(tp_size, 2))
        got_outer = lax.ppermute(tie(send_last, own_parts[0]), "tp", [(0, 3), (3, 0)])
        total = project(
            own_parts[:1], out_weight, None, chunks, head_count, None, everything, None
        )
        plan = ((0, None, None), (1, None, 0), (1, None, 1), (3, (1, 2), None))
        *settled, settled_done = settle(
            [kept, near_pages, got_near, got_inner], plan, head_count, tp_size * cap, (), (total,)
        )
        total = project(
            [own_parts[1], near_parts[0]],
            held,
            (0, 1),
            chunks,
            head_count,
            total,
            everything,
            None,
            (settled_done,),
        )
        results = []
        for first in (0, out_width // 2):
            columns = (first, out_width // 2)
            keep, send = project(
                [near_parts[1]], held, (2,), chunks, head_count, total, columns, chunk_lines
            )
            results.append(sum_heads(keep, send, kv_size))
        attention_out, finished = finish(results, step_count)
        slot_rows = slot_rows_near(
            bounds,
            payload,
            theirs,
            pages_here,
            3 * group,
            page_len,
            cap,
            (head_count, tp_size * cap),
            step_count,
            (results[1][0],),
        )
        plan = ((2, None, None), (3, (0, 3), None))
        slot_keys, slot_values, _ = settle(
            [got_far, got_outer], plan, head_count, tp_size * cap, settled, (finished,)
        )
        return (attention_out, slot_keys, slot_values, slot_rows)

    def hand_over(cache):
        jobs = tuple((d, True) for d in range(tp_size))
        sent = place_pages(page_owner, (cache,), jobs, cap, tp_size, True)
        got = lax.all_to_all(
            jnp.concatenate(sent), "tp", split_axis=0, concat_axis=0, tiled=True
        )
        return got.transpose(1, 0, 2, 3).reshape(head_count, tp_size * cap, page_width)

    slot_keys, slot_values = hand_over(cache_keys), hand_over(cache_values)
    slot_rows = slot_rows_gathered(page_owner, page_counts, cap)
    attended = []
    for head in range(head_count):
        cut = slice(head, head + 1)
        lanes = slice(head * HD, (head + 1) * HD)
        tokens, query, bounds = gather_tokens(
            0,
            [cache[cut] for cache in caches],
            [new[:, :, lanes] for new in fresh],
            page_owner[cut],
            queries[:, :, head * head_width : (head + 1) * head_width],
            page_counts,
        )
        (payload,) = attend(
            bounds, query, tokens, 0, own_lines, step_count, (), (), True
        )
        raw = payload[:, part:].astype(jnp.float32)
        sums = raw[:, :group] + raw[:, group : 2 * group] + raw[:, 2 * group : 3 * group]
        weight = jnp.exp(sums - lax.pmax(sums, "tp"))
        numer = payload[:, :part].astype(jnp.float32).reshape(row_lines, group, HD)
        numer = lax.psum(numer * weight[..., None], "tp")
        joined = numer / lax.psum(weight, "tp")[..., None]
        attended.append(joined.reshape(row_lines, head_width).astype(jnp.bfloat16))
    keep, send = project(
        [jnp.concatenate(attended, axis=1)], out_weight, None, 1, 1, None, everything, chunk_lines
    )
    attention_out, _ = finish([sum_heads(keep, send, kv_size)], step_count)
    return (attention_out, slot_keys, slot_values, slot_rows)


def solution(mesh):
    return jax.shard_map(
        body,
        mesh=mesh,
        in_specs=(
            P("grp", None, "kv"),
            P(("grp", "tp"), None, "kv"),
            P(("grp", "tp"), None, "kv"),
            P(("grp", "kv"), "tp", None),
            P(("grp", "kv"), "tp", None),
            P("grp"),
            P(("grp", "kv"), "tp"),
            P("kv", "tp"),
        ),
        out_specs=(
            P(("grp", "kv"), None, "tp"),
            P(("grp", "kv"), "tp", None),
            P(("grp", "kv"), "tp", None),
            P(("grp", "kv"), "tp"),
        ),
        check_vma=False,
    )
```

time: 130 us -> 90.2 us (0.69)
  blocking collectives: 25.7 us -> 0 us
  local copies, waits for them, and re-layouts: 9.52 us -> 0 us
  waiting for transfers between devices: 43.8 us -> 37.6 us
  Pallas kernels: 30.3 us -> 33.4 us
  other arithmetic: 2.63 us -> 0 us
    all_gather x1 -> x0, blocking collectives: 25.7 us -> none  [list_slot_rows(): owners = lax.all_gather(page_owner, 'tp', axis=1, tiled=False)]
    all_to_all x2 -> x0, waiting for transfers between devices: 17.5 us -> none  [hand_over(): got = lax.all_to_all(pages, 'tp', split_axis=0, concat_axis=0, tiled=True)]
    all_to_all x2 -> x0, starting transfers between devices: 7.92 us -> none  [hand_over(): got = lax.all_to_all(pages, 'tp', split_axis=0, concat_axis=0, tiled=True)]
    ppermute x2, waiting for transfers between devices: 0.46 us -> 7.57 us  [body(): near_parts = [lax.ppermute(p, 'tp', flip(tp_size, 1)) for p in own_parts]]
    ppermute x7 -> x10, starting transfers between devices: 8.87 us -> 15.9 us  [the longest x1 3.72 us: body(): lax.ppermute(tie(send_last, own_parts[0]), 'tp', [(0, 3), (3, 0)])]
    ppermute x7 -> x10, waiting for transfers between devices: 25.8 us -> 30 us  [the longest x1 16.3 us: body(): got_near = lax.ppermute(tie(send_near, held_done), 'tp', flip(tp_size, 1))]
    reshape x4 -> x0, local copies, waits for them, and re-layouts: 3.67 us -> none  [the longest x2 1.52 us: by_head(): fresh.reshape(own_rows * step_count, head_count, HD).transpose(1, 0, 2)]
    transpose x2 -> x0, local copies, waits for them, and re-layouts: 3.33 us -> none  [hand_over(): got.transpose(1, 0, 2, 3).reshape(head_count, tp_size * cap, page_width)]
  transfers between devices with their start and end apart: 11 -> 12, of which waited for: 5 -> 8; matrix products, arithmetic and copies ran while one was open for 6% -> 0% of each run, Pallas kernels for 23% -> 33%
where the time goes in v2:
time: 90.2 us; the launch traced here: 90 us
  waiting for transfers between devices  37.6 us (42%)
  Pallas kernels  33.4 us (37%)
  starting transfers between devices  18 us (20%)
  between operations  0.95 us (1%)
    pallas_call x22, Pallas kernels, call(): pl.pallas_call(without_extra, in_specs=list(in_specs) + [anywhere()] * ex...  33.4 us
    ppermute x1, waiting for transfers between devices, body(): got_near = lax.ppermute(tie(send_near, held_done), 'tp', flip(tp_size, 1))  16.3 us
    ppermute x2, waiting for transfers between devices, body(): near_parts = [lax.ppermute(p, 'tp', flip(tp_size, 1)) for p in own_parts]  7.57 us
    ppermute x1, waiting for transfers between devices, body(): near_tokens = lax.ppermute(tokens, 'tp', flip(tp_size, 1))  5.7 us
    ppermute x2, waiting for transfers between devices, sum_heads(): lax.ppermute(part, 'kv', flip(kv_size, 2 * step))  4.48 us
    ppermute x1, starting transfers between devices, body(): lax.ppermute(tie(send_last, own_parts[0]), 'tp', [(0, 3), (3, 0)])  3.72 us
    ppermute x1, waiting for transfers between devices, body(): got_far = lax.ppermute(tie(send_far, own_parts[0]), 'tp', flip(tp_size, 2))  3.39 us
    ppermute x1, starting transfers between devices, body(): near_tokens = lax.ppermute(tokens, 'tp', flip(tp_size, 1))  3.09 us
  transfers between devices with their start and end apart: 12, of which 8 were waited for; matrix products, arithmetic and copies ran while one was open for 0% of the time, Pallas kernels for 33%

profile of v2, /device:TPU:0, one launch (start us, length us, event | category | flops | bytes accessed | tf_op | source)
XLA Modules:
  0.0 90.0 jit_solution(12543213416335465825)
XLA Ops:
  0.6 1.7 %gather_tokens.2 = (bf16[67,32,128]{2,1,0:T(8,128)(2,1)S(1)}, bf16[2,2,16,4096]{3,2,1,0:T(8,128)(2,1)S(1)}) custom-call(bf16[2,32,4096]{2,1,0:T(8,128)(2,1)} %refs_1_.6, bf16[2,32,4096]{2,1,0:T(8,128)(2,1)} %refs_2_.5, bf16[8,4,256]{2,1,0:T(4,128)(2,1)} %refs_2_.4, bf16[8,4,256]{2,1,0:T(4,128)(2,1)} %refs_3_.3, s32[2,32]{1,0:T(2,128)} %refs_0_.6), custom_call_target="tpu_custom_call" | custom-call | tf_op jit(solution)/shard_map/gather_tokens/pallas_call | solution.py:51
  2.3 3.1 %collective-permute-start = (bf16[67,32,128]{2,1,0:T(8,128)(2,1)S(1)}, bf16[67,32,128]{2,1,0:T(8,128)(2,1)S(1)}, u32[]{:S(2)}, u32[]{:S(2)}) collective-permute-start(bf16[67,32,128]{2,1,0:T(8,128)(2,1)S(1)} %get-tuple-element.37), channel_id=1, source_target_pairs={{0,4},{4,0},{8,12},{12,8},{1,5},{5,1},{9,13},{13,9},{2,6},{6,2},{1... | collective-permute-start | bytes 1646600 | tf_op jit(solution)/shard_map/ppermute | solution.py:976
  5.4 0.7 collective-permute-start.1
  6.1 1.4 %gather_tokens.3 = (bf16[67,32,128]{2,1,0:T(8,128)(2,1)S(1)}, bf16[128,2048]{1,0:T(8,128)(2,1)S(1)}, s32[8,128]{1,0:T(8,128)S(1)}) custom-call(bf16[2,32,4096]{2,1,0:T(8,128)(2,1)} %refs_1_.6, bf16[2,32,4096]{2,1,0:T(8,128)(2,1)} %refs_2_.5, bf16[8,4,256]{2,1,0:T(4,128)(2,1)} %refs_2_.4, bf16[8,4,256]{2,1,0:T(4,128)(2,1)} %refs_3_.3, s32[2,32]{1,0:T(2,128)} %refs_0_.6, ...), custom_call_target="tpu_custom_call" | custom-call | tf_op jit(solution)/shard_map/gather_tokens/pallas_call | solution.py:51
  7.5 2.9 %attend.2 = (f32[128,128]{1,0:T(8,128)S(1)}, f32[128,128]{1,0:T(8,128)S(1)}, f32[128,2048]{1,0:T(8,128)S(1)}) custom-call(s32[8,128]{1,0:T(8,128)S(1)} %get-tuple-element.35.refs_0_, bf16[128,2048]{1,0:T(8,128)(2,1)S(1)} %get-tuple-element.36.refs_1_, bf16[67,32,128]{2,1,0:T(8,128)(2,1)S(1)} %get-tuple-element.38.refs_2_.refs_6_), custom_call_target="tpu_custom_call" | custom-call | tf_op jit(solution)/shard_map/attend/pallas_call | solution.py:51
  10.4 1.7 %place_pages.1 = (bf16[2,2,16,4096]{3,2,1,0:T(8,128)(2,1)S(1)}, bf16[2,16,4096]{2,1,0:T(8,128)(2,1)S(1)}, bf16[2,2,16,4096]{3,2,1,0:T(8,128)(2,1)S(1)}) custom-call(s32[2,32]{1,0:T(2,128)} %refs_0_.6, bf16[2,32,4096]{2,1,0:T(8,128)(2,1)} %refs_1_.6, bf16[2,32,4096]{2,1,0:T(8,128)(2,1)} %refs_2_.5, f32[128,128]{1,0:T(8,128)S(1)} %get-tuple-element.39.refs_3_), custom_call_target="tpu_custom_call" | custom-call | tf_op jit(solution)/shard_map/place_pages/pallas_call | solution.py:51
  12.1 5.7 %collective-permute-done.refs_2_.refs_0_ = bf16[67,32,128]{2,1,0:T(8,128)(2,1)S(1)} collective-permute-done((bf16[67,32,128]{2,1,0:T(8,128)(2,1)S(1)}, bf16[67,32,128]{2,1,0:T(8,128)(2,1)S(1)}, u32[]{:S(2)}, u32[]{:S(2)}) %collective-permute-start) | collective-permute-done | bytes 548896 | tf_op jit(solution)/shard_map/ppermute | solution.py:976
  17.8 3.4 %attend.3.refs_0_ = bf16[128,2176]{1,0:T(8,128)(2,1)S(1)} custom-call(s32[8,128]{1,0:T(8,128)S(1)} %get-tuple-element.35.refs_0_, bf16[128,2048]{1,0:T(8,128)(2,1)S(1)} %get-tuple-element.36.refs_1_, bf16[67,32,128]{2,1,0:T(8,128)(2,1)S(1)} %collective-permute-done.refs_2_.refs_0_, f32[128,128]{1,0:T(8,128)S(1)} %get-tuple-element.39.refs_3_, ...), custom_call_target="tpu_custom_call" | custom-call | tf_op jit(solution)/shard_map/attend/pallas_call | solution.py:51
  21.2 0.0 collective-permute-done.1.refs_1_.refs_3_
  21.2 2.8 %collective-permute-start.2 = (bf16[128,2176]{1,0:T(8,128)(2,1)S(1)}, bf16[128,2176]{1,0:T(8,128)(2,1)S(1)}, u32[]{:S(2)}, u32[]{:S(2)}) collective-permute-start(bf16[128,2176]{1,0:T(8,128)(2,1)S(1)} %tie.4.refs_1_.refs_0_), channel_id=1, source_target_pairs={{0,8},{4,12},{8,0},{12,4},{1,9},{5,13},{9,1},{13,5},{2,10},{6,14},... | collective-permute-start | bytes 1671176 | tf_op jit(solution)/shard_map/ppermute | solution.py:991
  24.0 8.3 %fetch.1 = (bf16[3072,4096]{1,0:T(8,128)(2,1)S(1)}, f32[8,128]{1,0:T(8,128)S(1)}) custom-call(bf16[4096,4096]{1,0:T(8,128)(2,1)} %refs_1_.7, bf16[128,2176]{1,0:T(8,128)(2,1)S(1)} %tie.4.refs_1_.refs_0_), custom_call_target="tpu_custom_call" | custom-call | tf_op jit(solution)/shard_map/fetch/pallas_call | solution.py:51
  32.4 1.6 %collective-permute-start.3 = (bf16[2,16,4096]{2,1,0:T(8,128)(2,1)S(1)}, bf16[2,16,4096]{2,1,0:T(8,128)(2,1)S(1)}, u32[]{:S(2)}, u32[]{:S(2)}) collective-permute-start(bf16[2,16,4096]{2,1,0:T(8,128)(2,1)S(1)} %tie.5), channel_id=1, source_target_pairs={{0,4},{4,0},{8,12},{12,8},{1,5},{5,1},{9,13},{13,9},{2,6},{6,2},{1... | collective-permute-start | bytes 786440 | tf_op jit(solution)/shard_map/ppermute | solution.py:994
  34.0 16.3 %collective-permute-done.3.refs_2_ = bf16[2,16,4096]{2,1,0:T(8,128)(2,1)S(1)} collective-permute-done((bf16[2,16,4096]{2,1,0:T(8,128)(2,1)S(1)}, bf16[2,16,4096]{2,1,0:T(8,128)(2,1)S(1)}, u32[]{:S(2)}, u32[]{:S(2)}) %collective-permute-start.3) | collective-permute-done | bytes 262176 | tf_op jit(solution)/shard_map/ppermute | solution.py:994
  50.3 0.0 collective-permute-done.2.refs_1_.refs_2_
  50.4 0.8 combine.1
  51.1 0.1 collective-permute-start.5
  51.2 2.0 %collective-permute-start.4 = (bf16[128,1024]{1,0:T(8,128)(2,1)S(1)}, bf16[128,1024]{1,0:T(8,128)(2,1)S(1)}, u32[]{:S(2)}, u32[]{:S(2)}) collective-permute-start(bf16[128,1024]{1,0:T(8,128)(2,1)S(1)} %get-tuple-element.45.refs_0_), channel_id=1, source_target_pairs={{0,4},{4,0},{8,12},{12,8},{1,5},{5,1},{9,13},{13,9},{2,6},{6,2},{1... | collective-permute-start | bytes 786440 | tf_op jit(solution)/shard_map/ppermute | solution.py:997
  53.2 0.8 collective-permute-start.10
  54.0 3.7 %collective-permute-start.11 = (bf16[2,2,16,4096]{3,2,1,0:T(8,128)(2,1)S(1)}, bf16[2,2,16,4096]{3,2,1,0:T(8,128)(2,1)S(1)}, u32[]{:S(2)}, u32[]{:S(2)}) collective-permute-start(bf16[2,2,16,4096]{3,2,1,0:T(8,128)(2,1)S(1)} %tie.7), channel_id=1, source_target_pairs={{0,12},{12,0},{1,13},{13,1},{2,14},{14,2},{3,15},{15,3},{16,28},{2... | collective-permute-start | bytes 1572872 | tf_op jit(solution)/shard_map/ppermute | solution.py:999
  57.7 0.4 place_near.1.refs_1_
  58.1 3.9 %project.4.refs_4_.refs_3_ = f32[128,4096]{1,0:T(8,128)S(1)} custom-call(bf16[128,1024]{1,0:T(8,128)(2,1)S(1)} %get-tuple-element.47.refs_0_.refs_1_, bf16[4096,4096]{1,0:T(8,128)(2,1)} %refs_1_.7), custom_call_target="tpu_custom_call" | custom-call | tf_op jit(solution)/shard_map/project/pallas_call | solution.py:51
  62.0 1.1 %settle.2 = (bf16[2,64,4096]{2,1,0:T(8,128)(2,1)}, bf16[2,64,4096]{2,1,0:T(8,128)(2,1)}, f32[8,128]{1,0:T(8,128)S(1)}) custom-call(bf16[2,2,16,4096]{3,2,1,0:T(8,128)(2,1)S(1)} %get-tuple-element.42.refs_7_.refs_0_, bf16[2,16,4096]{2,1,0:T(8,128)(2,1)S(1)} %place_near.1.refs_1_, bf16[2,16,4096]{2,1,0:T(8,128)(2,1)S(1)} %collective-permute-done.3.refs_2_, ...), custom_call_target="tpu_custom_call" | custom-call | tf_op jit(solution)/shard_map/settle/pallas_call | solution.py:51
  63.1 6.9 %collective-permute-done.5.refs_1_ = bf16[128,1024]{1,0:T(8,128)(2,1)S(1)} collective-permute-done((bf16[128,1024]{1,0:T(8,128)(2,1)S(1)}, bf16[128,1024]{1,0:T(8,128)(2,1)S(1)}, u32[]{:S(2)}, u32[]{:S(2)}) %collective-permute-start.5) | collective-permute-done | bytes 262176 | tf_op jit(solution)/shard_map/ppermute | solution.py:997
  70.1 2.5 %project.5.refs_2_ = f32[128,4096]{1,0:T(8,128)S(1)} custom-call(bf16[128,1024]{1,0:T(8,128)(2,1)S(1)} %get-tuple-element.45.refs_0_, bf16[128,1024]{1,0:T(8,128)(2,1)S(1)} %collective-permute-done.5.refs_1_, bf16[3072,4096]{1,0:T(8,128)(2,1)S(1)} %get-tuple-element.46.refs_2_.refs_1_, f32[128,4096]{1,0:T(8,128)S(1)} %project.4.refs_4_.refs_3_, ...), custom_call_target="tpu_custom_call" | custom-call | tf_op jit(solution)/shard_map/project/pallas_call | solution.py:51
  72.5 0.6 collective-permute-done.4.refs_0_
  73.2 0.8 project.7
  74.0 0.1 collective-permute-start.8
  74.0 0.8 project.6
  74.8 0.6 collective-permute-start.6
  75.4 0.2 collective-permute-done.8.refs_1_
  75.6 1.5 %collective-permute-start.9 = (bf16[32,2048]{1,0:T(8,128)(2,1)S(1)}, bf16[32,2048]{1,0:T(8,128)(2,1)S(1)}, u32[]{:S(2)}, u32[]{:S(2)}) collective-permute-start(bf16[32,2048]{1,0:T(8,128)(2,1)S(1)} %get-tuple-element.56), channel_id=1, source_target_pairs={{0,2},{1,3},{2,0},{3,1},{4,6},{5,7},{6,4},{7,5},{8,10},{9,11},{10,... | collective-permute-start | bytes 393224 | tf_op jit(solution)/shard_map/ppermute | solution.py:916
  77.2 0.0 collective-permute-done.6.refs_1_
  77.2 1.0 %collective-permute-start.7 = (bf16[32,2048]{1,0:T(8,128)(2,1)S(1)}, bf16[32,2048]{1,0:T(8,128)(2,1)S(1)}, u32[]{:S(2)}, u32[]{:S(2)}) collective-permute-start(bf16[32,2048]{1,0:T(8,128)(2,1)S(1)} %get-tuple-element.52), channel_id=1, source_target_pairs={{0,2},{1,3},{2,0},{3,1},{4,6},{5,7},{6,4},{7,5},{8,10},{9,11},{10,... | collective-permute-start | bytes 393224 | tf_op jit(solution)/shard_map/ppermute | solution.py:916
  78.2 1.4 %slot_rows.1 = s32[2,64]{1,0:T(2,128)} custom-call(s32[8,128]{1,0:T(8,128)S(1)} %get-tuple-element.35.refs_0_, bf16[128,2176]{1,0:T(8,128)(2,1)S(1)} %tie.4.refs_1_.refs_0_, bf16[128,2176]{1,0:T(8,128)(2,1)S(1)} %collective-permute-done.2.refs_1_.refs_2_, f32[32,2048]{1,0:T(8,128)S(1)} %get-tuple-element.55.refs_2_.refs_3_), custom_call_target="tpu_custom_call" | custom-call | tf_op jit(solution)/shard_map/slot_rows/pallas_call | solution.py:51
  79.5 2.5 %collective-permute-done.9.refs_3_ = bf16[32,2048]{1,0:T(8,128)(2,1)S(1)} collective-permute-done((bf16[32,2048]{1,0:T(8,128)(2,1)S(1)}, bf16[32,2048]{1,0:T(8,128)(2,1)S(1)}, u32[]{:S(2)}, u32[]{:S(2)}) %collective-permute-start.9) | collective-permute-done | bytes 131104 | tf_op jit(solution)/shard_map/ppermute | solution.py:916
  82.0 2.0 %collective-permute-done.7.refs_1_ = bf16[32,2048]{1,0:T(8,128)(2,1)S(1)} collective-permute-done((bf16[32,2048]{1,0:T(8,128)(2,1)S(1)}, bf16[32,2048]{1,0:T(8,128)(2,1)S(1)}, u32[]{:S(2)}, u32[]{:S(2)}) %collective-permute-start.7) | collective-permute-done | bytes 131104 | tf_op jit(solution)/shard_map/ppermute | solution.py:916
  84.0 0.8 finish.1
  84.8 3.4 %collective-permute-done.10.refs_0_ = bf16[2,2,16,4096]{3,2,1,0:T(8,128)(2,1)S(1)} collective-permute-done((bf16[2,2,16,4096]{3,2,1,0:T(8,128)(2,1)S(1)}, bf16[2,2,16,4096]{3,2,1,0:T(8,128)(2,1)S(1)}, u32[]{:S(2)}, u32[]{:S(2)}) %collective-permute-start.10) | collective-permute-done | bytes 524320 | tf_op jit(solution)/shard_map/ppermute | solution.py:998
  88.2 0.0 collective-permute-done.11.refs_1_
  88.2 1.6 %settle.3 = (bf16[2,64,4096]{2,1,0:T(8,128)(2,1)}, bf16[2,64,4096]{2,1,0:T(8,128)(2,1)}, f32[8,128]{1,0:T(8,128)}) custom-call(bf16[2,2,16,4096]{3,2,1,0:T(8,128)(2,1)S(1)} %collective-permute-done.10.refs_0_, bf16[2,2,16,4096]{3,2,1,0:T(8,128)(2,1)S(1)} %collective-permute-done.11.refs_1_, ...), custom_call_target="tpu_custom_call", output_to_operand_aliasing={{0}: (2, {}), {1}: (3, {})} | custom-call | tf_op jit(solution)/shard_map/settle/pallas_call | solution.py:51
  (6 shorter events, 0.1 us)
Async XLA Ops:
  2.3 15.5 %collective-permute-start = (bf16[67,32,128]{2,1,0:T(8,128)(2,1)S(1)}, bf16[67,32,128]{2,1,0:T(8,128)(2,1)S(1)}, u32[]{:S(2)}, u32[]{:S(2)}) collective-permute-start(bf16[67,32,128]{2,1,0:T(8,128)(2,1)S(1)} %get-tuple-element.37), channel_id=1, source_target_pairs={{0,4},{4,0},{8,12},{12,8},{1,5},{5,1},{9,13},{13,9},{2,6},{6,2},{1... | collective-permute-start | bytes 1646600 | tf_op jit(solution)/shard_map/ppermute | solution.py:976
  5.4 15.8 %collective-permute-start.1 = (bf16[2,2,16,4096]{3,2,1,0:T(8,128)(2,1)S(1)}, bf16[2,2,16,4096]{3,2,1,0:T(8,128)(2,1)S(1)}, u32[]{:S(2)}, u32[]{:S(2)}) collective-permute-start(bf16[2,2,16,4096]{3,2,1,0:T(8,128)(2,1)S(1)} %get-tuple-element.34.refs_7_.refs_0_), channel_id=1, source_target_pairs={{4,8},{8,4},{5,9},{9,5},{6,10},{10,6},{7,11},{11,7},{20,24},{24,20... | collective-permute-start | bytes 1572872 | tf_op jit(solution)/shard_map/ppermute | solution.py:977
  21.2 29.1 %collective-permute-start.2 = (bf16[128,2176]{1,0:T(8,128)(2,1)S(1)}, bf16[128,2176]{1,0:T(8,128)(2,1)S(1)}, u32[]{:S(2)}, u32[]{:S(2)}) collective-permute-start(bf16[128,2176]{1,0:T(8,128)(2,1)S(1)} %tie.4.refs_1_.refs_0_), channel_id=1, source_target_pairs={{0,8},{4,12},{8,0},{12,4},{1,9},{5,13},{9,1},{13,5},{2,10},{6,14},... | collective-permute-start | bytes 1671176 | tf_op jit(solution)/shard_map/ppermute | solution.py:991
  32.4 18.0 %collective-permute-start.3 = (bf16[2,16,4096]{2,1,0:T(8,128)(2,1)S(1)}, bf16[2,16,4096]{2,1,0:T(8,128)(2,1)S(1)}, u32[]{:S(2)}, u32[]{:S(2)}) collective-permute-start(bf16[2,16,4096]{2,1,0:T(8,128)(2,1)S(1)} %tie.5), channel_id=1, source_target_pairs={{0,4},{4,0},{8,12},{12,8},{1,5},{5,1},{9,13},{13,9},{2,6},{6,2},{1... | collective-permute-start | bytes 786440 | tf_op jit(solution)/shard_map/ppermute | solution.py:994
  51.1 19.0 %collective-permute-start.5 = (bf16[128,1024]{1,0:T(8,128)(2,1)S(1)}, bf16[128,1024]{1,0:T(8,128)(2,1)S(1)}, u32[]{:S(2)}, u32[]{:S(2)}) collective-permute-start(bf16[128,1024]{1,0:T(8,128)(2,1)S(1)} %get-tuple-element.47.refs_0_.refs_1_), channel_id=1, source_target_pairs={{0,4},{4,0},{8,12},{12,8},{1,5},{5,1},{9,13},{13,9},{2,6},{6,2},{1... | collective-permute-start | bytes 786440 | tf_op jit(solution)/shard_map/ppermute | solution.py:997
  51.2 22.0 %collective-permute-start.4 = (bf16[128,1024]{1,0:T(8,128)(2,1)S(1)}, bf16[128,1024]{1,0:T(8,128)(2,1)S(1)}, u32[]{:S(2)}, u32[]{:S(2)}) collective-permute-start(bf16[128,1024]{1,0:T(8,128)(2,1)S(1)} %get-tuple-element.45.refs_0_), channel_id=1, source_target_pairs={{0,4},{4,0},{8,12},{12,8},{1,5},{5,1},{9,13},{13,9},{2,6},{6,2},{1... | collective-permute-start | bytes 786440 | tf_op jit(solution)/shard_map/ppermute | solution.py:997
  53.2 35.0 %collective-permute-start.10 = (bf16[2,2,16,4096]{3,2,1,0:T(8,128)(2,1)S(1)}, bf16[2,2,16,4096]{3,2,1,0:T(8,128)(2,1)S(1)}, u32[]{:S(2)}, u32[]{:S(2)}) collective-permute-start(bf16[2,2,16,4096]{3,2,1,0:T(8,128)(2,1)S(1)} %tie.6), channel_id=1, source_target_pairs={{0,8},{4,12},{8,0},{12,4},{1,9},{5,13},{9,1},{13,5},{2,10},{6,14},... | collective-permute-start | bytes 1572872 | tf_op jit(solution)/shard_map/ppermute | solution.py:998
  54.0 34.2 %collective-permute-start.11 = (bf16[2,2,16,4096]{3,2,1,0:T(8,128)(2,1)S(1)}, bf16[2,2,16,4096]{3,2,1,0:T(8,128)(2,1)S(1)}, u32[]{:S(2)}, u32[]{:S(2)}) collective-permute-start(bf16[2,2,16,4096]{3,2,1,0:T(8,128)(2,1)S(1)} %tie.7), channel_id=1, source_target_pairs={{0,12},{12,0},{1,13},{13,1},{2,14},{14,2},{3,15},{15,3},{16,28},{2... | collective-permute-start | bytes 1572872 | tf_op jit(solution)/shard_map/ppermute | solution.py:999
  74.0 1.6 %collective-permute-start.8 = (bf16[2,32,2048]{2,1,0:T(8,128)(2,1)S(1)}, bf16[2,32,2048]{2,1,0:T(8,128)(2,1)S(1)}, u32[]{:S(2)}, u32[]{:S(2)}) collective-permute-start(bf16[2,32,2048]{2,1,0:T(8,128)(2,1)S(1)} %get-tuple-element.54), channel_id=1, source_target_pairs={{0,1},{1,0},{2,3},{3,2},{4,5},{5,4},{6,7},{7,6},{8,9},{9,8},{10,11... | collective-permute-start | bytes 786440 | tf_op jit(solution)/shard_map/ppermute | solution.py:903
  74.8 2.3 %collective-permute-start.6 = (bf16[2,32,2048]{2,1,0:T(8,128)(2,1)S(1)}, bf16[2,32,2048]{2,1,0:T(8,128)(2,1)S(1)}, u32[]{:S(2)}, u32[]{:S(2)}) collective-permute-start(bf16[2,32,2048]{2,1,0:T(8,128)(2,1)S(1)} %get-tuple-element.50), channel_id=1, source_target_pairs={{0,1},{1,0},{2,3},{3,2},{4,5},{5,4},{6,7},{7,6},{8,9},{9,8},{10,11... | collective-permute-start | bytes 786440 | tf_op jit(solution)/shard_map/ppermute | solution.py:903
  75.6 6.4 %collective-permute-start.9 = (bf16[32,2048]{1,0:T(8,128)(2,1)S(1)}, bf16[32,2048]{1,0:T(8,128)(2,1)S(1)}, u32[]{:S(2)}, u32[]{:S(2)}) collective-permute-start(bf16[32,2048]{1,0:T(8,128)(2,1)S(1)} %get-tuple-element.56), channel_id=1, source_target_pairs={{0,2},{1,3},{2,0},{3,1},{4,6},{5,7},{6,4},{7,5},{8,10},{9,11},{10,... | collective-permute-start | bytes 393224 | tf_op jit(solution)/shard_map/ppermute | solution.py:916
  77.2 6.8 %collective-permute-start.7 = (bf16[32,2048]{1,0:T(8,128)(2,1)S(1)}, bf16[32,2048]{1,0:T(8,128)(2,1)S(1)}, u32[]{:S(2)}, u32[]{:S(2)}) collective-permute-start(bf16[32,2048]{1,0:T(8,128)(2,1)S(1)} %get-tuple-element.52), channel_id=1, source_target_pairs={{0,2},{1,3},{2,0},{3,1},{4,6},{5,7},{6,4},{7,5},{8,10},{9,11},{10,... | collective-permute-start | bytes 393224 | tf_op jit(solution)/shard_map/ppermute | solution.py:916

commit v3 on v2

--- a/solution.py
+++ b/solution.py
@@ -42,7 +42,7 @@
     return pl.BlockSpec(memory_space=pl.ANY)
 
 
-def call(kernel, operands, in_specs, follows=(), **rest):
+def call(kernel, operands, in_specs, follows=(), flops=0, **rest):
     count, extra = len(operands), len(follows)
 
     def without_extra(*refs):
@@ -51,7 +51,7 @@
     return pl.pallas_call(
         without_extra,
         in_specs=list(in_specs) + [anywhere()] * extra,
-        cost_estimate=pl.CostEstimate(flops=0, bytes_accessed=0, transcendentals=0),
+        cost_estimate=pl.CostEstimate(flops=flops, bytes_accessed=0, transcendentals=0),
         **rest,
     )(*operands, *follows)
 
@@ -170,32 +170,31 @@
     )
 
 
-def place_near_kernel(tp_size, head_count, tokens_ref, out_ref):
+def place_near_kernel(tp_size, head_count, keys_ref, values_ref, out_ref):
     cap, width = out_ref.shape[1:]
-    held, page_len = (tokens_ref.shape[0] - 1) // 2, tokens_ref.shape[1]
-    pages = held - 1
+    pages, page_len = values_ref.shape[0] - 1, values_ref.shape[1]
     me = lax.axis_index("tp")
     head = lax.rem(me, head_count)
-    lists = tokens_ref[2 * held].astype(jnp.float32)[:, :pages].astype(jnp.int32)
+    lists = keys_ref[pages + 1].astype(jnp.float32)[:, :pages].astype(jnp.int32)
     owner = lists[0:1]
     for which in range(1, head_count):
         owner = jnp.where(head == which, lists[which : which + 1], owner)
     rank = rank_pages(owner, earlier_pages(pages), round_up(tp_size, 8))
     row = lax.broadcasted_iota(jnp.int32, (cap, pages), 0)
     pick = ((owner == me) & (rank == row)).astype(jnp.bfloat16)
-    for index in range(2):
-        paged = tokens_ref[index * held : index * held + pages].reshape(pages, page_len * HD)
+    for index, source in enumerate((keys_ref, values_ref)):
+        paged = source[:pages].reshape(pages, page_len * HD)
         out_ref[index] = jnp.dot(pick, paged, preferred_element_type=jnp.float32).astype(
             jnp.bfloat16
         )
 
 
-def place_near(tokens, head_count, cap, tp_size):
-    pages, page_len = (tokens.shape[0] - 1) // 2 - 1, tokens.shape[1]
+def place_near(keys, values, head_count, cap, tp_size):
+    page_len = keys.shape[1]
     return call(
         functools.partial(place_near_kernel, tp_size, head_count),
-        (tokens,),
-        [vmem()],
+        (keys, values),
+        [vmem()] * 2,
         out_specs=vmem(),
         out_shape=jax.ShapeDtypeStruct((2, cap, page_len * HD), jnp.bfloat16),
         compiler_params=params(8),
@@ -346,13 +345,13 @@
     key_ref, value_ref, fresh_key_ref, fresh_value_ref, owner_ref = refs[:5]
     arrived = refs[-1]
     if with_queries:
-        all_query_ref, count_ref, out_ref, query_ref, bounds_ref = refs[5:10]
-        held, fresh, owners, queries, counts = refs[10:15]
+        all_query_ref, count_ref, *outs, query_ref, bounds_ref = refs[5:11]
+        held, fresh, owners, queries, counts = refs[11:16]
     elif handing:
-        out_ref, hand_ref, held, fresh, owners = refs[5:10]
+        *outs, hand_ref, held, fresh, owners = refs[5:11]
     else:
-        out_ref, held, fresh, owners = refs[5:9]
-    pages, page_len = key_ref.shape[1], out_ref.shape[1]
+        *outs, held, fresh, owners = refs[5:10]
+    pages, page_len = key_ref.shape[1], outs[0].shape[1]
     head_count, own_rows, steps = key_ref.shape[0], fresh.shape[1], fresh.shape[2]
     me = lax.axis_index("tp")
     head = lax.rem(me + other, head_count)
@@ -376,7 +375,7 @@
     for copy in copies:
         copy.start()
     copies[0].wait()
-    out_ref[2 * pages + 2] = owner_page(owners[...], page_len).astype(jnp.bfloat16)
+    outs[0][pages + 1] = owner_page(owners[...], page_len).astype(jnp.bfloat16)
     if handing:
         cap = hand_ref.shape[2]
         picks = slot_picks(owners, me, [handing], cap, lax.axis_size("tp"))
@@ -390,12 +389,11 @@
         if own_rows * steps < page_len:
             spare = jnp.zeros((page_len - own_rows * steps, HD), jnp.bfloat16)
             lines = jnp.concatenate([lines, spare])
-        out_ref[pages + i * (pages + 1)] = lines
+        outs[i][pages] = lines
     for i in range(2):
         copies[3 + i].wait()
-        first = i * (pages + 1)
         paged = held[i, head] if handing else held[i, 0]
-        out_ref[first : first + pages] = paged.reshape(pages, page_len, HD)
+        outs[i][:pages] = paged.reshape(pages, page_len, HD)
     if handing:
         for i in range(2):
             for which in range(head_count):
@@ -430,7 +428,9 @@
     page_len = width // HD
     with_queries = queries is not None
     operands = [*caches, *fresh, owner]
-    out_shape = [jax.ShapeDtypeStruct((2 * pages + 3, page_len, HD), jnp.bfloat16)]
+    out_shape = [
+        jax.ShapeDtypeStruct((pages + extra, page_len, HD), jnp.bfloat16) for extra in (2, 1)
+    ]
     scratch = [
         pltpu.VMEM((2, head_count if handing else 1, pages, width), jnp.bfloat16),
         pltpu.VMEM((2,) + fresh[0].shape, jnp.bfloat16),
@@ -478,171 +478,259 @@
     return member, jnp.transpose(member)
 
 
-def attend_kernel(steps, own_lines, neighbour, has_earlier, last, *refs):
-    bounds_ref, query_ref, tokens_ref = refs[:3]
-    refs = refs[3:]
+def prepare_kernel(steps, own_lines, page_len, neighbours, bounds_ref, query_ref, *refs):
+    row_lines = query_ref.shape[0]
+    for place, neighbour in enumerate(neighbours):
+        chosen_ref, member_ref, turned_ref = refs[3 * place : 3 * place + 3]
+        member_lines = member_ref.shape[0]
+        pages = (member_lines - round_up(page_len, LANES)) // steps
+        member, turned = membership(
+            bounds_ref[...],
+            lax.axis_index("tp") ^ neighbour,
+            pages,
+            own_lines,
+            member_lines,
+            row_lines,
+            steps,
+        )
+        chosen_ref[...] = jnp.dot(
+            member.astype(jnp.bfloat16), query_ref[...], preferred_element_type=jnp.float32
+        ).astype(jnp.bfloat16)
+        member_ref[...] = member
+        turned_ref[...] = turned
+
+
+def prepare(bounds, query, neighbours, pages, page_len, own_lines, steps):
+    row_lines, query_width = query.shape
+    member_lines = pages * steps + round_up(page_len, LANES)
+    shapes = (
+        jax.ShapeDtypeStruct((member_lines, query_width), jnp.bfloat16),
+        jax.ShapeDtypeStruct((member_lines, row_lines), jnp.float32),
+        jax.ShapeDtypeStruct((row_lines, member_lines), jnp.float32),
+    )
+    out = call(
+        functools.partial(prepare_kernel, steps, own_lines, page_len, neighbours),
+        (bounds, query),
+        [vmem()] * 2,
+        out_specs=[vmem()] * (3 * len(neighbours)),
+        out_shape=shapes * len(neighbours),
+        compiler_params=params(8),
+        name="prepare",
+    )
+    return [out[3 * place : 3 * place + 3] for place in range(len(neighbours))]
+
+
+def page_batch(pages, page_len):
+    return min(pages, max(1, LANES // page_len))
+
+
+def score_kernel(steps, has_earlier, chosen, member_ref, turned_ref, keys_ref, *refs):
     if has_earlier:
-        early_max_ref, early_total_ref, early_numer_ref = refs[:3]
-        refs = refs[3:]
-    if last:
-        if has_earlier:
-            own_tokens_ref, refs = refs[0], refs[1:]
-        payload_ref, refs = refs[0], refs[1:]
-    else:
-        out_max_ref, out_total_ref, out_numer_ref = refs[:3]
-        refs = refs[3:]
-    chosen, numers, high, low = refs
-
-    row_lines, query_width = query_ref.shape
+        early_max_ref, early_total_ref = refs[:2]
+        refs = refs[2:]
+    weights_ref, fresh_ref, max_ref, total_ref, scores, fresh_scores = refs
+    row_lines, query_width = turned_ref.shape[0], chosen.shape[1]
     group = query_width // HD
-    held, page_len = (tokens_ref.shape[0] - 1) // 2, tokens_ref.shape[1]
-    pages = held - 1
-    page_lines = pages * steps
-    used_lines = page_lines + page_len
-    member_lines = chosen.shape[0]
+    page_len = keys_ref.shape[1]
+    batch = weights_ref.shape[2] // page_len
+    blocks, lines = weights_ref.shape[0], batch * steps
+    pages = blocks * batch
+    spare = member_ref.shape[0] - pages * steps - page_len
     scale = HD ** (-0.5)
     lane = lax.broadcasted_iota(jnp.int32, (1, LANES), 1)
-    me = lax.axis_index("tp")
-    member, member_t = membership(
-        bounds_ref[...], me ^ neighbour, pages, own_lines, member_lines, row_lines, steps
-    )
-    is_member = member_t > 0
-    chosen[...] = jnp.dot(
-        member.astype(jnp.bfloat16), query_ref[...], preferred_element_type=jnp.float32
-    ).astype(jnp.bfloat16)
-
-    maxima, totals = [], []
-
-    def one_block(first_line, lines, keys, values, mask):
-        queries = jnp.concatenate(
-            [
-                chosen[first_line : first_line + lines, g * HD : (g + 1) * HD]
-                for g in range(group)
-            ],
-            axis=0,
-        )
-        scores = (
-            lax.dot_general(
-                queries, keys, (((1,), (1,)), ((), ())), preferred_element_type=jnp.float32
-            )
-            * scale
-        )
-        scores = jnp.where(mask, scores, NEGATIVE)
-        largest = jnp.max(scores, axis=1, keepdims=True)
-        weights = jnp.exp(scores - largest).astype(jnp.bfloat16)
-        total = jnp.sum(weights.astype(jnp.float32), axis=1, keepdims=True)
-        numer = jnp.dot(weights, values, preferred_element_type=jnp.float32)
-        block_max = jnp.zeros((lines, LANES), jnp.float32)
-        block_total = jnp.zeros((lines, LANES), jnp.float32)
-        for g in range(group):
-            part = slice(g * lines, (g + 1) * lines)
-            block_max = jnp.where(lane == g, largest[part], block_max)
-            block_total = jnp.where(lane == g, total[part], block_total)
-            numers[first_line : first_line + lines, g * HD : (g + 1) * HD] = numer[part]
-        maxima.append(block_max)
-        totals.append(block_total)
-
-    batch = min(pages, max(1, 128 // page_len))
-    lines = batch * steps
+    member, turned = member_ref[...], turned_ref[...]
+    is_member = turned > 0
+
     line = lax.broadcasted_iota(jnp.int32, (group * lines, batch * page_len), 0)
     token = lax.broadcasted_iota(jnp.int32, (group * lines, batch * page_len), 1)
-    mask = (line % lines) // steps == token // page_len
-    for first in range(0, pages, batch):
-        one_block(
-            first * steps,
-            lines,
-            tokens_ref[first : first + batch].reshape(batch * page_len, HD),
-            tokens_ref[held + first : held + first + batch].reshape(batch * page_len, HD),
-            mask,
-        )
+    page_mask = (line % lines) // steps == token // page_len
     line = lax.broadcasted_iota(jnp.int32, (group * page_len, page_len), 0) % page_len
     token = lax.broadcasted_iota(jnp.int32, (group * page_len, page_len), 1)
-    mask = (line // steps == token // steps) & (token % steps <= line % steps)
-    one_block(page_lines, page_len, tokens_ref[pages], tokens_ref[held + pages], mask)
-
-    spare = member_lines - used_lines
+    fresh_mask = (line // steps == token // steps) & (token % steps <= line % steps)
+
+    def score(first_line, count, keys, mask):
+        rows = slice(first_line, first_line + count)
+        queries = jnp.concatenate(
+            [chosen[rows, g * HD : (g + 1) * HD] for g in range(group)], axis=0
+        )
+        found = lax.dot_general(
+            queries, keys, (((1,), (1,)), ((), ())), preferred_element_type=jnp.float32
+        )
+        found = jnp.where(mask, found * scale, NEGATIVE)
+        largest = jnp.max(found, axis=1, keepdims=True)
+        block_max = jnp.zeros((count, LANES), jnp.float32)
+        for g in range(group):
+            block_max = jnp.where(lane == g, largest[g * count : (g + 1) * count], block_max)
+        return found, block_max
+
+    maxima = []
+    for block in range(blocks):
+        keys = keys_ref[block * batch : (block + 1) * batch].reshape(batch * page_len, HD)
+        scores[block], block_max = score(block * lines, lines, keys, page_mask)
+        maxima.append(block_max)
+    fresh_scores[...], block_max = score(pages * steps, page_len, keys_ref[pages], fresh_mask)
+    maxima.append(block_max)
     if spare:
         maxima.append(jnp.zeros((spare, LANES), jnp.float32))
-        totals.append(jnp.zeros((spare, LANES), jnp.float32))
-    line_max = jnp.concatenate(maxima, axis=0)
-    line_total = jnp.concatenate(totals, axis=0)
-
-    line_max_t = jnp.transpose(line_max)
+
+    line_max = jnp.transpose(jnp.concatenate(maxima, axis=0))
     row_max = jnp.full((row_lines, LANES), NEGATIVE, jnp.float32)
     for g in range(group):
         best = jnp.max(
-            jnp.where(is_member, line_max_t[g : g + 1, :], NEGATIVE), axis=1, keepdims=True
+            jnp.where(is_member, line_max[g : g + 1, :], NEGATIVE), axis=1, keepdims=True
         )
         row_max = jnp.where(lane == g, best, row_max)
+    if has_earlier:
+        row_max = jnp.maximum(row_max, early_max_ref[...])
     spread = jnp.dot(
-        member,
-        row_max,
+        member, row_max, precision=HIGHEST, preferred_element_type=jnp.float32
+    )
+
+    def weigh(first_line, count, found, mask):
+        rows = spread[first_line : first_line + count]
+        shift = jnp.concatenate([rows[:, g : g + 1] for g in range(group)], axis=0)
+        weights = jnp.where(mask, jnp.exp(jnp.minimum(found - shift, 0.0)), 0.0)
+        weights = weights.astype(jnp.bfloat16)
+        total = jnp.sum(weights.astype(jnp.float32), axis=1, keepdims=True)
+        block_total = jnp.zeros((count, LANES), jnp.float32)
+        for g in range(group):
+            block_total = jnp.where(lane == g, total[g * count : (g + 1) * count], block_total)
+        return weights, block_total
+
+    totals = []
+    for block in range(blocks):
+        weights_ref[block], total = weigh(block * lines, lines, scores[block], page_mask)
+        totals.append(total)
+    fresh_ref[...], total = weigh(pages * steps, page_len, fresh_scores[...], fresh_mask)
+    totals.append(total)
+    if spare:
+        totals.append(jnp.zeros((spare, LANES), jnp.float32))
+    row_total = jnp.dot(
+        turned,
+        jnp.concatenate(totals, axis=0),
         precision=HIGHEST,
         preferred_element_type=jnp.float32,
     )
-    factor = jnp.exp(jnp.minimum(line_max - spread, 0.0))
-    row_total = jnp.dot(
-        member_t,
-        line_total * factor,
-        precision=HIGHEST,
-        preferred_element_type=jnp.float32,
-    )
-    turned = member_t.astype(jnp.bfloat16)
-    if spare:
-        high[used_lines:, :] = jnp.zeros((spare, query_width), jnp.bfloat16)
-        low[used_lines:, :] = jnp.zeros((spare, query_width), jnp.bfloat16)
+    if has_earlier:
+        row_total = row_total + early_total_ref[...] * jnp.exp(early_max_ref[...] - row_max)
+    max_ref[...] = row_max
+    total_ref[...] = row_total
+
+
+def score(choice, keys, steps, earlier=(), flops=0):
+    (member_lines, query_width), row_lines = choice[0].shape, choice[2].shape[0]
+    group = query_width // HD
+    page_len = keys.shape[1]
+    pages = (member_lines - round_up(page_len, LANES)) // steps
+    batch = page_batch(pages, page_len)
+    blocks = pages // batch
+    shapes = ((blocks, group * batch * steps, batch * page_len), (group * page_len, page_len))
+    stat = jax.ShapeDtypeStruct((row_lines, LANES), jnp.float32)
+    operands = (*choice, keys, *earlier)
+    return call(
+        functools.partial(score_kernel, steps, bool(earlier)),
+        operands,
+        [vmem()] * len(operands),
+        flops=flops,
+        out_specs=[vmem()] * 4,
+        out_shape=[jax.ShapeDtypeStruct(shape, jnp.bfloat16) for shape in shapes] + [stat, stat],
+        scratch_shapes=[pltpu.VMEM(shape, jnp.float32) for shape in shapes],
+        compiler_params=params(12),
+        name="score",
+    )
+
+
+def value_kernel(steps, chunk, chunks, has_earlier, has_notes, last, *refs):
+    weights_ref, fresh_ref, turned_ref, values_ref, max_ref, total_ref = refs[:6]
+    refs = refs[6:]
+    if has_earlier:
+        early_max_ref, early_numer_ref = refs[:2]
+        refs = refs[2:]
+    if has_notes:
+        own_keys_ref, near_keys_ref = refs[:2]
+        refs = refs[2:]
+    out_ref, high, low = refs
+    row_lines, member_lines = turned_ref.shape
+    page_len = values_ref.shape[1]
+    blocks, batch = weights_ref.shape[0], weights_ref.shape[2] // page_len
+    lines, pages = batch * steps, blocks * batch
+    all_groups = weights_ref.shape[1] // lines
+    group = all_groups // chunks
+    first = chunk * group
+    used = pages * steps + page_len
+
+    def gain(first_line, count, weights, values):
+        numer = jnp.dot(weights, values, preferred_element_type=jnp.float32)
+        rounded = numer.astype(jnp.bfloat16)
+        rest = (numer - rounded.astype(jnp.float32)).astype(jnp.bfloat16)
+        for g in range(group):
+            part = slice(g * count, (g + 1) * count)
+            columns = slice(g * HD, (g + 1) * HD)
+            high[first_line : first_line + count, columns] = rounded[part]
+            low[first_line : first_line + count, columns] = rest[part]
+
+    for block in range(blocks):
+        weights = weights_ref[block, first * lines : (first + group) * lines]
+        values = values_ref[block * batch : (block + 1) * batch].reshape(batch * page_len, HD)
+        gain(block * lines, lines, weights, values)
+    weights = fresh_ref[first * page_len : (first + group) * page_len]
+    gain(pages * steps, page_len, weights, values_ref[pages])
+    if member_lines > used:
+        high[used:, :] = jnp.zeros((member_lines - used, group * HD), jnp.bfloat16)
+        low[used:, :] = jnp.zeros((member_lines - used, group * HD), jnp.bfloat16)
+
+    lane = lax.broadcasted_iota(jnp.int32, (1, LANES), 1)
+    row_max, row_total = max_ref[...], total_ref[...]
+    present = row_total > 0
+    inverse = jnp.where(present, 1.0 / jnp.where(present, row_total, 1.0), 0.0)
+    if has_earlier:
+        scale_early = jnp.exp(early_max_ref[...] - row_max)
+    if last and chunk == 0:
+        log_sum = jnp.where(
+            present & (lane < all_groups),
+            row_max + jnp.log(jnp.where(present, row_total, 1.0)),
+            jnp.where(lane < all_groups, NEGATIVE, 0.0),
+        )
+        lanes = split_sums(log_sum, all_groups)
+        if has_notes:
+            lanes = lanes + owner_notes(
+                own_keys_ref[pages + 1], near_keys_ref[pages + 1], row_lines, 3 * all_groups
+            )
+        out_ref[:, group * HD :] = lanes.astype(jnp.bfloat16)
+    turned = turned_ref[...].astype(jnp.bfloat16)
     for g in range(group):
         columns = slice(g * HD, (g + 1) * HD)
-        scaled = numers[:, columns] * factor[:used_lines, g : g + 1]
-        rounded = scaled.astype(jnp.bfloat16)
-        high[:used_lines, columns] = rounded
-        low[:used_lines, columns] = (scaled - rounded.astype(jnp.float32)).astype(jnp.bfloat16)
-
-    if has_earlier:
-        early_max = early_max_ref[...]
-        largest = jnp.maximum(row_max, early_max)
-        scale_now = jnp.exp(row_max - largest)
-        scale_early = jnp.exp(early_max - largest)
-        row_total = row_total * scale_now + early_total_ref[...] * scale_early
-        row_max = largest
-    if last:
-        present = row_total > 0
-        inverse = jnp.where(present, 1.0 / jnp.where(present, row_total, 1.0), 0.0)
-        log_sum = jnp.where(
-            present & (lane < group),
-            row_max + jnp.log(jnp.where(present, row_total, 1.0)),
-            jnp.where(lane < group, NEGATIVE, 0.0),
+        which = slice(first + g, first + g + 1)
+        numer = jnp.dot(turned, high[:, columns], preferred_element_type=jnp.float32) + jnp.dot(
+            turned, low[:, columns], preferred_element_type=jnp.float32
         )
         if has_earlier:
-            scale_now = scale_now * inverse
-            scale_early = scale_early * inverse
-        else:
-            scale_now = inverse
-        lanes = split_sums(log_sum, group)
-        if has_earlier:
-            lanes = lanes + owner_notes(
-                own_tokens_ref[2 * held], tokens_ref[2 * held], row_lines, 3 * group
-            )
-        payload_ref[:, query_width:] = lanes.astype(jnp.bfloat16)
-    for g in range(group):
-        columns = slice(g * HD, (g + 1) * HD)
-        numer = jnp.dot(
-            turned, high[:, columns], preferred_element_type=jnp.float32
-        ) + jnp.dot(turned, low[:, columns], preferred_element_type=jnp.float32)
-        if has_earlier:
-            numer = (
-                numer * scale_now[:, g : g + 1]
-                + early_numer_ref[:, columns] * scale_early[:, g : g + 1]
-            )
-        elif last:
-            numer = numer * scale_now[:, g : g + 1]
+            early = early_numer_ref[:, (first + g) * HD : (first + g + 1) * HD]
+            numer = numer + early * scale_early[:, which]
         if last:
-            payload_ref[:, columns] = numer.astype(jnp.bfloat16)
-        else:
-            out_numer_ref[:, columns] = numer
-    if not last:
-        out_max_ref[...] = row_max
-        out_total_ref[...] = row_total
+            numer = numer * inverse[:, which]
+        out_ref[:, columns] = numer.astype(out_ref.dtype)
+
+
+def value(scored, turned, values, steps, chunk, chunks, last, earlier=(), notes=(), follows=()):
+    row_lines, member_lines = turned.shape
+    page_len = values.shape[1]
+    group = scored[1].shape[0] // page_len // chunks
+    wide = group * HD + (LANES if last and chunk == 0 else 0)
+    operands = (*scored[:2], turned, values, *scored[2:], *earlier, *notes)
+    return call(
+        functools.partial(value_kernel, steps, chunk, chunks, bool(earlier), bool(notes), last),
+        operands,
+        [vmem()] * len(operands),
+        follows,
+        out_specs=vmem(),
+        out_shape=jax.ShapeDtypeStruct(
+            (row_lines, wide), jnp.bfloat16 if last else jnp.float32
+        ),
+        scratch_shapes=[pltpu.VMEM((member_lines, group * HD), jnp.bfloat16)] * 2,
+        compiler_params=params(8),
+        name="value",
+    )
 
 
 def split_sums(value, group):
@@ -674,70 +762,35 @@
     )
 
 
-def attend(
-    bounds, query, tokens, neighbour, own_lines, steps, earlier, own_tokens, last, follows=()
-):
-    row_lines, query_width = query.shape
-    group = query_width // HD
-    held, page_len = (tokens.shape[0] - 1) // 2, tokens.shape[1]
-    used_lines = (held - 1) * steps + page_len
-    member_lines = round_up(used_lines, LANES)
-    stat = jax.ShapeDtypeStruct((row_lines, LANES), jnp.float32)
-    if last:
-        out_shape = (jax.ShapeDtypeStruct((row_lines, query_width + LANES), jnp.bfloat16),)
-    else:
-        out_shape = (stat, stat, jax.ShapeDtypeStruct((row_lines, query_width), jnp.float32))
-    operands = (bounds, query, tokens, *earlier, *own_tokens)
-    return call(
-        functools.partial(
-            attend_kernel, steps, own_lines, neighbour, bool(earlier), last
-        ),
-        operands,
-        [vmem()] * len(operands),
-        follows,
-        out_specs=tuple(vmem() for _ in out_shape),
-        out_shape=out_shape,
-        scratch_shapes=[
-            pltpu.VMEM((member_lines, query_width), jnp.bfloat16),
-            pltpu.VMEM((used_lines, query_width), jnp.float32),
-            pltpu.VMEM((member_lines, query_width), jnp.bfloat16),
-            pltpu.VMEM((member_lines, query_width), jnp.bfloat16),
-        ],
-        compiler_params=params(12),
-        name="attend",
-    )
-
-
-def combine_kernel(group, mine_ref, theirs_ref, *out_refs):
-    sums = join_sums(mine_ref[:, -LANES:], group)
-    their_sums = join_sums(theirs_ref[:, -LANES:], group)
+def combine_kernel(group, first, sums_ref, their_sums_ref, mine_ref, theirs_ref, out_ref):
+    sums = join_sums(sums_ref[:, -LANES:], group)
+    their_sums = join_sums(their_sums_ref[:, -LANES:], group)
     largest = jnp.maximum(sums, their_sums)
     weight = jnp.exp(sums - largest)
     their_weight = jnp.exp(their_sums - largest)
     inverse = 1.0 / (weight + their_weight)
     weight = weight * inverse
     their_weight = their_weight * inverse
-    part = group // len(out_refs)
-    for g in range(group):
-        columns = slice(g * HD, (g + 1) * HD)
-        place = g % part
-        out_refs[g // part][:, place * HD : (place + 1) * HD] = (
+    for place in range(out_ref.shape[1] // HD):
+        g = first + place
+        columns = slice(place * HD, (place + 1) * HD)
+        out_ref[:, columns] = (
             mine_ref[:, columns].astype(jnp.float32) * weight[:, g : g + 1]
             + theirs_ref[:, columns].astype(jnp.float32) * their_weight[:, g : g + 1]
         ).astype(jnp.bfloat16)
 
 
-def combine(mine, theirs, chunks, follows=()):
-    row_lines, width = mine.shape
-    group = (width - LANES) // HD
-    shape = jax.ShapeDtypeStruct((row_lines, group // chunks * HD), jnp.bfloat16)
+def combine(mine, theirs, chunk, follows=()):
+    row_lines, width = mine[0].shape
+    width -= LANES
+    group = width // HD * len(mine)
     return call(
-        functools.partial(combine_kernel, group),
-        (mine, theirs),
-        [vmem()] * 2,
+        functools.partial(combine_kernel, group, chunk * width // HD),
+        (mine[0], theirs[0], mine[chunk], theirs[chunk]),
+        [vmem()] * 4,
         follows,
-        out_specs=[vmem()] * chunks,
-        out_shape=[shape] * chunks,
+        out_specs=vmem(),
+        out_shape=jax.ShapeDtypeStruct((row_lines, width), jnp.bfloat16),
         compiler_params=params(4),
         name="combine",
     )
@@ -972,34 +1025,52 @@
     everything = (0, out_width)
 
     if paired:
-        tokens, send_last = gather_tokens(1, caches, fresh, page_owner, handing=3, cap=cap)
-        near_tokens = lax.ppermute(tokens, "tp", flip(tp_size, 1))
+        keys, values, send_last = gather_tokens(1, caches, fresh, page_owner, handing=3, cap=cap)
+        near_keys = lax.ppermute(keys, "tp", flip(tp_size, 1))
         got_inner = lax.ppermute(send_last, "tp", [(1, 2), (2, 1)])
-        own_tokens, query, bounds = gather_tokens(
+        own_keys, own_values, query, bounds = gather_tokens(
             0, caches, fresh, page_owner, queries, page_counts, follows=(send_last,)
         )
-        shapes = (own_lines, step_count)
-        earlier = attend(bounds, query, own_tokens, 0, *shapes, (), (), False)
+        near_values = lax.ppermute(tie(values, bounds), "tp", flip(tp_size, 1))
+        own_choice, near_choice = prepare(
+            bounds, query, (0, 1), pages_here, page_len, own_lines, step_count
+        )
+        scored = score(own_choice, own_keys, step_count)
+        early_numer = value(scored, own_choice[2], own_values, step_count, 0, 1, False)
+        early_max, early_total = scored[2:]
+        scored = score(near_choice, near_keys, step_count, (early_max, early_total), 1 << 34)
+        payload = [
+            value(
+                scored,
+                near_choice[2],
+                near_values,
+                step_count,
+                chunk,
+                chunks,
+                True,
+                (early_max, early_numer),
+                () if chunk else (own_keys, near_keys),
+            )
+            for chunk in range(chunks)
+        ]
         jobs = ((2, True), (1, False), (0, True))
         send_far, send_near, kept = place_pages(
-            page_owner, caches, jobs, cap, tp_size, False, (earlier[0],)
-        )
-        (payload,) = attend(
-            bounds, query, near_tokens, 1, *shapes, earlier, (own_tokens,), True, (kept,)
-        )
-        payload = tie(payload, got_inner)
-        theirs = lax.ppermute(payload, "tp", flip(tp_size, 2))
+            page_owner, caches, jobs, cap, tp_size, False, (payload[1],)
+        )
         blocks = ((True, 1), (False, 0), (False, 1))
-        held, held_done = fetch(out_weight, blocks, chunks, head_count, part, (payload,))
+        held, held_done = fetch(out_weight, blocks, chunks, head_count, part, payload[1:])
+        payload[1] = tie(payload[1], held_done)
+        theirs = [lax.ppermute(p, "tp", flip(tp_size, 2)) for p in payload]
         got_near = lax.ppermute(tie(send_near, held_done), "tp", flip(tp_size, 1))
-        near_pages = place_near(near_tokens, head_count, cap, tp_size)
-        own_parts = combine(payload, theirs, chunks, (got_near,))
-        near_parts = [lax.ppermute(p, "tp", flip(tp_size, 1)) for p in own_parts]
-        got_far = lax.ppermute(tie(send_far, own_parts[0]), "tp", flip(tp_size, 2))
-        got_outer = lax.ppermute(tie(send_last, own_parts[0]), "tp", [(0, 3), (3, 0)])
-        total = project(
-            own_parts[:1], out_weight, None, chunks, head_count, None, everything, None
-        )
+        near_pages = place_near(near_keys, near_values, head_count, cap, tp_size)
+        first_part = combine(payload, theirs, 0, (got_inner,))
+        near_first = lax.ppermute(first_part, "tp", flip(tp_size, 1))
+        total = project([first_part], out_weight, None, chunks, head_count, None, everything, None)
+        got_far = lax.ppermute(tie(send_far, total), "tp", flip(tp_size, 2))
+        got_outer = lax.ppermute(tie(send_last, total), "tp", [(0, 3), (3, 0)])
+        second_part = combine(payload, theirs, 1, (got_near, total))
+        near_second = lax.ppermute(second_part, "tp", flip(tp_size, 1))
+        own_parts, near_parts = (first_part, second_part), (near_first, near_second)
         plan = ((0, None, None), (1, None, 0), (1, None, 1), (3, (1, 2), None))
         *settled, settled_done = settle(
             [kept, near_pages, got_near, got_inner], plan, head_count, tp_size * cap, (), (total,)
@@ -1019,14 +1090,21 @@
         for first in (0, out_width // 2):
             columns = (first, out_width // 2)
             keep, send = project(
-                [near_parts[1]], held, (2,), chunks, head_count, total, columns, chunk_lines
+                [near_parts[1]],
+                held,
+                (2,),
+                chunks,
+                head_count,
+                total,
+                columns,
+                chunk_lines,
             )
             results.append(sum_heads(keep, send, kv_size))
         attention_out, finished = finish(results, step_count)
         slot_rows = slot_rows_near(
             bounds,
-            payload,
-            theirs,
+            payload[0],
+            theirs[0],
             pages_here,
             3 * group,
             page_len,
@@ -1055,7 +1133,7 @@
     for head in range(head_count):
         cut = slice(head, head + 1)
         lanes = slice(head * HD, (head + 1) * HD)
-        tokens, query, bounds = gather_tokens(
+        keys, values, query, bounds = gather_tokens(
             0,
             [cache[cut] for cache in caches],
             [new[:, :, lanes] for new in fresh],
@@ -1063,9 +1141,11 @@
             queries[:, :, head * head_width : (head + 1) * head_width],
             page_counts,
         )
-        (payload,) = attend(
-            bounds, query, tokens, 0, own_lines, step_count, (), (), True
-        )
+        (choice,) = prepare(
+            bounds, query, (0,), pages_here, page_len, own_lines, step_count
+        )
+        scored = score(choice, keys, step_count)
+        payload = value(scored, choice[2], values, step_count, 0, 1, True)
         raw = payload[:, part:].astype(jnp.float32)
         sums = raw[:, :group] + raw[:, group : 2 * group] + raw[:, 2 * group : 3 * group]
         weight = jnp.exp(sums - lax.pmax(sums, "tp"))

time: 90.2 us -> 87.2 us (0.967)
  waiting for transfers between devices: 37.6 us -> 26.2 us
  starting transfers between devices: 18 us -> 22.6 us
  Pallas kernels: 33.4 us -> 37.2 us
    ppermute x1, waiting for transfers between devices: 16.3 us -> 5.88 us  [body(): got_near = lax.ppermute(tie(send_near, held_done), 'tp', flip(tp_size, 1))]
    ppermute x6 -> x8, starting transfers between devices: 12.5 us -> 17.1 us  [the longest x1 4.53 us: body(): got_outer = lax.ppermute(tie(send_last, total), 'tp', [(0, 3), (3, 0)])]
    pallas_call x22 -> x28, Pallas kernels: 33.4 us -> 37.2 us  [call(): pl.pallas_call(without_extra, in_specs=list(in_specs) + [anywhere()] * ex...]
    ppermute x6 -> x8, waiting for transfers between devices: 16.7 us -> 15.7 us  [the longest x1 8.15 us: body(): got_far = lax.ppermute(tie(send_far, total), 'tp', flip(tp_size, 2))]
  transfers between devices with their start and end apart: 12 -> 14, of which waited for: 8 -> 8; matrix products, arithmetic and copies ran while one was open for 0% -> 0% of each run, Pallas kernels for 33% -> 39%
where the time goes in v3:
time: 87.2 us; the launch traced here: 87 us
  Pallas kernels  37.2 us (43%)
  waiting for transfers between devices  26.2 us (30%)
  starting transfers between devices  22.6 us (26%)
  between operations  0.99 us (1%)
    pallas_call x28, Pallas kernels, call(): pl.pallas_call(without_extra, in_specs=list(in_specs) + [anywhere()] * ex...  37.2 us
    ppermute x1, waiting for transfers between devices, body(): got_far = lax.ppermute(tie(send_far, total), 'tp', flip(tp_size, 2))  8.15 us
    ppermute x1, waiting for transfers between devices, body(): got_near = lax.ppermute(tie(send_near, held_done), 'tp', flip(tp_size, 1))  5.88 us
    ppermute x1, starting transfers between devices, body(): got_outer = lax.ppermute(tie(send_last, total), 'tp', [(0, 3), (3, 0)])  4.53 us
    ppermute x1, starting transfers between devices, body(): near_values = lax.ppermute(tie(values, bounds), 'tp', flip(tp_size, 1))  4.44 us
    ppermute x2, waiting for transfers between devices, sum_heads(): lax.ppermute(part, 'kv', flip(kv_size, 2 * step))  4.43 us
    ppermute x1, waiting for transfers between devices, body(): near_second = lax.ppermute(second_part, 'tp', flip(tp_size, 1))  4 us
    ppermute x1, starting transfers between devices, body(): near_keys = lax.ppermute(keys, 'tp', flip(tp_size, 1))  3.09 us
  transfers between devices with their start and end apart: 14, of which 8 were waited for; matrix products, arithmetic and copies ran while one was open for 0% of the time, Pallas kernels for 39%

profile of v3, /device:TPU:0, one launch (start us, length us, event | category | flops | bytes accessed | tf_op | source)
XLA Modules:
  0.0 87.0 jit_solution(14348048590896943752)
XLA Ops:
  0.6 1.7 %gather_tokens.2 = (bf16[34,32,128]{2,1,0:T(8,128)(2,1)S(1)}, bf16[33,32,128]{2,1,0:T(8,128)(2,1)S(1)}, bf16[2,2,16,4096]{3,2,1,0:T(8,128)(2,1)S(1)}) custom-call(bf16[2,32,4096]{2,1,0:T(8,128)(2,1)} %refs_1_.6, bf16[2,32,4096]{2,1,0:T(8,128)(2,1)} %refs_2_.5, bf16[8,4,256]{2,1,0:T(4,128)(2,1)} %refs_2_.4, bf16[8,4,256]{2,1,0:T(4,128)(2,1)} %refs_3_.3, ...), custom_call_target="tpu_custom_call" | custom-call | tf_op jit(solution)/shard_map/gather_tokens/pallas_call | solution.py:51
  2.3 3.1 %collective-permute-start = (bf16[34,32,128]{2,1,0:T(8,128)(2,1)S(1)}, bf16[34,32,128]{2,1,0:T(8,128)(2,1)S(1)}, u32[]{:S(2)}, u32[]{:S(2)}) collective-permute-start(bf16[34,32,128]{2,1,0:T(8,128)(2,1)S(1)} %get-tuple-element.51), channel_id=1, source_target_pairs={{0,4},{4,0},{8,12},{12,8},{1,5},{5,1},{9,13},{13,9},{2,6},{6,2},{1... | collective-permute-start | bytes 835592 | tf_op jit(solution)/shard_map/ppermute | solution.py:1029
  5.4 0.7 collective-permute-start.5
  6.1 1.4 %gather_tokens.3 = (bf16[34,32,128]{2,1,0:T(8,128)(2,1)S(1)}, bf16[33,32,128]{2,1,0:T(8,128)(2,1)S(1)}, bf16[128,2048]{1,0:T(8,128)(2,1)S(1)}, s32[8,128]{1,0:T(8,128)S(1)}) custom-call(bf16[2,32,4096]{2,1,0:T(8,128)(2,1)} %refs_1_.6, bf16[2,32,4096]{2,1,0:T(8,128)(2,1)} %refs_2_.5, bf16[8,4,256]{2,1,0:T(4,128)(2,1)} %refs_2_.4, bf16[8,4,256]{2,1,0:T(4,128)(2,1)} %refs_3_.3, ...), custom_call_target="tpu_custom_call" | custom-call | tf_op jit(solution)/shard_map/gather_tokens/pallas_call | solution.py:51
  7.5 4.4 %collective-permute-start.1 = (bf16[33,32,128]{2,1,0:T(8,128)(2,1)S(1)}, bf16[33,32,128]{2,1,0:T(8,128)(2,1)S(1)}, u32[]{:S(2)}, u32[]{:S(2)}) collective-permute-start(bf16[33,32,128]{2,1,0:T(8,128)(2,1)S(1)} %tie.5), channel_id=1, source_target_pairs={{0,4},{4,0},{8,12},{12,8},{1,5},{5,1},{9,13},{13,9},{2,6},{6,2},{1... | collective-permute-start | bytes 811016 | tf_op jit(solution)/shard_map/ppermute | solution.py:1034
  11.9 0.7 prepare.1
  12.6 3.2 %score.2 = (bf16[8,256,128]{2,1,0:T(8,128)(2,1)S(1)}, bf16[512,32]{1,0:T(8,128)(2,1)S(1)}, f32[128,128]{1,0:T(8,128)S(1)}, f32[128,128]{1,0:T(8,128)S(1)}) custom-call(bf16[256,2048]{1,0:T(8,128)(2,1)S(1)} %get-tuple-element.52.refs_0_, f32[256,128]{1,0:T(8,128)S(1)} %get-tuple-element.53.refs_1_, f32[128,256]{1,0:T(8,128)S(1)} %get-tuple-element.54.refs_2_, ...), custom_call_target="tpu_custom_call" | custom-call | tf_op jit(solution)/shard_map/score/pallas_call | solution.py:51
  15.9 1.1 %value.3.refs_7_ = f32[128,2048]{1,0:T(8,128)S(1)} custom-call(bf16[8,256,128]{2,1,0:T(8,128)(2,1)S(1)} %get-tuple-element.63.refs_0_, bf16[512,32]{1,0:T(8,128)(2,1)S(1)} %get-tuple-element.64.refs_1_, f32[128,256]{1,0:T(8,128)S(1)} %get-tuple-element.54.refs_2_, bf16[33,32,128]{2,1,0:T(8,128)(2,1)S(1)} %get-tuple-element.65.refs_3_, ...), custom_call_target="tpu_custom_call" | custom-call | tf_op jit(solution)/shard_map/value/pallas_call | solution.py:51
  17.0 0.0 collective-permute-done.refs_3_.refs_9_.refs_0_
  17.0 3.3 %score.3 = (bf16[8,256,128]{2,1,0:T(8,128)(2,1)S(1)}, bf16[512,32]{1,0:T(8,128)(2,1)S(1)}, f32[128,128]{1,0:T(8,128)S(1)}, f32[128,128]{1,0:T(8,128)S(1)}) custom-call(bf16[256,2048]{1,0:T(8,128)(2,1)S(1)} %get-tuple-element.48.refs_0_, f32[256,128]{1,0:T(8,128)S(1)} %get-tuple-element.49.refs_1_, f32[128,256]{1,0:T(8,128)S(1)} %get-tuple-element.50.refs_2_, ...), custom_call_target="tpu_custom_call" | custom-call | flops 17179869184 | tf_op jit(solution)/shard_map/score/pallas_call | solution.py:51
  20.3 0.0 collective-permute-done.1.refs_3_.refs_1_
  20.4 0.8 value.4.refs_0_.refs_2_.refs_1_
  21.1 0.3 collective-permute-start.2
  21.4 0.7 value.5.refs_1_.refs_0_.refs_3_
  22.2 1.7 %place_pages.1 = (bf16[2,2,16,4096]{3,2,1,0:T(8,128)(2,1)S(1)}, bf16[2,16,4096]{2,1,0:T(8,128)(2,1)S(1)}, bf16[2,2,16,4096]{3,2,1,0:T(8,128)(2,1)S(1)}) custom-call(s32[2,32]{1,0:T(2,128)} %refs_0_.7, bf16[2,32,4096]{2,1,0:T(8,128)(2,1)} %refs_1_.6, bf16[2,32,4096]{2,1,0:T(8,128)(2,1)} %refs_2_.5, bf16[128,1024]{1,0:T(8,128)(2,1)S(1)} %value.5.refs_1_.refs_0_.refs_3_), custom_call_target="tpu_custom_call" | custom-call | tf_op jit(solution)/shard_map/place_pages/pallas_call | solution.py:51
  23.9 8.4 %fetch.1 = (bf16[3072,4096]{1,0:T(8,128)(2,1)S(1)}, f32[8,128]{1,0:T(8,128)S(1)}) custom-call(bf16[4096,4096]{1,0:T(8,128)(2,1)} %refs_1_.7, bf16[128,1024]{1,0:T(8,128)(2,1)S(1)} %value.5.refs_1_.refs_0_.refs_3_), custom_call_target="tpu_custom_call" | custom-call | tf_op jit(solution)/shard_map/fetch/pallas_call | solution.py:51
  32.3 1.6 %collective-permute-start.4 = (bf16[2,16,4096]{2,1,0:T(8,128)(2,1)S(1)}, bf16[2,16,4096]{2,1,0:T(8,128)(2,1)S(1)}, u32[]{:S(2)}, u32[]{:S(2)}) collective-permute-start(bf16[2,16,4096]{2,1,0:T(8,128)(2,1)S(1)} %tie.7), channel_id=1, source_target_pairs={{0,4},{4,0},{8,12},{12,8},{1,5},{5,1},{9,13},{13,9},{2,6},{6,2},{1... | collective-permute-start | bytes 786440 | tf_op jit(solution)/shard_map/ppermute | solution.py:1064
  33.9 1.2 %collective-permute-start.3 = (bf16[128,1024]{1,0:T(8,128)(2,1)S(1)}, bf16[128,1024]{1,0:T(8,128)(2,1)S(1)}, u32[]{:S(2)}, u32[]{:S(2)}) collective-permute-start(bf16[128,1024]{1,0:T(8,128)(2,1)S(1)} %tie.6.refs_2_), channel_id=1, source_target_pairs={{0,8},{4,12},{8,0},{12,4},{1,9},{5,13},{9,1},{13,5},{2,10},{6,14},... | collective-permute-start | bytes 786440 | tf_op jit(solution)/shard_map/ppermute | solution.py:1063
  35.1 0.0 collective-permute-done.5.refs_4_.refs_3_
  35.1 1.1 %collective-permute-done.2.refs_1_.refs_3_.refs_2_ = bf16[128,1152]{1,0:T(8,128)(2,1)S(1)} collective-permute-done((bf16[128,1152]{1,0:T(8,128)(2,1)S(1)}, bf16[128,1152]{1,0:T(8,128)(2,1)S(1)}, u32[]{:S(2)}, u32[]{:S(2)}) %collective-permute-start.2) | collective-permute-done | bytes 294944 | tf_op jit(solution)/shard_map/ppermute | solution.py:1063
  36.2 0.5 combine.2.refs_0_
  36.7 0.9 %collective-permute-start.7 = (bf16[128,1024]{1,0:T(8,128)(2,1)S(1)}, bf16[128,1024]{1,0:T(8,128)(2,1)S(1)}, u32[]{:S(2)}, u32[]{:S(2)}) collective-permute-start(bf16[128,1024]{1,0:T(8,128)(2,1)S(1)} %combine.2.refs_0_), channel_id=1, source_target_pairs={{0,4},{4,0},{8,12},{12,8},{1,5},{5,1},{9,13},{13,9},{2,6},{6,2},{1... | collective-permute-start | bytes 786440 | tf_op jit(solution)/shard_map/ppermute | solution.py:1067
  37.6 3.9 %project.4.refs_5_.refs_4_.refs_3_.refs_1_ = f32[128,4096]{1,0:T(8,128)S(1)} custom-call(bf16[128,1024]{1,0:T(8,128)(2,1)S(1)} %combine.2.refs_0_, bf16[4096,4096]{1,0:T(8,128)(2,1)} %refs_1_.7), custom_call_target="tpu_custom_call" | custom-call | tf_op jit(solution)/shard_map/project/pallas_call | solution.py:51
  41.5 5.9 %collective-permute-done.4.refs_4_.refs_2_ = bf16[2,16,4096]{2,1,0:T(8,128)(2,1)S(1)} collective-permute-done((bf16[2,16,4096]{2,1,0:T(8,128)(2,1)S(1)}, bf16[2,16,4096]{2,1,0:T(8,128)(2,1)S(1)}, u32[]{:S(2)}, u32[]{:S(2)}) %collective-permute-start.4) | collective-permute-done | bytes 262176 | tf_op jit(solution)/shard_map/ppermute | solution.py:1064
  47.4 0.0 collective-permute-done.3.refs_3_
  47.4 0.5 combine.3.refs_0_
  47.9 2.6 %collective-permute-start.6 = (bf16[128,1024]{1,0:T(8,128)(2,1)S(1)}, bf16[128,1024]{1,0:T(8,128)(2,1)S(1)}, u32[]{:S(2)}, u32[]{:S(2)}) collective-permute-start(bf16[128,1024]{1,0:T(8,128)(2,1)S(1)} %combine.3.refs_0_), channel_id=1, source_target_pairs={{0,4},{4,0},{8,12},{12,8},{1,5},{5,1},{9,13},{13,9},{2,6},{6,2},{1... | collective-permute-start | bytes 786440 | tf_op jit(solution)/shard_map/ppermute | solution.py:1072
  50.5 0.0 collective-permute-start.12
  50.5 4.5 %collective-permute-start.13 = (bf16[2,2,16,4096]{3,2,1,0:T(8,128)(2,1)S(1)}, bf16[2,2,16,4096]{3,2,1,0:T(8,128)(2,1)S(1)}, u32[]{:S(2)}, u32[]{:S(2)}) collective-permute-start(bf16[2,2,16,4096]{3,2,1,0:T(8,128)(2,1)S(1)} %tie.9), channel_id=1, source_target_pairs={{0,12},{12,0},{1,13},{13,1},{2,14},{14,2},{3,15},{15,3},{16,28},{2... | collective-permute-start | bytes 1572872 | tf_op jit(solution)/shard_map/ppermute | solution.py:1070
  55.0 0.4 place_near.1.refs_1_
  55.4 1.1 %settle.2 = (bf16[2,64,4096]{2,1,0:T(8,128)(2,1)}, bf16[2,64,4096]{2,1,0:T(8,128)(2,1)}, f32[8,128]{1,0:T(8,128)S(1)}) custom-call(bf16[2,2,16,4096]{3,2,1,0:T(8,128)(2,1)S(1)} %get-tuple-element.69.refs_0_, bf16[2,16,4096]{2,1,0:T(8,128)(2,1)S(1)} %place_near.1.refs_1_, bf16[2,16,4096]{2,1,0:T(8,128)(2,1)S(1)} %collective-permute-done.4.refs_4_.refs_2_, ...), custom_call_target="tpu_custom_call" | custom-call | tf_op jit(solution)/shard_map/settle/pallas_call | solution.py:51
  56.5 2.4 %collective-permute-done.7.refs_1_ = bf16[128,1024]{1,0:T(8,128)(2,1)S(1)} collective-permute-done((bf16[128,1024]{1,0:T(8,128)(2,1)S(1)}, bf16[128,1024]{1,0:T(8,128)(2,1)S(1)}, u32[]{:S(2)}, u32[]{:S(2)}) %collective-permute-start.7) | collective-permute-done | bytes 262176 | tf_op jit(solution)/shard_map/ppermute | solution.py:1067
  58.9 2.4 %project.5.refs_2_ = f32[128,4096]{1,0:T(8,128)S(1)} custom-call(bf16[128,1024]{1,0:T(8,128)(2,1)S(1)} %combine.3.refs_0_, bf16[128,1024]{1,0:T(8,128)(2,1)S(1)} %collective-permute-done.7.refs_1_, bf16[3072,4096]{1,0:T(8,128)(2,1)S(1)} %get-tuple-element.68.refs_2_.refs_1_, f32[128,4096]{1,0:T(8,128)S(1)} %project.4.refs_5_.refs_4_.refs_3_.refs_1_, ...), custom_call_target="tpu_custom_call" | custom-call | tf_op jit(solution)/shard_map/project/pallas_call | solution.py:51
  61.4 4.0 %collective-permute-done.6.refs_0_ = bf16[128,1024]{1,0:T(8,128)(2,1)S(1)} collective-permute-done((bf16[128,1024]{1,0:T(8,128)(2,1)S(1)}, bf16[128,1024]{1,0:T(8,128)(2,1)S(1)}, u32[]{:S(2)}, u32[]{:S(2)}) %collective-permute-start.6) | collective-permute-done | bytes 262176 | tf_op jit(solution)/shard_map/ppermute | solution.py:1072
  65.4 0.8 project.7
  66.2 0.1 collective-permute-start.10
  66.3 0.8 project.6
  67.1 0.6 collective-permute-start.8
  67.6 0.2 collective-permute-done.10.refs_1_
  67.9 1.6 %collective-permute-start.11 = (bf16[32,2048]{1,0:T(8,128)(2,1)S(1)}, bf16[32,2048]{1,0:T(8,128)(2,1)S(1)}, u32[]{:S(2)}, u32[]{:S(2)}) collective-permute-start(bf16[32,2048]{1,0:T(8,128)(2,1)S(1)} %get-tuple-element.78), channel_id=1, source_target_pairs={{0,2},{1,3},{2,0},{3,1},{4,6},{5,7},{6,4},{7,5},{8,10},{9,11},{10,... | collective-permute-start | bytes 393224 | tf_op jit(solution)/shard_map/ppermute | solution.py:969
  69.4 0.0 collective-permute-done.8.refs_1_
  69.5 1.0 %collective-permute-start.9 = (bf16[32,2048]{1,0:T(8,128)(2,1)S(1)}, bf16[32,2048]{1,0:T(8,128)(2,1)S(1)}, u32[]{:S(2)}, u32[]{:S(2)}) collective-permute-start(bf16[32,2048]{1,0:T(8,128)(2,1)S(1)} %get-tuple-element.74), channel_id=1, source_target_pairs={{0,2},{1,3},{2,0},{3,1},{4,6},{5,7},{6,4},{7,5},{8,10},{9,11},{10,... | collective-permute-start | bytes 393224 | tf_op jit(solution)/shard_map/ppermute | solution.py:969
  70.5 1.4 %slot_rows.1 = s32[2,64]{1,0:T(2,128)} custom-call(s32[8,128]{1,0:T(8,128)S(1)} %get-tuple-element.46.refs_0_.refs_1_, bf16[128,1152]{1,0:T(8,128)(2,1)S(1)} %value.4.refs_0_.refs_2_.refs_1_, bf16[128,1152]{1,0:T(8,128)(2,1)S(1)} %collective-permute-done.2.refs_1_.refs_3_.refs_2_, f32[32,2048]{1,0:T(8,128)S(1)} %get-tuple-element.77.refs_2_.refs_3_), custom_call_target="tpu_custom_call" | custom-call | tf_op jit(solution)/shard_map/slot_rows/pallas_call | solution.py:51
  71.8 2.4 %collective-permute-done.11.refs_3_ = bf16[32,2048]{1,0:T(8,128)(2,1)S(1)} collective-permute-done((bf16[32,2048]{1,0:T(8,128)(2,1)S(1)}, bf16[32,2048]{1,0:T(8,128)(2,1)S(1)}, u32[]{:S(2)}, u32[]{:S(2)}) %collective-permute-start.11) | collective-permute-done | bytes 131104 | tf_op jit(solution)/shard_map/ppermute | solution.py:969
  74.3 2.0 %collective-permute-done.9.refs_1_ = bf16[32,2048]{1,0:T(8,128)(2,1)S(1)} collective-permute-done((bf16[32,2048]{1,0:T(8,128)(2,1)S(1)}, bf16[32,2048]{1,0:T(8,128)(2,1)S(1)}, u32[]{:S(2)}, u32[]{:S(2)}) %collective-permute-start.9) | collective-permute-done | bytes 131104 | tf_op jit(solution)/shard_map/ppermute | solution.py:969
  76.3 0.8 finish.1
  77.0 8.2 %collective-permute-done.12.refs_0_ = bf16[2,2,16,4096]{3,2,1,0:T(8,128)(2,1)S(1)} collective-permute-done((bf16[2,2,16,4096]{3,2,1,0:T(8,128)(2,1)S(1)}, bf16[2,2,16,4096]{3,2,1,0:T(8,128)(2,1)S(1)}, u32[]{:S(2)}, u32[]{:S(2)}) %collective-permute-start.12) | collective-permute-done | bytes 524320 | tf_op jit(solution)/shard_map/ppermute | solution.py:1069
  85.2 0.0 collective-permute-done.13.refs_1_
  85.2 1.6 %settle.3 = (bf16[2,64,4096]{2,1,0:T(8,128)(2,1)}, bf16[2,64,4096]{2,1,0:T(8,128)(2,1)}, f32[8,128]{1,0:T(8,128)}) custom-call(bf16[2,2,16,4096]{3,2,1,0:T(8,128)(2,1)S(1)} %collective-permute-done.12.refs_0_, bf16[2,2,16,4096]{3,2,1,0:T(8,128)(2,1)S(1)} %collective-permute-done.13.refs_1_, ...), custom_call_target="tpu_custom_call", output_to_operand_aliasing={{0}: (2, {}), {1}: (3, {})} | custom-call | tf_op jit(solution)/shard_map/settle/pallas_call | solution.py:51
  (7 shorter events, 0.1 us)
Async XLA Ops:
  2.3 14.7 %collective-permute-start = (bf16[34,32,128]{2,1,0:T(8,128)(2,1)S(1)}, bf16[34,32,128]{2,1,0:T(8,128)(2,1)S(1)}, u32[]{:S(2)}, u32[]{:S(2)}) collective-permute-start(bf16[34,32,128]{2,1,0:T(8,128)(2,1)S(1)} %get-tuple-element.51), channel_id=1, source_target_pairs={{0,4},{4,0},{8,12},{12,8},{1,5},{5,1},{9,13},{13,9},{2,6},{6,2},{1... | collective-permute-start | bytes 835592 | tf_op jit(solution)/shard_map/ppermute | solution.py:1029
  5.4 29.7 %collective-permute-start.5 = (bf16[2,2,16,4096]{3,2,1,0:T(8,128)(2,1)S(1)}, bf16[2,2,16,4096]{3,2,1,0:T(8,128)(2,1)S(1)}, u32[]{:S(2)}, u32[]{:S(2)}) collective-permute-start(bf16[2,2,16,4096]{3,2,1,0:T(8,128)(2,1)S(1)} %get-tuple-element.45.refs_7_.refs_0_), channel_id=1, source_target_pairs={{4,8},{8,4},{5,9},{9,5},{6,10},{10,6},{7,11},{11,7},{20,24},{24,20... | collective-permute-start | bytes 1572872 | tf_op jit(solution)/shard_map/ppermute | solution.py:1030
  7.5 12.9 %collective-permute-start.1 = (bf16[33,32,128]{2,1,0:T(8,128)(2,1)S(1)}, bf16[33,32,128]{2,1,0:T(8,128)(2,1)S(1)}, u32[]{:S(2)}, u32[]{:S(2)}) collective-permute-start(bf16[33,32,128]{2,1,0:T(8,128)(2,1)S(1)} %tie.5), channel_id=1, source_target_pairs={{0,4},{4,0},{8,12},{12,8},{1,5},{5,1},{9,13},{13,9},{2,6},{6,2},{1... | collective-permute-start | bytes 811016 | tf_op jit(solution)/shard_map/ppermute | solution.py:1034
  21.1 15.1 %collective-permute-start.2 = (bf16[128,1152]{1,0:T(8,128)(2,1)S(1)}, bf16[128,1152]{1,0:T(8,128)(2,1)S(1)}, u32[]{:S(2)}, u32[]{:S(2)}) collective-permute-start(bf16[128,1152]{1,0:T(8,128)(2,1)S(1)} %value.4.refs_0_.refs_2_.refs_1_), channel_id=1, source_target_pairs={{0,8},{4,12},{8,0},{12,4},{1,9},{5,13},{9,1},{13,5},{2,10},{6,14},... | collective-permute-start | bytes 884744 | tf_op jit(solution)/shard_map/ppermute | solution.py:1063
  32.3 15.1 %collective-permute-start.4 = (bf16[2,16,4096]{2,1,0:T(8,128)(2,1)S(1)}, bf16[2,16,4096]{2,1,0:T(8,128)(2,1)S(1)}, u32[]{:S(2)}, u32[]{:S(2)}) collective-permute-start(bf16[2,16,4096]{2,1,0:T(8,128)(2,1)S(1)} %tie.7), channel_id=1, source_target_pairs={{0,4},{4,0},{8,12},{12,8},{1,5},{5,1},{9,13},{13,9},{2,6},{6,2},{1... | collective-permute-start | bytes 786440 | tf_op jit(solution)/shard_map/ppermute | solution.py:1064
  33.9 13.5 %collective-permute-start.3 = (bf16[128,1024]{1,0:T(8,128)(2,1)S(1)}, bf16[128,1024]{1,0:T(8,128)(2,1)S(1)}, u32[]{:S(2)}, u32[]{:S(2)}) collective-permute-start(bf16[128,1024]{1,0:T(8,128)(2,1)S(1)} %tie.6.refs_2_), channel_id=1, source_target_pairs={{0,8},{4,12},{8,0},{12,4},{1,9},{5,13},{9,1},{13,5},{2,10},{6,14},... | collective-permute-start | bytes 786440 | tf_op jit(solution)/shard_map/ppermute | solution.py:1063
  36.7 22.2 %collective-permute-start.7 = (bf16[128,1024]{1,0:T(8,128)(2,1)S(1)}, bf16[128,1024]{1,0:T(8,128)(2,1)S(1)}, u32[]{:S(2)}, u32[]{:S(2)}) collective-permute-start(bf16[128,1024]{1,0:T(8,128)(2,1)S(1)} %combine.2.refs_0_), channel_id=1, source_target_pairs={{0,4},{4,0},{8,12},{12,8},{1,5},{5,1},{9,13},{13,9},{2,6},{6,2},{1... | collective-permute-start | bytes 786440 | tf_op jit(solution)/shard_map/ppermute | solution.py:1067
  47.9 17.5 %collective-permute-start.6 = (bf16[128,1024]{1,0:T(8,128)(2,1)S(1)}, bf16[128,1024]{1,0:T(8,128)(2,1)S(1)}, u32[]{:S(2)}, u32[]{:S(2)}) collective-permute-start(bf16[128,1024]{1,0:T(8,128)(2,1)S(1)} %combine.3.refs_0_), channel_id=1, source_target_pairs={{0,4},{4,0},{8,12},{12,8},{1,5},{5,1},{9,13},{13,9},{2,6},{6,2},{1... | collective-permute-start | bytes 786440 | tf_op jit(solution)/shard_map/ppermute | solution.py:1072
  50.5 34.7 %collective-permute-start.12 = (bf16[2,2,16,4096]{3,2,1,0:T(8,128)(2,1)S(1)}, bf16[2,2,16,4096]{3,2,1,0:T(8,128)(2,1)S(1)}, u32[]{:S(2)}, u32[]{:S(2)}) collective-permute-start(bf16[2,2,16,4096]{3,2,1,0:T(8,128)(2,1)S(1)} %tie.8), channel_id=1, source_target_pairs={{0,8},{4,12},{8,0},{12,4},{1,9},{5,13},{9,1},{13,5},{2,10},{6,14},... | collective-permute-start | bytes 1572872 | tf_op jit(solution)/shard_map/ppermute | solution.py:1069
  50.5 34.7 %collective-permute-start.13 = (bf16[2,2,16,4096]{3,2,1,0:T(8,128)(2,1)S(1)}, bf16[2,2,16,4096]{3,2,1,0:T(8,128)(2,1)S(1)}, u32[]{:S(2)}, u32[]{:S(2)}) collective-permute-start(bf16[2,2,16,4096]{3,2,1,0:T(8,128)(2,1)S(1)} %tie.9), channel_id=1, source_target_pairs={{0,12},{12,0},{1,13},{13,1},{2,14},{14,2},{3,15},{15,3},{16,28},{2... | collective-permute-start | bytes 1572872 | tf_op jit(solution)/shard_map/ppermute | solution.py:1070
  66.2 1.6 %collective-permute-start.10 = (bf16[2,32,2048]{2,1,0:T(8,128)(2,1)S(1)}, bf16[2,32,2048]{2,1,0:T(8,128)(2,1)S(1)}, u32[]{:S(2)}, u32[]{:S(2)}) collective-permute-start(bf16[2,32,2048]{2,1,0:T(8,128)(2,1)S(1)} %get-tuple-element.76), channel_id=1, source_target_pairs={{0,1},{1,0},{2,3},{3,2},{4,5},{5,4},{6,7},{7,6},{8,9},{9,8},{10,11... | collective-permute-start | bytes 786440 | tf_op jit(solution)/shard_map/ppermute | solution.py:956
  67.1 2.4 %collective-permute-start.8 = (bf16[2,32,2048]{2,1,0:T(8,128)(2,1)S(1)}, bf16[2,32,2048]{2,1,0:T(8,128)(2,1)S(1)}, u32[]{:S(2)}, u32[]{:S(2)}) collective-permute-start(bf16[2,32,2048]{2,1,0:T(8,128)(2,1)S(1)} %get-tuple-element.72), channel_id=1, source_target_pairs={{0,1},{1,0},{2,3},{3,2},{4,5},{5,4},{6,7},{7,6},{8,9},{9,8},{10,11... | collective-permute-start | bytes 786440 | tf_op jit(solution)/shard_map/ppermute | solution.py:956
  67.9 6.4 %collective-permute-start.11 = (bf16[32,2048]{1,0:T(8,128)(2,1)S(1)}, bf16[32,2048]{1,0:T(8,128)(2,1)S(1)}, u32[]{:S(2)}, u32[]{:S(2)}) collective-permute-start(bf16[32,2048]{1,0:T(8,128)(2,1)S(1)} %get-tuple-element.78), channel_id=1, source_target_pairs={{0,2},{1,3},{2,0},{3,1},{4,6},{5,7},{6,4},{7,5},{8,10},{9,11},{10,... | collective-permute-start | bytes 393224 | tf_op jit(solution)/shard_map/ppermute | solution.py:969
  69.5 6.8 %collective-permute-start.9 = (bf16[32,2048]{1,0:T(8,128)(2,1)S(1)}, bf16[32,2048]{1,0:T(8,128)(2,1)S(1)}, u32[]{:S(2)}, u32[]{:S(2)}) collective-permute-start(bf16[32,2048]{1,0:T(8,128)(2,1)S(1)} %get-tuple-element.74), channel_id=1, source_target_pairs={{0,2},{1,3},{2,0},{3,1},{4,6},{5,7},{6,4},{7,5},{8,10},{9,11},{10,... | collective-permute-start | bytes 393224 | tf_op jit(solution)/shard_map/ppermute | solution.py:969

commit v4 on v3

--- a/solution.py
+++ b/solution.py
@@ -591,7 +591,8 @@
         shift = jnp.concatenate([rows[:, g : g + 1] for g in range(group)], axis=0)
         weights = jnp.where(mask, jnp.exp(jnp.minimum(found - shift, 0.0)), 0.0)
         weights = weights.astype(jnp.bfloat16)
-        total = jnp.sum(weights.astype(jnp.float32), axis=1, keepdims=True)
+        ones = jnp.ones((weights.shape[1], LANES), jnp.bfloat16)
+        total = jnp.dot(weights, ones, preferred_element_type=jnp.float32)
         block_total = jnp.zeros((count, LANES), jnp.float32)
         for g in range(group):
             block_total = jnp.where(lane == g, total[g * count : (g + 1) * count], block_total)
@@ -1057,18 +1058,21 @@
         send_far, send_near, kept = place_pages(
             page_owner, caches, jobs, cap, tp_size, False, (payload[1],)
         )
-        blocks = ((True, 1), (False, 0), (False, 1))
+        blocks = ((True, 1), (False, 0))
         held, held_done = fetch(out_weight, blocks, chunks, head_count, part, payload[1:])
         payload[1] = tie(payload[1], held_done)
+        held_last, held_done = fetch(
+            out_weight, ((False, 1),), chunks, head_count, part, (held_done,)
+        )
         theirs = [lax.ppermute(p, "tp", flip(tp_size, 2)) for p in payload]
         got_near = lax.ppermute(tie(send_near, held_done), "tp", flip(tp_size, 1))
         near_pages = place_near(near_keys, near_values, head_count, cap, tp_size)
-        first_part = combine(payload, theirs, 0, (got_inner,))
+        first_part = combine(payload, theirs, 0)
         near_first = lax.ppermute(first_part, "tp", flip(tp_size, 1))
         total = project([first_part], out_weight, None, chunks, head_count, None, everything, None)
         got_far = lax.ppermute(tie(send_far, total), "tp", flip(tp_size, 2))
         got_outer = lax.ppermute(tie(send_last, total), "tp", [(0, 3), (3, 0)])
-        second_part = combine(payload, theirs, 1, (got_near, total))
+        second_part = combine(payload, theirs, 1, (got_near, total, got_inner))
         near_second = lax.ppermute(second_part, "tp", flip(tp_size, 1))
         own_parts, near_parts = (first_part, second_part), (near_first, near_second)
         plan = ((0, None, None), (1, None, 0), (1, None, 1), (3, (1, 2), None))
@@ -1091,8 +1095,8 @@
             columns = (first, out_width // 2)
             keep, send = project(
                 [near_parts[1]],
-                held,
-                (2,),
+                held_last,
+                (0,),
                 chunks,
                 head_count,
                 total,

time: 87.2 us -> 85.4 us (0.979)
  waiting for transfers between devices: 26.2 us -> 24.2 us
    ppermute x1, waiting for transfers between devices: 2.45 us -> 5.38 us  [body(): near_first = lax.ppermute(first_part, 'tp', flip(tp_size, 1))]
    ppermute x1, waiting for transfers between devices: 4 us -> 1.38 us  [body(): near_second = lax.ppermute(second_part, 'tp', flip(tp_size, 1))]
    ppermute x1, waiting for transfers between devices: 8.15 us -> 6.21 us  [body(): got_far = lax.ppermute(tie(send_far, total), 'tp', flip(tp_size, 2))]
    ppermute x1, starting transfers between devices: 0.01 us -> 1.33 us  [body(): got_far = lax.ppermute(tie(send_far, total), 'tp', flip(tp_size, 2))]
    ppermute x2, waiting for transfers between devices: 1.12 us -> 0.01 us  [body(): theirs = [lax.ppermute(p, 'tp', flip(tp_size, 2)) for p in payload]]
    ppermute x1, starting transfers between devices: 4.53 us -> 3.48 us  [body(): got_outer = lax.ppermute(tie(send_last, total), 'tp', [(0, 3), (3, 0)])]
    ppermute x1, starting transfers between devices: 2.61 us -> 1.72 us  [body(): near_second = lax.ppermute(second_part, 'tp', flip(tp_size, 1))]
    pallas_call x28 -> x29, Pallas kernels: 37.2 us -> 36.8 us  [call(): pl.pallas_call(without_extra, in_specs=list(in_specs) + [anywhere()] * ex...]
  transfers between devices with their start and end apart: 14 -> 14, of which waited for: 8 -> 7; matrix products, arithmetic and copies ran while one was open for 0% -> 0% of each run, Pallas kernels for 39% -> 39%
where the time goes in v4:
time: 85.4 us; the launch traced here: 85.2 us
  Pallas kernels  36.8 us (43%)
  waiting for transfers between devices  24.2 us (28%)
  starting transfers between devices  23.2 us (27%)
  between operations  1 us (1%)
    pallas_call x29, Pallas kernels, call(): pl.pallas_call(without_extra, in_specs=list(in_specs) + [anywhere()] * ex...  36.8 us
    ppermute x1, waiting for transfers between devices, body(): got_near = lax.ppermute(tie(send_near, held_done), 'tp', flip(tp_size, 1))  6.75 us
    ppermute x1, waiting for transfers between devices, body(): got_far = lax.ppermute(tie(send_far, total), 'tp', flip(tp_size, 2))  6.21 us
    ppermute x1, waiting for transfers between devices, body(): near_first = lax.ppermute(first_part, 'tp', flip(tp_size, 1))  5.38 us
    ppermute x1, starting transfers between devices, body(): near_values = lax.ppermute(tie(values, bounds), 'tp', flip(tp_size, 1))  4.44 us
    ppermute x2, waiting for transfers between devices, sum_heads(): lax.ppermute(part, 'kv', flip(kv_size, 2 * step))  4.33 us
    ppermute x1, starting transfers between devices, body(): got_outer = lax.ppermute(tie(send_last, total), 'tp', [(0, 3), (3, 0)])  3.48 us
    ppermute x1, starting transfers between devices, body(): near_keys = lax.ppermute(keys, 'tp', flip(tp_size, 1))  3.09 us
  transfers between devices with their start and end apart: 14, of which 7 were waited for; matrix products, arithmetic and copies ran while one was open for 0% of the time, Pallas kernels for 39%

profile of v4, /device:TPU:0, one launch (start us, length us, event | category | flops | bytes accessed | tf_op | source)
XLA Modules:
  0.0 85.2 jit_solution(13672261954605831021)
XLA Ops:
  0.6 1.7 %gather_tokens.2 = (bf16[34,32,128]{2,1,0:T(8,128)(2,1)S(1)}, bf16[33,32,128]{2,1,0:T(8,128)(2,1)S(1)}, bf16[2,2,16,4096]{3,2,1,0:T(8,128)(2,1)S(1)}) custom-call(bf16[2,32,4096]{2,1,0:T(8,128)(2,1)} %refs_1_.6, bf16[2,32,4096]{2,1,0:T(8,128)(2,1)} %refs_2_.5, bf16[8,4,256]{2,1,0:T(4,128)(2,1)} %refs_2_.4, bf16[8,4,256]{2,1,0:T(4,128)(2,1)} %refs_3_.3, ...), custom_call_target="tpu_custom_call" | custom-call | tf_op jit(solution)/shard_map/gather_tokens/pallas_call | solution.py:51
  2.3 3.1 %collective-permute-start = (bf16[34,32,128]{2,1,0:T(8,128)(2,1)S(1)}, bf16[34,32,128]{2,1,0:T(8,128)(2,1)S(1)}, u32[]{:S(2)}, u32[]{:S(2)}) collective-permute-start(bf16[34,32,128]{2,1,0:T(8,128)(2,1)S(1)} %get-tuple-element.53), channel_id=1, source_target_pairs={{0,4},{4,0},{8,12},{12,8},{1,5},{5,1},{9,13},{13,9},{2,6},{6,2},{1... | collective-permute-start | bytes 835592 | tf_op jit(solution)/shard_map/ppermute | solution.py:1030
  5.4 0.7 collective-permute-start.5
  6.1 1.4 %gather_tokens.3 = (bf16[34,32,128]{2,1,0:T(8,128)(2,1)S(1)}, bf16[33,32,128]{2,1,0:T(8,128)(2,1)S(1)}, bf16[128,2048]{1,0:T(8,128)(2,1)S(1)}, s32[8,128]{1,0:T(8,128)S(1)}) custom-call(bf16[2,32,4096]{2,1,0:T(8,128)(2,1)} %refs_1_.6, bf16[2,32,4096]{2,1,0:T(8,128)(2,1)} %refs_2_.5, bf16[8,4,256]{2,1,0:T(4,128)(2,1)} %refs_2_.4, bf16[8,4,256]{2,1,0:T(4,128)(2,1)} %refs_3_.3, ...), custom_call_target="tpu_custom_call" | custom-call | tf_op jit(solution)/shard_map/gather_tokens/pallas_call | solution.py:51
  7.5 4.4 %collective-permute-start.1 = (bf16[33,32,128]{2,1,0:T(8,128)(2,1)S(1)}, bf16[33,32,128]{2,1,0:T(8,128)(2,1)S(1)}, u32[]{:S(2)}, u32[]{:S(2)}) collective-permute-start(bf16[33,32,128]{2,1,0:T(8,128)(2,1)S(1)} %tie.5), channel_id=1, source_target_pairs={{0,4},{4,0},{8,12},{12,8},{1,5},{5,1},{9,13},{13,9},{2,6},{6,2},{1... | collective-permute-start | bytes 811016 | tf_op jit(solution)/shard_map/ppermute | solution.py:1035
  11.9 0.7 prepare.1
  12.6 2.5 %score.2 = (bf16[8,256,128]{2,1,0:T(8,128)(2,1)S(1)}, bf16[512,32]{1,0:T(8,128)(2,1)S(1)}, f32[128,128]{1,0:T(8,128)S(1)}, f32[128,128]{1,0:T(8,128)S(1)}) custom-call(bf16[256,2048]{1,0:T(8,128)(2,1)S(1)} %get-tuple-element.54.refs_0_, f32[256,128]{1,0:T(8,128)S(1)} %get-tuple-element.55.refs_1_, f32[128,256]{1,0:T(8,128)S(1)} %get-tuple-element.56.refs_2_, ...), custom_call_target="tpu_custom_call" | custom-call | tf_op jit(solution)/shard_map/score/pallas_call | solution.py:51
  15.2 1.1 %value.3.refs_7_ = f32[128,2048]{1,0:T(8,128)S(1)} custom-call(bf16[8,256,128]{2,1,0:T(8,128)(2,1)S(1)} %get-tuple-element.65.refs_0_, bf16[512,32]{1,0:T(8,128)(2,1)S(1)} %get-tuple-element.66.refs_1_, f32[128,256]{1,0:T(8,128)S(1)} %get-tuple-element.56.refs_2_, bf16[33,32,128]{2,1,0:T(8,128)(2,1)S(1)} %get-tuple-element.67.refs_3_, ...), custom_call_target="tpu_custom_call" | custom-call | tf_op jit(solution)/shard_map/value/pallas_call | solution.py:51
  16.3 0.0 collective-permute-done.refs_3_.refs_9_.refs_0_
  16.3 2.5 %score.3 = (bf16[8,256,128]{2,1,0:T(8,128)(2,1)S(1)}, bf16[512,32]{1,0:T(8,128)(2,1)S(1)}, f32[128,128]{1,0:T(8,128)S(1)}, f32[128,128]{1,0:T(8,128)S(1)}) custom-call(bf16[256,2048]{1,0:T(8,128)(2,1)S(1)} %get-tuple-element.50.refs_0_, f32[256,128]{1,0:T(8,128)S(1)} %get-tuple-element.51.refs_1_, f32[128,256]{1,0:T(8,128)S(1)} %get-tuple-element.52.refs_2_, ...), custom_call_target="tpu_custom_call" | custom-call | flops 17179869184 | tf_op jit(solution)/shard_map/score/pallas_call | solution.py:51
  18.9 0.0 collective-permute-done.1.refs_3_.refs_1_
  18.9 0.8 value.4.refs_0_.refs_2_.refs_1_
  19.6 1.8 %collective-permute-start.2 = (bf16[128,1152]{1,0:T(8,128)(2,1)S(1)}, bf16[128,1152]{1,0:T(8,128)(2,1)S(1)}, u32[]{:S(2)}, u32[]{:S(2)}) collective-permute-start(bf16[128,1152]{1,0:T(8,128)(2,1)S(1)} %value.4.refs_0_.refs_2_.refs_1_), channel_id=1, source_target_pairs={{0,8},{4,12},{8,0},{12,4},{1,9},{5,13},{9,1},{13,5},{2,10},{6,14},... | collective-permute-start | bytes 884744 | tf_op jit(solution)/shard_map/ppermute | solution.py:1067
  21.4 0.7 value.5.refs_1_.refs_0_.refs_3_
  22.2 1.7 %place_pages.1 = (bf16[2,2,16,4096]{3,2,1,0:T(8,128)(2,1)S(1)}, bf16[2,16,4096]{2,1,0:T(8,128)(2,1)S(1)}, bf16[2,2,16,4096]{3,2,1,0:T(8,128)(2,1)S(1)}) custom-call(s32[2,32]{1,0:T(2,128)} %refs_0_.8, bf16[2,32,4096]{2,1,0:T(8,128)(2,1)} %refs_1_.6, bf16[2,32,4096]{2,1,0:T(8,128)(2,1)} %refs_2_.5, bf16[128,1024]{1,0:T(8,128)(2,1)S(1)} %value.5.refs_1_.refs_0_.refs_3_), custom_call_target="tpu_custom_call" | custom-call | tf_op jit(solution)/shard_map/place_pages/pallas_call | solution.py:51
  23.9 5.9 %fetch.2 = (bf16[2048,4096]{1,0:T(8,128)(2,1)S(1)}, f32[8,128]{1,0:T(8,128)S(1)}) custom-call(bf16[4096,4096]{1,0:T(8,128)(2,1)} %refs_1_.7, bf16[128,1024]{1,0:T(8,128)(2,1)S(1)} %value.5.refs_1_.refs_0_.refs_3_), custom_call_target="tpu_custom_call" | custom-call | tf_op jit(solution)/shard_map/fetch/pallas_call | solution.py:51
  29.8 3.5 %fetch.3 = (bf16[1024,4096]{1,0:T(8,128)(2,1)S(1)}, f32[8,128]{1,0:T(8,128)S(1)}) custom-call(bf16[4096,4096]{1,0:T(8,128)(2,1)} %refs_1_.7, f32[8,128]{1,0:T(8,128)S(1)} %get-tuple-element.68.refs_1_), custom_call_target="tpu_custom_call" | custom-call | tf_op jit(solution)/shard_map/fetch/pallas_call | solution.py:51
  33.4 1.6 %collective-permute-start.4 = (bf16[2,16,4096]{2,1,0:T(8,128)(2,1)S(1)}, bf16[2,16,4096]{2,1,0:T(8,128)(2,1)S(1)}, u32[]{:S(2)}, u32[]{:S(2)}) collective-permute-start(bf16[2,16,4096]{2,1,0:T(8,128)(2,1)S(1)} %tie.7), channel_id=1, source_target_pairs={{0,4},{4,0},{8,12},{12,8},{1,5},{5,1},{9,13},{13,9},{2,6},{6,2},{1... | collective-permute-start | bytes 786440 | tf_op jit(solution)/shard_map/ppermute | solution.py:1068
  35.0 0.4 collective-permute-start.3
  35.4 0.0 collective-permute-done.2.refs_1_.refs_3_.refs_2_
  35.4 0.5 combine.2.refs_0_
  35.9 3.9 %project.4.refs_5_.refs_4_.refs_3_.refs_1_ = f32[128,4096]{1,0:T(8,128)S(1)} custom-call(bf16[128,1024]{1,0:T(8,128)(2,1)S(1)} %combine.2.refs_0_, bf16[4096,4096]{1,0:T(8,128)(2,1)} %refs_1_.7), custom_call_target="tpu_custom_call" | custom-call | tf_op jit(solution)/shard_map/project/pallas_call | solution.py:51
  39.8 1.4 %collective-permute-start.7 = (bf16[128,1024]{1,0:T(8,128)(2,1)S(1)}, bf16[128,1024]{1,0:T(8,128)(2,1)S(1)}, u32[]{:S(2)}, u32[]{:S(2)}) collective-permute-start(bf16[128,1024]{1,0:T(8,128)(2,1)S(1)} %combine.2.refs_0_), channel_id=1, source_target_pairs={{0,4},{4,0},{8,12},{12,8},{1,5},{5,1},{9,13},{13,9},{2,6},{6,2},{1... | collective-permute-start | bytes 786440 | tf_op jit(solution)/shard_map/ppermute | solution.py:1071
  41.1 0.0 collective-permute-done.5.refs_6_.refs_3_
  41.1 6.7 %collective-permute-done.4.refs_4_.refs_2_ = bf16[2,16,4096]{2,1,0:T(8,128)(2,1)S(1)} collective-permute-done((bf16[2,16,4096]{2,1,0:T(8,128)(2,1)S(1)}, bf16[2,16,4096]{2,1,0:T(8,128)(2,1)S(1)}, u32[]{:S(2)}, u32[]{:S(2)}) %collective-permute-start.4) | collective-permute-done | bytes 262176 | tf_op jit(solution)/shard_map/ppermute | solution.py:1068
  47.9 0.0 collective-permute-done.3.refs_3_
  47.9 0.5 combine.3.refs_0_
  48.4 1.7 %collective-permute-start.6 = (bf16[128,1024]{1,0:T(8,128)(2,1)S(1)}, bf16[128,1024]{1,0:T(8,128)(2,1)S(1)}, u32[]{:S(2)}, u32[]{:S(2)}) collective-permute-start(bf16[128,1024]{1,0:T(8,128)(2,1)S(1)} %combine.3.refs_0_), channel_id=1, source_target_pairs={{0,4},{4,0},{8,12},{12,8},{1,5},{5,1},{9,13},{13,9},{2,6},{6,2},{1... | collective-permute-start | bytes 786440 | tf_op jit(solution)/shard_map/ppermute | solution.py:1076
  50.1 1.3 %collective-permute-start.12 = (bf16[2,2,16,4096]{3,2,1,0:T(8,128)(2,1)S(1)}, bf16[2,2,16,4096]{3,2,1,0:T(8,128)(2,1)S(1)}, u32[]{:S(2)}, u32[]{:S(2)}) collective-permute-start(bf16[2,2,16,4096]{3,2,1,0:T(8,128)(2,1)S(1)} %tie.8), channel_id=1, source_target_pairs={{0,8},{4,12},{8,0},{12,4},{1,9},{5,13},{9,1},{13,5},{2,10},{6,14},... | collective-permute-start | bytes 1572872 | tf_op jit(solution)/shard_map/ppermute | solution.py:1073
  51.4 3.5 %collective-permute-start.13 = (bf16[2,2,16,4096]{3,2,1,0:T(8,128)(2,1)S(1)}, bf16[2,2,16,4096]{3,2,1,0:T(8,128)(2,1)S(1)}, u32[]{:S(2)}, u32[]{:S(2)}) collective-permute-start(bf16[2,2,16,4096]{3,2,1,0:T(8,128)(2,1)S(1)} %tie.9), channel_id=1, source_target_pairs={{0,12},{12,0},{1,13},{13,1},{2,14},{14,2},{3,15},{15,3},{16,28},{2... | collective-permute-start | bytes 1572872 | tf_op jit(solution)/shard_map/ppermute | solution.py:1074
  54.9 0.4 place_near.1.refs_1_
  55.3 1.1 %settle.2 = (bf16[2,64,4096]{2,1,0:T(8,128)(2,1)}, bf16[2,64,4096]{2,1,0:T(8,128)(2,1)}, f32[8,128]{1,0:T(8,128)S(1)}) custom-call(bf16[2,2,16,4096]{3,2,1,0:T(8,128)(2,1)S(1)} %get-tuple-element.73.refs_0_, bf16[2,16,4096]{2,1,0:T(8,128)(2,1)S(1)} %place_near.1.refs_1_, bf16[2,16,4096]{2,1,0:T(8,128)(2,1)S(1)} %collective-permute-done.4.refs_4_.refs_2_, ...), custom_call_target="tpu_custom_call" | custom-call | tf_op jit(solution)/shard_map/settle/pallas_call | solution.py:51
  56.4 5.4 %collective-permute-done.7.refs_1_ = bf16[128,1024]{1,0:T(8,128)(2,1)S(1)} collective-permute-done((bf16[128,1024]{1,0:T(8,128)(2,1)S(1)}, bf16[128,1024]{1,0:T(8,128)(2,1)S(1)}, u32[]{:S(2)}, u32[]{:S(2)}) %collective-permute-start.7) | collective-permute-done | bytes 262176 | tf_op jit(solution)/shard_map/ppermute | solution.py:1071
  61.8 2.4 %project.5.refs_2_ = f32[128,4096]{1,0:T(8,128)S(1)} custom-call(bf16[128,1024]{1,0:T(8,128)(2,1)S(1)} %combine.3.refs_0_, bf16[128,1024]{1,0:T(8,128)(2,1)S(1)} %collective-permute-done.7.refs_1_, bf16[2048,4096]{1,0:T(8,128)(2,1)S(1)} %get-tuple-element.72.refs_2_, f32[128,4096]{1,0:T(8,128)S(1)} %project.4.refs_5_.refs_4_.refs_3_.refs_1_, ...), custom_call_target="tpu_custom_call" | custom-call | tf_op jit(solution)/shard_map/project/pallas_call | solution.py:51
  64.2 1.4 %collective-permute-done.6.refs_0_ = bf16[128,1024]{1,0:T(8,128)(2,1)S(1)} collective-permute-done((bf16[128,1024]{1,0:T(8,128)(2,1)S(1)}, bf16[128,1024]{1,0:T(8,128)(2,1)S(1)}, u32[]{:S(2)}, u32[]{:S(2)}) %collective-permute-start.6) | collective-permute-done | bytes 262176 | tf_op jit(solution)/shard_map/ppermute | solution.py:1076
  65.6 0.8 project.7
  66.4 0.1 collective-permute-start.10
  66.4 0.8 project.6
  67.2 0.6 collective-permute-start.8
  67.8 0.2 collective-permute-done.10.refs_1_
  68.0 1.7 %collective-permute-start.11 = (bf16[32,2048]{1,0:T(8,128)(2,1)S(1)}, bf16[32,2048]{1,0:T(8,128)(2,1)S(1)}, u32[]{:S(2)}, u32[]{:S(2)}) collective-permute-start(bf16[32,2048]{1,0:T(8,128)(2,1)S(1)} %get-tuple-element.82), channel_id=1, source_target_pairs={{0,2},{1,3},{2,0},{3,1},{4,6},{5,7},{6,4},{7,5},{8,10},{9,11},{10,... | collective-permute-start | bytes 393224 | tf_op jit(solution)/shard_map/ppermute | solution.py:970
  69.7 0.0 collective-permute-done.8.refs_1_
  69.7 0.1 add_core.2
  69.8 1.0 %collective-permute-start.9 = (bf16[32,2048]{1,0:T(8,128)(2,1)S(1)}, bf16[32,2048]{1,0:T(8,128)(2,1)S(1)}, u32[]{:S(2)}, u32[]{:S(2)}) collective-permute-start(bf16[32,2048]{1,0:T(8,128)(2,1)S(1)} %get-tuple-element.78), channel_id=1, source_target_pairs={{0,2},{1,3},{2,0},{3,1},{4,6},{5,7},{6,4},{7,5},{8,10},{9,11},{10,... | collective-permute-start | bytes 393224 | tf_op jit(solution)/shard_map/ppermute | solution.py:970
  70.7 1.4 %slot_rows.1 = s32[2,64]{1,0:T(2,128)} custom-call(s32[8,128]{1,0:T(8,128)S(1)} %get-tuple-element.48.refs_0_.refs_1_, bf16[128,1152]{1,0:T(8,128)(2,1)S(1)} %value.4.refs_0_.refs_2_.refs_1_, bf16[128,1152]{1,0:T(8,128)(2,1)S(1)} %collective-permute-done.2.refs_1_.refs_3_.refs_2_, f32[32,2048]{1,0:T(8,128)S(1)} %get-tuple-element.81.refs_2_.refs_3_), custom_call_target="tpu_custom_call" | custom-call | tf_op jit(solution)/shard_map/slot_rows/pallas_call | solution.py:51
  72.1 2.3 %collective-permute-done.11.refs_3_ = bf16[32,2048]{1,0:T(8,128)(2,1)S(1)} collective-permute-done((bf16[32,2048]{1,0:T(8,128)(2,1)S(1)}, bf16[32,2048]{1,0:T(8,128)(2,1)S(1)}, u32[]{:S(2)}, u32[]{:S(2)}) %collective-permute-start.11) | collective-permute-done | bytes 131104 | tf_op jit(solution)/shard_map/ppermute | solution.py:970
  74.4 2.0 %collective-permute-done.9.refs_1_ = bf16[32,2048]{1,0:T(8,128)(2,1)S(1)} collective-permute-done((bf16[32,2048]{1,0:T(8,128)(2,1)S(1)}, bf16[32,2048]{1,0:T(8,128)(2,1)S(1)}, u32[]{:S(2)}, u32[]{:S(2)}) %collective-permute-start.9) | collective-permute-done | bytes 131104 | tf_op jit(solution)/shard_map/ppermute | solution.py:970
  76.4 0.8 finish.1
  77.2 6.2 %collective-permute-done.12.refs_0_ = bf16[2,2,16,4096]{3,2,1,0:T(8,128)(2,1)S(1)} collective-permute-done((bf16[2,2,16,4096]{3,2,1,0:T(8,128)(2,1)S(1)}, bf16[2,2,16,4096]{3,2,1,0:T(8,128)(2,1)S(1)}, u32[]{:S(2)}, u32[]{:S(2)}) %collective-permute-start.12) | collective-permute-done | bytes 524320 | tf_op jit(solution)/shard_map/ppermute | solution.py:1073
  83.4 0.0 collective-permute-done.13.refs_1_
  83.4 1.6 %settle.3 = (bf16[2,64,4096]{2,1,0:T(8,128)(2,1)}, bf16[2,64,4096]{2,1,0:T(8,128)(2,1)}, f32[8,128]{1,0:T(8,128)}) custom-call(bf16[2,2,16,4096]{3,2,1,0:T(8,128)(2,1)S(1)} %collective-permute-done.12.refs_0_, bf16[2,2,16,4096]{3,2,1,0:T(8,128)(2,1)S(1)} %collective-permute-done.13.refs_1_, ...), custom_call_target="tpu_custom_call", output_to_operand_aliasing={{0}: (2, {}), {1}: (3, {})} | custom-call | tf_op jit(solution)/shard_map/settle/pallas_call | solution.py:51
  (6 shorter events, 0.1 us)
Async XLA Ops:
  2.3 14.0 %collective-permute-start = (bf16[34,32,128]{2,1,0:T(8,128)(2,1)S(1)}, bf16[34,32,128]{2,1,0:T(8,128)(2,1)S(1)}, u32[]{:S(2)}, u32[]{:S(2)}) collective-permute-start(bf16[34,32,128]{2,1,0:T(8,128)(2,1)S(1)} %get-tuple-element.53), channel_id=1, source_target_pairs={{0,4},{4,0},{8,12},{12,8},{1,5},{5,1},{9,13},{13,9},{2,6},{6,2},{1... | collective-permute-start | bytes 835592 | tf_op jit(solution)/shard_map/ppermute | solution.py:1030
  5.4 35.7 %collective-permute-start.5 = (bf16[2,2,16,4096]{3,2,1,0:T(8,128)(2,1)S(1)}, bf16[2,2,16,4096]{3,2,1,0:T(8,128)(2,1)S(1)}, u32[]{:S(2)}, u32[]{:S(2)}) collective-permute-start(bf16[2,2,16,4096]{3,2,1,0:T(8,128)(2,1)S(1)} %get-tuple-element.47.refs_7_.refs_0_), channel_id=1, source_target_pairs={{4,8},{8,4},{5,9},{9,5},{6,10},{10,6},{7,11},{11,7},{20,24},{24,20... | collective-permute-start | bytes 1572872 | tf_op jit(solution)/shard_map/ppermute | solution.py:1031
  7.5 11.4 %collective-permute-start.1 = (bf16[33,32,128]{2,1,0:T(8,128)(2,1)S(1)}, bf16[33,32,128]{2,1,0:T(8,128)(2,1)S(1)}, u32[]{:S(2)}, u32[]{:S(2)}) collective-permute-start(bf16[33,32,128]{2,1,0:T(8,128)(2,1)S(1)} %tie.5), channel_id=1, source_target_pairs={{0,4},{4,0},{8,12},{12,8},{1,5},{5,1},{9,13},{13,9},{2,6},{6,2},{1... | collective-permute-start | bytes 811016 | tf_op jit(solution)/shard_map/ppermute | solution.py:1035
  19.6 15.8 %collective-permute-start.2 = (bf16[128,1152]{1,0:T(8,128)(2,1)S(1)}, bf16[128,1152]{1,0:T(8,128)(2,1)S(1)}, u32[]{:S(2)}, u32[]{:S(2)}) collective-permute-start(bf16[128,1152]{1,0:T(8,128)(2,1)S(1)} %value.4.refs_0_.refs_2_.refs_1_), channel_id=1, source_target_pairs={{0,8},{4,12},{8,0},{12,4},{1,9},{5,13},{9,1},{13,5},{2,10},{6,14},... | collective-permute-start | bytes 884744 | tf_op jit(solution)/shard_map/ppermute | solution.py:1067
  33.4 14.5 %collective-permute-start.4 = (bf16[2,16,4096]{2,1,0:T(8,128)(2,1)S(1)}, bf16[2,16,4096]{2,1,0:T(8,128)(2,1)S(1)}, u32[]{:S(2)}, u32[]{:S(2)}) collective-permute-start(bf16[2,16,4096]{2,1,0:T(8,128)(2,1)S(1)} %tie.7), channel_id=1, source_target_pairs={{0,4},{4,0},{8,12},{12,8},{1,5},{5,1},{9,13},{13,9},{2,6},{6,2},{1... | collective-permute-start | bytes 786440 | tf_op jit(solution)/shard_map/ppermute | solution.py:1068
  35.0 12.9 %collective-permute-start.3 = (bf16[128,1024]{1,0:T(8,128)(2,1)S(1)}, bf16[128,1024]{1,0:T(8,128)(2,1)S(1)}, u32[]{:S(2)}, u32[]{:S(2)}) collective-permute-start(bf16[128,1024]{1,0:T(8,128)(2,1)S(1)} %tie.6.refs_2_), channel_id=1, source_target_pairs={{0,8},{4,12},{8,0},{12,4},{1,9},{5,13},{9,1},{13,5},{2,10},{6,14},... | collective-permute-start | bytes 786440 | tf_op jit(solution)/shard_map/ppermute | solution.py:1067
  39.8 22.0 %collective-permute-start.7 = (bf16[128,1024]{1,0:T(8,128)(2,1)S(1)}, bf16[128,1024]{1,0:T(8,128)(2,1)S(1)}, u32[]{:S(2)}, u32[]{:S(2)}) collective-permute-start(bf16[128,1024]{1,0:T(8,128)(2,1)S(1)} %combine.2.refs_0_), channel_id=1, source_target_pairs={{0,4},{4,0},{8,12},{12,8},{1,5},{5,1},{9,13},{13,9},{2,6},{6,2},{1... | collective-permute-start | bytes 786440 | tf_op jit(solution)/shard_map/ppermute | solution.py:1071
  48.4 17.2 %collective-permute-start.6 = (bf16[128,1024]{1,0:T(8,128)(2,1)S(1)}, bf16[128,1024]{1,0:T(8,128)(2,1)S(1)}, u32[]{:S(2)}, u32[]{:S(2)}) collective-permute-start(bf16[128,1024]{1,0:T(8,128)(2,1)S(1)} %combine.3.refs_0_), channel_id=1, source_target_pairs={{0,4},{4,0},{8,12},{12,8},{1,5},{5,1},{9,13},{13,9},{2,6},{6,2},{1... | collective-permute-start | bytes 786440 | tf_op jit(solution)/shard_map/ppermute | solution.py:1076
  50.1 33.3 %collective-permute-start.12 = (bf16[2,2,16,4096]{3,2,1,0:T(8,128)(2,1)S(1)}, bf16[2,2,16,4096]{3,2,1,0:T(8,128)(2,1)S(1)}, u32[]{:S(2)}, u32[]{:S(2)}) collective-permute-start(bf16[2,2,16,4096]{3,2,1,0:T(8,128)(2,1)S(1)} %tie.8), channel_id=1, source_target_pairs={{0,8},{4,12},{8,0},{12,4},{1,9},{5,13},{9,1},{13,5},{2,10},{6,14},... | collective-permute-start | bytes 1572872 | tf_op jit(solution)/shard_map/ppermute | solution.py:1073
  51.4 32.0 %collective-permute-start.13 = (bf16[2,2,16,4096]{3,2,1,0:T(8,128)(2,1)S(1)}, bf16[2,2,16,4096]{3,2,1,0:T(8,128)(2,1)S(1)}, u32[]{:S(2)}, u32[]{:S(2)}) collective-permute-start(bf16[2,2,16,4096]{3,2,1,0:T(8,128)(2,1)S(1)} %tie.9), channel_id=1, source_target_pairs={{0,12},{12,0},{1,13},{13,1},{2,14},{14,2},{3,15},{15,3},{16,28},{2... | collective-permute-start | bytes 1572872 | tf_op jit(solution)/shard_map/ppermute | solution.py:1074
  66.4 1.6 %collective-permute-start.10 = (bf16[2,32,2048]{2,1,0:T(8,128)(2,1)S(1)}, bf16[2,32,2048]{2,1,0:T(8,128)(2,1)S(1)}, u32[]{:S(2)}, u32[]{:S(2)}) collective-permute-start(bf16[2,32,2048]{2,1,0:T(8,128)(2,1)S(1)} %get-tuple-element.80), channel_id=1, source_target_pairs={{0,1},{1,0},{2,3},{3,2},{4,5},{5,4},{6,7},{7,6},{8,9},{9,8},{10,11... | collective-permute-start | bytes 786440 | tf_op jit(solution)/shard_map/ppermute | solution.py:957
  67.2 2.5 %collective-permute-start.8 = (bf16[2,32,2048]{2,1,0:T(8,128)(2,1)S(1)}, bf16[2,32,2048]{2,1,0:T(8,128)(2,1)S(1)}, u32[]{:S(2)}, u32[]{:S(2)}) collective-permute-start(bf16[2,32,2048]{2,1,0:T(8,128)(2,1)S(1)} %get-tuple-element.76), channel_id=1, source_target_pairs={{0,1},{1,0},{2,3},{3,2},{4,5},{5,4},{6,7},{7,6},{8,9},{9,8},{10,11... | collective-permute-start | bytes 786440 | tf_op jit(solution)/shard_map/ppermute | solution.py:957
  68.0 6.4 %collective-permute-start.11 = (bf16[32,2048]{1,0:T(8,128)(2,1)S(1)}, bf16[32,2048]{1,0:T(8,128)(2,1)S(1)}, u32[]{:S(2)}, u32[]{:S(2)}) collective-permute-start(bf16[32,2048]{1,0:T(8,128)(2,1)S(1)} %get-tuple-element.82), channel_id=1, source_target_pairs={{0,2},{1,3},{2,0},{3,1},{4,6},{5,7},{6,4},{7,5},{8,10},{9,11},{10,... | collective-permute-start | bytes 393224 | tf_op jit(solution)/shard_map/ppermute | solution.py:970
  69.8 6.7 %collective-permute-start.9 = (bf16[32,2048]{1,0:T(8,128)(2,1)S(1)}, bf16[32,2048]{1,0:T(8,128)(2,1)S(1)}, u32[]{:S(2)}, u32[]{:S(2)}) collective-permute-start(bf16[32,2048]{1,0:T(8,128)(2,1)S(1)} %get-tuple-element.78), channel_id=1, source_target_pairs={{0,2},{1,3},{2,0},{3,1},{4,6},{5,7},{6,4},{7,5},{8,10},{9,11},{10,... | collective-permute-start | bytes 393224 | tf_op jit(solution)/shard_map/ppermute | solution.py:970

commit v5 on v4

--- a/solution.py
+++ b/solution.py
@@ -586,11 +586,10 @@
         member, row_max, precision=HIGHEST, preferred_element_type=jnp.float32
     )
 
-    def weigh(first_line, count, found, mask):
+    def weigh(first_line, count, found):
         rows = spread[first_line : first_line + count]
         shift = jnp.concatenate([rows[:, g : g + 1] for g in range(group)], axis=0)
-        weights = jnp.where(mask, jnp.exp(jnp.minimum(found - shift, 0.0)), 0.0)
-        weights = weights.astype(jnp.bfloat16)
+        weights = jnp.exp(jnp.minimum(found - shift, 0.0)).astype(jnp.bfloat16)
         ones = jnp.ones((weights.shape[1], LANES), jnp.bfloat16)
         total = jnp.dot(weights, ones, preferred_element_type=jnp.float32)
         block_total = jnp.zeros((count, LANES), jnp.float32)
@@ -600,9 +599,9 @@
 
     totals = []
     for block in range(blocks):
-        weights_ref[block], total = weigh(block * lines, lines, scores[block], page_mask)
+        weights_ref[block], total = weigh(block * lines, lines, scores[block])
         totals.append(total)
-    fresh_ref[...], total = weigh(pages * steps, page_len, fresh_scores[...], fresh_mask)
+    fresh_ref[...], total = weigh(pages * steps, page_len, fresh_scores[...])
     totals.append(total)
     if spare:
         totals.append(jnp.zeros((spare, LANES), jnp.float32))
@@ -706,8 +705,7 @@
             turned, low[:, columns], preferred_element_type=jnp.float32
         )
         if has_earlier:
-            early = early_numer_ref[:, (first + g) * HD : (first + g + 1) * HD]
-            numer = numer + early * scale_early[:, which]
+            numer = numer + early_numer_ref[:, columns] * scale_early[:, which]
         if last:
             numer = numer * inverse[:, which]
         out_ref[:, columns] = numer.astype(out_ref.dtype)
@@ -1037,7 +1035,10 @@
             bounds, query, (0, 1), pages_here, page_len, own_lines, step_count
         )
         scored = score(own_choice, own_keys, step_count)
-        early_numer = value(scored, own_choice[2], own_values, step_count, 0, 1, False)
+        early_numers = [
+            value(scored, own_choice[2], own_values, step_count, chunk, chunks, False)
+            for chunk in range(chunks)
+        ]
         early_max, early_total = scored[2:]
         scored = score(near_choice, near_keys, step_count, (early_max, early_total), 1 << 34)
         payload = [
@@ -1049,7 +1050,7 @@
                 chunk,
                 chunks,
                 True,
-                (early_max, early_numer),
+                (early_max, early_numers[chunk]),
                 () if chunk else (own_keys, near_keys),
             )
             for chunk in range(chunks)

time: 85.4 us -> 85.2 us (level)
    ppermute x1, waiting for transfers between devices: 6.21 us -> 5.06 us  [body(): got_far = lax.ppermute(tie(send_far, total), 'tp', flip(tp_size, 2))]
    pallas_call x29 -> x30, Pallas kernels: 36.8 us -> 36.9 us  [call(): pl.pallas_call(without_extra, in_specs=list(in_specs) + [anywhere()] * ex...]
  transfers between devices with their start and end apart: 14 -> 14, of which waited for: 7 -> 7; matrix products, arithmetic and copies ran while one was open for 0% -> 0% of each run, Pallas kernels for 39% -> 40%
where the time goes in v5:
time: 85.2 us; the launch traced here: 85 us
  Pallas kernels  36.9 us (43%)
  waiting for transfers between devices  24.1 us (28%)
  starting transfers between devices  23 us (27%)
  between operations  1.01 us (1%)
    pallas_call x30, Pallas kernels, call(): pl.pallas_call(without_extra, in_specs=list(in_specs) + [anywhere()] * ex...  36.9 us
    ppermute x1, waiting for transfers between devices, body(): got_near = lax.ppermute(tie(send_near, held_done), 'tp', flip(tp_size, 1))  7.59 us
    ppermute x1, waiting for transfers between devices, body(): near_first = lax.ppermute(first_part, 'tp', flip(tp_size, 1))  5.77 us
    ppermute x1, waiting for transfers between devices, body(): got_far = lax.ppermute(tie(send_far, total), 'tp', flip(tp_size, 2))  5.06 us
    ppermute x2, waiting for transfers between devices, sum_heads(): lax.ppermute(part, 'kv', flip(kv_size, 2 * step))  4.47 us
    ppermute x1, starting transfers between devices, body(): near_values = lax.ppermute(tie(values, bounds), 'tp', flip(tp_size, 1))  4.44 us
    ppermute x1, starting transfers between devices, body(): got_outer = lax.ppermute(tie(send_last, total), 'tp', [(0, 3), (3, 0)])  3.73 us
    ppermute x1, starting transfers between devices, body(): near_keys = lax.ppermute(keys, 'tp', flip(tp_size, 1))  3.09 us
  transfers between devices with their start and end apart: 14, of which 7 were waited for; matrix products, arithmetic and copies ran while one was open for 0% of the time, Pallas kernels for 40%

profile of v5, /device:TPU:0, one launch (start us, length us, event | category | flops | bytes accessed | tf_op | source)
XLA Modules:
  0.0 85.0 jit_solution(4721415604904596862)
XLA Ops:
  0.6 1.7 %gather_tokens.2 = (bf16[34,32,128]{2,1,0:T(8,128)(2,1)S(1)}, bf16[33,32,128]{2,1,0:T(8,128)(2,1)S(1)}, bf16[2,2,16,4096]{3,2,1,0:T(8,128)(2,1)S(1)}) custom-call(bf16[2,32,4096]{2,1,0:T(8,128)(2,1)} %refs_1_.6, bf16[2,32,4096]{2,1,0:T(8,128)(2,1)} %refs_2_.5, bf16[8,4,256]{2,1,0:T(4,128)(2,1)} %refs_2_.4, bf16[8,4,256]{2,1,0:T(4,128)(2,1)} %refs_3_.3, ...), custom_call_target="tpu_custom_call" | custom-call | tf_op jit(solution)/shard_map/gather_tokens/pallas_call | solution.py:51
  2.3 3.1 %collective-permute-start = (bf16[34,32,128]{2,1,0:T(8,128)(2,1)S(1)}, bf16[34,32,128]{2,1,0:T(8,128)(2,1)S(1)}, u32[]{:S(2)}, u32[]{:S(2)}) collective-permute-start(bf16[34,32,128]{2,1,0:T(8,128)(2,1)S(1)} %get-tuple-element.53), channel_id=1, source_target_pairs={{0,4},{4,0},{8,12},{12,8},{1,5},{5,1},{9,13},{13,9},{2,6},{6,2},{1... | collective-permute-start | bytes 835592 | tf_op jit(solution)/shard_map/ppermute | solution.py:1028
  5.4 0.7 collective-permute-start.5
  6.1 1.4 %gather_tokens.3 = (bf16[34,32,128]{2,1,0:T(8,128)(2,1)S(1)}, bf16[33,32,128]{2,1,0:T(8,128)(2,1)S(1)}, bf16[128,2048]{1,0:T(8,128)(2,1)S(1)}, s32[8,128]{1,0:T(8,128)S(1)}) custom-call(bf16[2,32,4096]{2,1,0:T(8,128)(2,1)} %refs_1_.6, bf16[2,32,4096]{2,1,0:T(8,128)(2,1)} %refs_2_.5, bf16[8,4,256]{2,1,0:T(4,128)(2,1)} %refs_2_.4, bf16[8,4,256]{2,1,0:T(4,128)(2,1)} %refs_3_.3, ...), custom_call_target="tpu_custom_call" | custom-call | tf_op jit(solution)/shard_map/gather_tokens/pallas_call | solution.py:51
  7.5 4.4 %collective-permute-start.1 = (bf16[33,32,128]{2,1,0:T(8,128)(2,1)S(1)}, bf16[33,32,128]{2,1,0:T(8,128)(2,1)S(1)}, u32[]{:S(2)}, u32[]{:S(2)}) collective-permute-start(bf16[33,32,128]{2,1,0:T(8,128)(2,1)S(1)} %tie.5), channel_id=1, source_target_pairs={{0,4},{4,0},{8,12},{12,8},{1,5},{5,1},{9,13},{13,9},{2,6},{6,2},{1... | collective-permute-start | bytes 811016 | tf_op jit(solution)/shard_map/ppermute | solution.py:1033
  11.9 0.7 prepare.1
  12.6 2.5 %score.2 = (bf16[8,256,128]{2,1,0:T(8,128)(2,1)S(1)}, bf16[512,32]{1,0:T(8,128)(2,1)S(1)}, f32[128,128]{1,0:T(8,128)S(1)}, f32[128,128]{1,0:T(8,128)S(1)}) custom-call(bf16[256,2048]{1,0:T(8,128)(2,1)S(1)} %get-tuple-element.54.refs_0_, f32[256,128]{1,0:T(8,128)S(1)} %get-tuple-element.55.refs_1_, f32[128,256]{1,0:T(8,128)S(1)} %get-tuple-element.56.refs_2_, ...), custom_call_target="tpu_custom_call" | custom-call | tf_op jit(solution)/shard_map/score/pallas_call | solution.py:51
  15.1 0.7 value.4.refs_7_
  15.8 0.0 collective-permute-done.refs_3_.refs_9_.refs_0_
  15.8 2.5 %score.3 = (bf16[8,256,128]{2,1,0:T(8,128)(2,1)S(1)}, bf16[512,32]{1,0:T(8,128)(2,1)S(1)}, f32[128,128]{1,0:T(8,128)S(1)}, f32[128,128]{1,0:T(8,128)S(1)}) custom-call(bf16[256,2048]{1,0:T(8,128)(2,1)S(1)} %get-tuple-element.50.refs_0_, f32[256,128]{1,0:T(8,128)S(1)} %get-tuple-element.51.refs_1_, f32[128,256]{1,0:T(8,128)S(1)} %get-tuple-element.52.refs_2_, ...), custom_call_target="tpu_custom_call" | custom-call | flops 17179869184 | tf_op jit(solution)/shard_map/score/pallas_call | solution.py:51
  18.3 0.0 collective-permute-done.1.refs_3_.refs_1_
  18.3 0.8 value.5.refs_0_.refs_2_.refs_1_
  19.1 2.3 %collective-permute-start.2 = (bf16[128,1152]{1,0:T(8,128)(2,1)S(1)}, bf16[128,1152]{1,0:T(8,128)(2,1)S(1)}, u32[]{:S(2)}, u32[]{:S(2)}) collective-permute-start(bf16[128,1152]{1,0:T(8,128)(2,1)S(1)} %value.5.refs_0_.refs_2_.refs_1_), channel_id=1, source_target_pairs={{0,8},{4,12},{8,0},{12,4},{1,9},{5,13},{9,1},{13,5},{2,10},{6,14},... | collective-permute-start | bytes 884744 | tf_op jit(solution)/shard_map/ppermute | solution.py:1068
  21.4 0.7 value.6.refs_7_
  22.1 0.7 value.7.refs_1_.refs_0_.refs_3_
  22.8 1.7 %place_pages.1 = (bf16[2,2,16,4096]{3,2,1,0:T(8,128)(2,1)S(1)}, bf16[2,16,4096]{2,1,0:T(8,128)(2,1)S(1)}, bf16[2,2,16,4096]{3,2,1,0:T(8,128)(2,1)S(1)}) custom-call(s32[2,32]{1,0:T(2,128)} %refs_0_.8, bf16[2,32,4096]{2,1,0:T(8,128)(2,1)} %refs_1_.6, bf16[2,32,4096]{2,1,0:T(8,128)(2,1)} %refs_2_.5, bf16[128,1024]{1,0:T(8,128)(2,1)S(1)} %value.7.refs_1_.refs_0_.refs_3_), custom_call_target="tpu_custom_call" | custom-call | tf_op jit(solution)/shard_map/place_pages/pallas_call | solution.py:51
  24.6 5.9 %fetch.2 = (bf16[2048,4096]{1,0:T(8,128)(2,1)S(1)}, f32[8,128]{1,0:T(8,128)S(1)}) custom-call(bf16[4096,4096]{1,0:T(8,128)(2,1)} %refs_1_.7, bf16[128,1024]{1,0:T(8,128)(2,1)S(1)} %value.7.refs_1_.refs_0_.refs_3_), custom_call_target="tpu_custom_call" | custom-call | tf_op jit(solution)/shard_map/fetch/pallas_call | solution.py:51
  30.5 3.5 %fetch.3 = (bf16[1024,4096]{1,0:T(8,128)(2,1)S(1)}, f32[8,128]{1,0:T(8,128)S(1)}) custom-call(bf16[4096,4096]{1,0:T(8,128)(2,1)} %refs_1_.7, f32[8,128]{1,0:T(8,128)S(1)} %get-tuple-element.68.refs_1_), custom_call_target="tpu_custom_call" | custom-call | tf_op jit(solution)/shard_map/fetch/pallas_call | solution.py:51
  34.1 1.7 %collective-permute-start.4 = (bf16[2,16,4096]{2,1,0:T(8,128)(2,1)S(1)}, bf16[2,16,4096]{2,1,0:T(8,128)(2,1)S(1)}, u32[]{:S(2)}, u32[]{:S(2)}) collective-permute-start(bf16[2,16,4096]{2,1,0:T(8,128)(2,1)S(1)} %tie.7), channel_id=1, source_target_pairs={{0,4},{4,0},{8,12},{12,8},{1,5},{5,1},{9,13},{13,9},{2,6},{6,2},{1... | collective-permute-start | bytes 786440 | tf_op jit(solution)/shard_map/ppermute | solution.py:1069
  35.7 0.3 collective-permute-start.3
  36.0 0.0 collective-permute-done.2.refs_1_.refs_3_.refs_2_
  36.0 0.5 combine.2.refs_0_
  36.5 3.9 %project.4.refs_5_.refs_4_.refs_3_.refs_1_ = f32[128,4096]{1,0:T(8,128)S(1)} custom-call(bf16[128,1024]{1,0:T(8,128)(2,1)S(1)} %combine.2.refs_0_, bf16[4096,4096]{1,0:T(8,128)(2,1)} %refs_1_.7), custom_call_target="tpu_custom_call" | custom-call | tf_op jit(solution)/shard_map/project/pallas_call | solution.py:51
  40.4 0.9 %collective-permute-start.7 = (bf16[128,1024]{1,0:T(8,128)(2,1)S(1)}, bf16[128,1024]{1,0:T(8,128)(2,1)S(1)}, u32[]{:S(2)}, u32[]{:S(2)}) collective-permute-start(bf16[128,1024]{1,0:T(8,128)(2,1)S(1)} %combine.2.refs_0_), channel_id=1, source_target_pairs={{0,4},{4,0},{8,12},{12,8},{1,5},{5,1},{9,13},{13,9},{2,6},{6,2},{1... | collective-permute-start | bytes 786440 | tf_op jit(solution)/shard_map/ppermute | solution.py:1072
  41.3 0.0 collective-permute-done.5.refs_6_.refs_3_
  41.3 7.6 %collective-permute-done.4.refs_4_.refs_2_ = bf16[2,16,4096]{2,1,0:T(8,128)(2,1)S(1)} collective-permute-done((bf16[2,16,4096]{2,1,0:T(8,128)(2,1)S(1)}, bf16[2,16,4096]{2,1,0:T(8,128)(2,1)S(1)}, u32[]{:S(2)}, u32[]{:S(2)}) %collective-permute-start.4) | collective-permute-done | bytes 262176 | tf_op jit(solution)/shard_map/ppermute | solution.py:1069
  48.8 0.0 collective-permute-done.3.refs_3_
  48.9 0.5 combine.3.refs_0_
  49.3 0.9 %collective-permute-start.6 = (bf16[128,1024]{1,0:T(8,128)(2,1)S(1)}, bf16[128,1024]{1,0:T(8,128)(2,1)S(1)}, u32[]{:S(2)}, u32[]{:S(2)}) collective-permute-start(bf16[128,1024]{1,0:T(8,128)(2,1)S(1)} %combine.3.refs_0_), channel_id=1, source_target_pairs={{0,4},{4,0},{8,12},{12,8},{1,5},{5,1},{9,13},{13,9},{2,6},{6,2},{1... | collective-permute-start | bytes 786440 | tf_op jit(solution)/shard_map/ppermute | solution.py:1077
  50.2 1.9 %collective-permute-start.12 = (bf16[2,2,16,4096]{3,2,1,0:T(8,128)(2,1)S(1)}, bf16[2,2,16,4096]{3,2,1,0:T(8,128)(2,1)S(1)}, u32[]{:S(2)}, u32[]{:S(2)}) collective-permute-start(bf16[2,2,16,4096]{3,2,1,0:T(8,128)(2,1)S(1)} %tie.8), channel_id=1, source_target_pairs={{0,8},{4,12},{8,0},{12,4},{1,9},{5,13},{9,1},{13,5},{2,10},{6,14},... | collective-permute-start | bytes 1572872 | tf_op jit(solution)/shard_map/ppermute | solution.py:1074
  52.1 3.7 %collective-permute-start.13 = (bf16[2,2,16,4096]{3,2,1,0:T(8,128)(2,1)S(1)}, bf16[2,2,16,4096]{3,2,1,0:T(8,128)(2,1)S(1)}, u32[]{:S(2)}, u32[]{:S(2)}) collective-permute-start(bf16[2,2,16,4096]{3,2,1,0:T(8,128)(2,1)S(1)} %tie.9), channel_id=1, source_target_pairs={{0,12},{12,0},{1,13},{13,1},{2,14},{14,2},{3,15},{15,3},{16,28},{2... | collective-permute-start | bytes 1572872 | tf_op jit(solution)/shard_map/ppermute | solution.py:1075
  55.9 0.4 place_near.1.refs_1_
  56.2 1.1 %settle.2 = (bf16[2,64,4096]{2,1,0:T(8,128)(2,1)}, bf16[2,64,4096]{2,1,0:T(8,128)(2,1)}, f32[8,128]{1,0:T(8,128)S(1)}) custom-call(bf16[2,2,16,4096]{3,2,1,0:T(8,128)(2,1)S(1)} %get-tuple-element.73.refs_0_, bf16[2,16,4096]{2,1,0:T(8,128)(2,1)S(1)} %place_near.1.refs_1_, bf16[2,16,4096]{2,1,0:T(8,128)(2,1)S(1)} %collective-permute-done.4.refs_4_.refs_2_, ...), custom_call_target="tpu_custom_call" | custom-call | tf_op jit(solution)/shard_map/settle/pallas_call | solution.py:51
  57.4 5.8 %collective-permute-done.7.refs_1_ = bf16[128,1024]{1,0:T(8,128)(2,1)S(1)} collective-permute-done((bf16[128,1024]{1,0:T(8,128)(2,1)S(1)}, bf16[128,1024]{1,0:T(8,128)(2,1)S(1)}, u32[]{:S(2)}, u32[]{:S(2)}) %collective-permute-start.7) | collective-permute-done | bytes 262176 | tf_op jit(solution)/shard_map/ppermute | solution.py:1072
  63.1 2.4 %project.5.refs_2_ = f32[128,4096]{1,0:T(8,128)S(1)} custom-call(bf16[128,1024]{1,0:T(8,128)(2,1)S(1)} %combine.3.refs_0_, bf16[128,1024]{1,0:T(8,128)(2,1)S(1)} %collective-permute-done.7.refs_1_, bf16[2048,4096]{1,0:T(8,128)(2,1)S(1)} %get-tuple-element.72.refs_2_, f32[128,4096]{1,0:T(8,128)S(1)} %project.4.refs_5_.refs_4_.refs_3_.refs_1_, ...), custom_call_target="tpu_custom_call" | custom-call | tf_op jit(solution)/shard_map/project/pallas_call | solution.py:51
  65.5 1.0 %collective-permute-done.6.refs_0_ = bf16[128,1024]{1,0:T(8,128)(2,1)S(1)} collective-permute-done((bf16[128,1024]{1,0:T(8,128)(2,1)S(1)}, bf16[128,1024]{1,0:T(8,128)(2,1)S(1)}, u32[]{:S(2)}, u32[]{:S(2)}) %collective-permute-start.6) | collective-permute-done | bytes 262176 | tf_op jit(solution)/shard_map/ppermute | solution.py:1077
  66.5 0.8 project.7
  67.3 0.1 collective-permute-start.10
  67.4 0.8 project.6
  68.2 0.6 collective-permute-start.8
  68.8 0.2 collective-permute-done.10.refs_1_
  69.0 1.5 %collective-permute-start.11 = (bf16[32,2048]{1,0:T(8,128)(2,1)S(1)}, bf16[32,2048]{1,0:T(8,128)(2,1)S(1)}, u32[]{:S(2)}, u32[]{:S(2)}) collective-permute-start(bf16[32,2048]{1,0:T(8,128)(2,1)S(1)} %get-tuple-element.82), channel_id=1, source_target_pairs={{0,2},{1,3},{2,0},{3,1},{4,6},{5,7},{6,4},{7,5},{8,10},{9,11},{10,... | collective-permute-start | bytes 393224 | tf_op jit(solution)/shard_map/ppermute | solution.py:968
  70.5 0.0 collective-permute-done.8.refs_1_
  70.5 0.1 add_core.2
  70.6 1.0 %collective-permute-start.9 = (bf16[32,2048]{1,0:T(8,128)(2,1)S(1)}, bf16[32,2048]{1,0:T(8,128)(2,1)S(1)}, u32[]{:S(2)}, u32[]{:S(2)}) collective-permute-start(bf16[32,2048]{1,0:T(8,128)(2,1)S(1)} %get-tuple-element.78), channel_id=1, source_target_pairs={{0,2},{1,3},{2,0},{3,1},{4,6},{5,7},{6,4},{7,5},{8,10},{9,11},{10,... | collective-permute-start | bytes 393224 | tf_op jit(solution)/shard_map/ppermute | solution.py:968
  71.6 1.4 %slot_rows.1 = s32[2,64]{1,0:T(2,128)} custom-call(s32[8,128]{1,0:T(8,128)S(1)} %get-tuple-element.48.refs_0_.refs_1_, bf16[128,1152]{1,0:T(8,128)(2,1)S(1)} %value.5.refs_0_.refs_2_.refs_1_, bf16[128,1152]{1,0:T(8,128)(2,1)S(1)} %collective-permute-done.2.refs_1_.refs_3_.refs_2_, f32[32,2048]{1,0:T(8,128)S(1)} %get-tuple-element.81.refs_2_.refs_3_), custom_call_target="tpu_custom_call" | custom-call | tf_op jit(solution)/shard_map/slot_rows/pallas_call | solution.py:51
  72.9 2.5 %collective-permute-done.11.refs_3_ = bf16[32,2048]{1,0:T(8,128)(2,1)S(1)} collective-permute-done((bf16[32,2048]{1,0:T(8,128)(2,1)S(1)}, bf16[32,2048]{1,0:T(8,128)(2,1)S(1)}, u32[]{:S(2)}, u32[]{:S(2)}) %collective-permute-start.11) | collective-permute-done | bytes 131104 | tf_op jit(solution)/shard_map/ppermute | solution.py:968
  75.4 2.0 %collective-permute-done.9.refs_1_ = bf16[32,2048]{1,0:T(8,128)(2,1)S(1)} collective-permute-done((bf16[32,2048]{1,0:T(8,128)(2,1)S(1)}, bf16[32,2048]{1,0:T(8,128)(2,1)S(1)}, u32[]{:S(2)}, u32[]{:S(2)}) %collective-permute-start.9) | collective-permute-done | bytes 131104 | tf_op jit(solution)/shard_map/ppermute | solution.py:968
  77.4 0.8 finish.1
  78.2 5.1 %collective-permute-done.12.refs_0_ = bf16[2,2,16,4096]{3,2,1,0:T(8,128)(2,1)S(1)} collective-permute-done((bf16[2,2,16,4096]{3,2,1,0:T(8,128)(2,1)S(1)}, bf16[2,2,16,4096]{3,2,1,0:T(8,128)(2,1)S(1)}, u32[]{:S(2)}, u32[]{:S(2)}) %collective-permute-start.12) | collective-permute-done | bytes 524320 | tf_op jit(solution)/shard_map/ppermute | solution.py:1074
  83.2 0.0 collective-permute-done.13.refs_1_
  83.2 1.6 %settle.3 = (bf16[2,64,4096]{2,1,0:T(8,128)(2,1)}, bf16[2,64,4096]{2,1,0:T(8,128)(2,1)}, f32[8,128]{1,0:T(8,128)}) custom-call(bf16[2,2,16,4096]{3,2,1,0:T(8,128)(2,1)S(1)} %collective-permute-done.12.refs_0_, bf16[2,2,16,4096]{3,2,1,0:T(8,128)(2,1)S(1)} %collective-permute-done.13.refs_1_, ...), custom_call_target="tpu_custom_call", output_to_operand_aliasing={{0}: (2, {}), {1}: (3, {})} | custom-call | tf_op jit(solution)/shard_map/settle/pallas_call | solution.py:51
  (6 shorter events, 0.1 us)
Async XLA Ops:
  2.3 13.5 %collective-permute-start = (bf16[34,32,128]{2,1,0:T(8,128)(2,1)S(1)}, bf16[34,32,128]{2,1,0:T(8,128)(2,1)S(1)}, u32[]{:S(2)}, u32[]{:S(2)}) collective-permute-start(bf16[34,32,128]{2,1,0:T(8,128)(2,1)S(1)} %get-tuple-element.53), channel_id=1, source_target_pairs={{0,4},{4,0},{8,12},{12,8},{1,5},{5,1},{9,13},{13,9},{2,6},{6,2},{1... | collective-permute-start | bytes 835592 | tf_op jit(solution)/shard_map/ppermute | solution.py:1028
  5.4 35.9 %collective-permute-start.5 = (bf16[2,2,16,4096]{3,2,1,0:T(8,128)(2,1)S(1)}, bf16[2,2,16,4096]{3,2,1,0:T(8,128)(2,1)S(1)}, u32[]{:S(2)}, u32[]{:S(2)}) collective-permute-start(bf16[2,2,16,4096]{3,2,1,0:T(8,128)(2,1)S(1)} %get-tuple-element.47.refs_7_.refs_0_), channel_id=1, source_target_pairs={{4,8},{8,4},{5,9},{9,5},{6,10},{10,6},{7,11},{11,7},{20,24},{24,20... | collective-permute-start | bytes 1572872 | tf_op jit(solution)/shard_map/ppermute | solution.py:1029
  7.5 10.8 %collective-permute-start.1 = (bf16[33,32,128]{2,1,0:T(8,128)(2,1)S(1)}, bf16[33,32,128]{2,1,0:T(8,128)(2,1)S(1)}, u32[]{:S(2)}, u32[]{:S(2)}) collective-permute-start(bf16[33,32,128]{2,1,0:T(8,128)(2,1)S(1)} %tie.5), channel_id=1, source_target_pairs={{0,4},{4,0},{8,12},{12,8},{1,5},{5,1},{9,13},{13,9},{2,6},{6,2},{1... | collective-permute-start | bytes 811016 | tf_op jit(solution)/shard_map/ppermute | solution.py:1033
  19.1 16.9 %collective-permute-start.2 = (bf16[128,1152]{1,0:T(8,128)(2,1)S(1)}, bf16[128,1152]{1,0:T(8,128)(2,1)S(1)}, u32[]{:S(2)}, u32[]{:S(2)}) collective-permute-start(bf16[128,1152]{1,0:T(8,128)(2,1)S(1)} %value.5.refs_0_.refs_2_.refs_1_), channel_id=1, source_target_pairs={{0,8},{4,12},{8,0},{12,4},{1,9},{5,13},{9,1},{13,5},{2,10},{6,14},... | collective-permute-start | bytes 884744 | tf_op jit(solution)/shard_map/ppermute | solution.py:1068
  34.1 14.8 %collective-permute-start.4 = (bf16[2,16,4096]{2,1,0:T(8,128)(2,1)S(1)}, bf16[2,16,4096]{2,1,0:T(8,128)(2,1)S(1)}, u32[]{:S(2)}, u32[]{:S(2)}) collective-permute-start(bf16[2,16,4096]{2,1,0:T(8,128)(2,1)S(1)} %tie.7), channel_id=1, source_target_pairs={{0,4},{4,0},{8,12},{12,8},{1,5},{5,1},{9,13},{13,9},{2,6},{6,2},{1... | collective-permute-start | bytes 786440 | tf_op jit(solution)/shard_map/ppermute | solution.py:1069
  35.7 13.1 %collective-permute-start.3 = (bf16[128,1024]{1,0:T(8,128)(2,1)S(1)}, bf16[128,1024]{1,0:T(8,128)(2,1)S(1)}, u32[]{:S(2)}, u32[]{:S(2)}) collective-permute-start(bf16[128,1024]{1,0:T(8,128)(2,1)S(1)} %tie.6.refs_2_), channel_id=1, source_target_pairs={{0,8},{4,12},{8,0},{12,4},{1,9},{5,13},{9,1},{13,5},{2,10},{6,14},... | collective-permute-start | bytes 786440 | tf_op jit(solution)/shard_map/ppermute | solution.py:1068
  40.4 22.7 %collective-permute-start.7 = (bf16[128,1024]{1,0:T(8,128)(2,1)S(1)}, bf16[128,1024]{1,0:T(8,128)(2,1)S(1)}, u32[]{:S(2)}, u32[]{:S(2)}) collective-permute-start(bf16[128,1024]{1,0:T(8,128)(2,1)S(1)} %combine.2.refs_0_), channel_id=1, source_target_pairs={{0,4},{4,0},{8,12},{12,8},{1,5},{5,1},{9,13},{13,9},{2,6},{6,2},{1... | collective-permute-start | bytes 786440 | tf_op jit(solution)/shard_map/ppermute | solution.py:1072
  49.3 17.2 %collective-permute-start.6 = (bf16[128,1024]{1,0:T(8,128)(2,1)S(1)}, bf16[128,1024]{1,0:T(8,128)(2,1)S(1)}, u32[]{:S(2)}, u32[]{:S(2)}) collective-permute-start(bf16[128,1024]{1,0:T(8,128)(2,1)S(1)} %combine.3.refs_0_), channel_id=1, source_target_pairs={{0,4},{4,0},{8,12},{12,8},{1,5},{5,1},{9,13},{13,9},{2,6},{6,2},{1... | collective-permute-start | bytes 786440 | tf_op jit(solution)/shard_map/ppermute | solution.py:1077
  50.2 33.0 %collective-permute-start.12 = (bf16[2,2,16,4096]{3,2,1,0:T(8,128)(2,1)S(1)}, bf16[2,2,16,4096]{3,2,1,0:T(8,128)(2,1)S(1)}, u32[]{:S(2)}, u32[]{:S(2)}) collective-permute-start(bf16[2,2,16,4096]{3,2,1,0:T(8,128)(2,1)S(1)} %tie.8), channel_id=1, source_target_pairs={{0,8},{4,12},{8,0},{12,4},{1,9},{5,13},{9,1},{13,5},{2,10},{6,14},... | collective-permute-start | bytes 1572872 | tf_op jit(solution)/shard_map/ppermute | solution.py:1074
  52.1 31.1 %collective-permute-start.13 = (bf16[2,2,16,4096]{3,2,1,0:T(8,128)(2,1)S(1)}, bf16[2,2,16,4096]{3,2,1,0:T(8,128)(2,1)S(1)}, u32[]{:S(2)}, u32[]{:S(2)}) collective-permute-start(bf16[2,2,16,4096]{3,2,1,0:T(8,128)(2,1)S(1)} %tie.9), channel_id=1, source_target_pairs={{0,12},{12,0},{1,13},{13,1},{2,14},{14,2},{3,15},{15,3},{16,28},{2... | collective-permute-start | bytes 1572872 | tf_op jit(solution)/shard_map/ppermute | solution.py:1075
  67.3 1.6 %collective-permute-start.10 = (bf16[2,32,2048]{2,1,0:T(8,128)(2,1)S(1)}, bf16[2,32,2048]{2,1,0:T(8,128)(2,1)S(1)}, u32[]{:S(2)}, u32[]{:S(2)}) collective-permute-start(bf16[2,32,2048]{2,1,0:T(8,128)(2,1)S(1)} %get-tuple-element.80), channel_id=1, source_target_pairs={{0,1},{1,0},{2,3},{3,2},{4,5},{5,4},{6,7},{7,6},{8,9},{9,8},{10,11... | collective-permute-start | bytes 786440 | tf_op jit(solution)/shard_map/ppermute | solution.py:955
  68.2 2.3 %collective-permute-start.8 = (bf16[2,32,2048]{2,1,0:T(8,128)(2,1)S(1)}, bf16[2,32,2048]{2,1,0:T(8,128)(2,1)S(1)}, u32[]{:S(2)}, u32[]{:S(2)}) collective-permute-start(bf16[2,32,2048]{2,1,0:T(8,128)(2,1)S(1)} %get-tuple-element.76), channel_id=1, source_target_pairs={{0,1},{1,0},{2,3},{3,2},{4,5},{5,4},{6,7},{7,6},{8,9},{9,8},{10,11... | collective-permute-start | bytes 786440 | tf_op jit(solution)/shard_map/ppermute | solution.py:955
  69.0 6.4 %collective-permute-start.11 = (bf16[32,2048]{1,0:T(8,128)(2,1)S(1)}, bf16[32,2048]{1,0:T(8,128)(2,1)S(1)}, u32[]{:S(2)}, u32[]{:S(2)}) collective-permute-start(bf16[32,2048]{1,0:T(8,128)(2,1)S(1)} %get-tuple-element.82), channel_id=1, source_target_pairs={{0,2},{1,3},{2,0},{3,1},{4,6},{5,7},{6,4},{7,5},{8,10},{9,11},{10,... | collective-permute-start | bytes 393224 | tf_op jit(solution)/shard_map/ppermute | solution.py:968
  70.6 6.8 %collective-permute-start.9 = (bf16[32,2048]{1,0:T(8,128)(2,1)S(1)}, bf16[32,2048]{1,0:T(8,128)(2,1)S(1)}, u32[]{:S(2)}, u32[]{:S(2)}) collective-permute-start(bf16[32,2048]{1,0:T(8,128)(2,1)S(1)} %get-tuple-element.78), channel_id=1, source_target_pairs={{0,2},{1,3},{2,0},{3,1},{4,6},{5,7},{6,4},{7,5},{8,10},{9,11},{10,... | collective-permute-start | bytes 393224 | tf_op jit(solution)/shard_map/ppermute | solution.py:968

commit v6 on v5

--- a/solution.py
+++ b/solution.py
@@ -214,19 +214,17 @@
         first = pl.multiple_of((me ^ distance) * cap, cap)
         copies = []
         for index, target in enumerate((key_ref, value_ref)):
-            for head in range(head_count if other is None else 1):
-                source = parts[place].at[index]
-                if other is None:
-                    source = source.at[head]
-                else:
-                    head = lax.rem(me + other, head_count)
-                copies.append(
-                    pltpu.make_async_copy(
-                        source,
-                        target.at[head, pl.ds(first, cap)],
-                        arrived.at[place * 2 * head_count + len(copies)],
-                    )
+            if other is None:
+                slots = target.at[:, pl.ds(first, cap)]
+            else:
+                slots = target.at[lax.rem(me + other, head_count), pl.ds(first, cap)]
+            copies.append(
+                pltpu.make_async_copy(
+                    parts[place].at[index],
+                    slots,
+                    arrived.at[place * 2 * head_count + len(copies)],
                 )
+            )
         return copies
 
     def move(place, action):

time: 85.2 us -> 85.2 us (level)
  no operation moved by 1% of the time
where the time goes in v6:
time: 85.2 us; the launch traced here: 85 us
  Pallas kernels  36.9 us (43%)
  waiting for transfers between devices  24.1 us (28%)
  starting transfers between devices  23 us (27%)
  between operations  1.01 us (1%)
    pallas_call x30, Pallas kernels, call(): pl.pallas_call(without_extra, in_specs=list(in_specs) + [anywhere()] * ex...  36.9 us
    ppermute x1, waiting for transfers between devices, body(): got_near = lax.ppermute(tie(send_near, held_done), 'tp', flip(tp_size, 1))  7.59 us
    ppermute x1, waiting for transfers between devices, body(): near_first = lax.ppermute(first_part, 'tp', flip(tp_size, 1))  5.77 us
    ppermute x1, waiting for transfers between devices, body(): got_far = lax.ppermute(tie(send_far, total), 'tp', flip(tp_size, 2))  5.06 us
    ppermute x2, waiting for transfers between devices, sum_heads(): lax.ppermute(part, 'kv', flip(kv_size, 2 * step))  4.47 us
    ppermute x1, starting transfers between devices, body(): near_values = lax.ppermute(tie(values, bounds), 'tp', flip(tp_size, 1))  4.44 us
    ppermute x1, starting transfers between devices, body(): got_outer = lax.ppermute(tie(send_last, total), 'tp', [(0, 3), (3, 0)])  3.73 us
    ppermute x1, starting transfers between devices, body(): near_keys = lax.ppermute(keys, 'tp', flip(tp_size, 1))  3.09 us
  transfers between devices with their start and end apart: 14, of which 7 were waited for; matrix products, arithmetic and copies ran while one was open for 0% of the time, Pallas kernels for 40%

profile of v6, /device:TPU:0, one launch (start us, length us, event | category | flops | bytes accessed | tf_op | source)
XLA Modules:
  0.0 85.0 jit_solution(3541782664716578821)
XLA Ops:
  0.6 1.7 %gather_tokens.2 = (bf16[34,32,128]{2,1,0:T(8,128)(2,1)S(1)}, bf16[33,32,128]{2,1,0:T(8,128)(2,1)S(1)}, bf16[2,2,16,4096]{3,2,1,0:T(8,128)(2,1)S(1)}) custom-call(bf16[2,32,4096]{2,1,0:T(8,128)(2,1)} %refs_1_.6, bf16[2,32,4096]{2,1,0:T(8,128)(2,1)} %refs_2_.5, bf16[8,4,256]{2,1,0:T(4,128)(2,1)} %refs_2_.4, bf16[8,4,256]{2,1,0:T(4,128)(2,1)} %refs_3_.3, ...), custom_call_target="tpu_custom_call" | custom-call | tf_op jit(solution)/shard_map/gather_tokens/pallas_call | solution.py:51
  2.3 3.1 %collective-permute-start = (bf16[34,32,128]{2,1,0:T(8,128)(2,1)S(1)}, bf16[34,32,128]{2,1,0:T(8,128)(2,1)S(1)}, u32[]{:S(2)}, u32[]{:S(2)}) collective-permute-start(bf16[34,32,128]{2,1,0:T(8,128)(2,1)S(1)} %get-tuple-element.53), channel_id=1, source_target_pairs={{0,4},{4,0},{8,12},{12,8},{1,5},{5,1},{9,13},{13,9},{2,6},{6,2},{1... | collective-permute-start | bytes 835592 | tf_op jit(solution)/shard_map/ppermute | solution.py:1026
  5.4 0.7 collective-permute-start.5
  6.1 1.4 %gather_tokens.3 = (bf16[34,32,128]{2,1,0:T(8,128)(2,1)S(1)}, bf16[33,32,128]{2,1,0:T(8,128)(2,1)S(1)}, bf16[128,2048]{1,0:T(8,128)(2,1)S(1)}, s32[8,128]{1,0:T(8,128)S(1)}) custom-call(bf16[2,32,4096]{2,1,0:T(8,128)(2,1)} %refs_1_.6, bf16[2,32,4096]{2,1,0:T(8,128)(2,1)} %refs_2_.5, bf16[8,4,256]{2,1,0:T(4,128)(2,1)} %refs_2_.4, bf16[8,4,256]{2,1,0:T(4,128)(2,1)} %refs_3_.3, ...), custom_call_target="tpu_custom_call" | custom-call | tf_op jit(solution)/shard_map/gather_tokens/pallas_call | solution.py:51
  7.5 4.4 %collective-permute-start.1 = (bf16[33,32,128]{2,1,0:T(8,128)(2,1)S(1)}, bf16[33,32,128]{2,1,0:T(8,128)(2,1)S(1)}, u32[]{:S(2)}, u32[]{:S(2)}) collective-permute-start(bf16[33,32,128]{2,1,0:T(8,128)(2,1)S(1)} %tie.5), channel_id=1, source_target_pairs={{0,4},{4,0},{8,12},{12,8},{1,5},{5,1},{9,13},{13,9},{2,6},{6,2},{1... | collective-permute-start | bytes 811016 | tf_op jit(solution)/shard_map/ppermute | solution.py:1031
  11.9 0.7 prepare.1
  12.6 2.5 %score.2 = (bf16[8,256,128]{2,1,0:T(8,128)(2,1)S(1)}, bf16[512,32]{1,0:T(8,128)(2,1)S(1)}, f32[128,128]{1,0:T(8,128)S(1)}, f32[128,128]{1,0:T(8,128)S(1)}) custom-call(bf16[256,2048]{1,0:T(8,128)(2,1)S(1)} %get-tuple-element.54.refs_0_, f32[256,128]{1,0:T(8,128)S(1)} %get-tuple-element.55.refs_1_, f32[128,256]{1,0:T(8,128)S(1)} %get-tuple-element.56.refs_2_, ...), custom_call_target="tpu_custom_call" | custom-call | tf_op jit(solution)/shard_map/score/pallas_call | solution.py:51
  15.1 0.7 value.4.refs_7_
  15.8 0.0 collective-permute-done.refs_3_.refs_9_.refs_0_
  15.8 2.5 %score.3 = (bf16[8,256,128]{2,1,0:T(8,128)(2,1)S(1)}, bf16[512,32]{1,0:T(8,128)(2,1)S(1)}, f32[128,128]{1,0:T(8,128)S(1)}, f32[128,128]{1,0:T(8,128)S(1)}) custom-call(bf16[256,2048]{1,0:T(8,128)(2,1)S(1)} %get-tuple-element.50.refs_0_, f32[256,128]{1,0:T(8,128)S(1)} %get-tuple-element.51.refs_1_, f32[128,256]{1,0:T(8,128)S(1)} %get-tuple-element.52.refs_2_, ...), custom_call_target="tpu_custom_call" | custom-call | flops 17179869184 | tf_op jit(solution)/shard_map/score/pallas_call | solution.py:51
  18.3 0.0 collective-permute-done.1.refs_3_.refs_1_
  18.3 0.8 value.5.refs_0_.refs_2_.refs_1_
  19.1 2.3 %collective-permute-start.2 = (bf16[128,1152]{1,0:T(8,128)(2,1)S(1)}, bf16[128,1152]{1,0:T(8,128)(2,1)S(1)}, u32[]{:S(2)}, u32[]{:S(2)}) collective-permute-start(bf16[128,1152]{1,0:T(8,128)(2,1)S(1)} %value.5.refs_0_.refs_2_.refs_1_), channel_id=1, source_target_pairs={{0,8},{4,12},{8,0},{12,4},{1,9},{5,13},{9,1},{13,5},{2,10},{6,14},... | collective-permute-start | bytes 884744 | tf_op jit(solution)/shard_map/ppermute | solution.py:1066
  21.4 0.7 value.6.refs_7_
  22.1 0.7 value.7.refs_1_.refs_0_.refs_3_
  22.8 1.7 %place_pages.1 = (bf16[2,2,16,4096]{3,2,1,0:T(8,128)(2,1)S(1)}, bf16[2,16,4096]{2,1,0:T(8,128)(2,1)S(1)}, bf16[2,2,16,4096]{3,2,1,0:T(8,128)(2,1)S(1)}) custom-call(s32[2,32]{1,0:T(2,128)} %refs_0_.8, bf16[2,32,4096]{2,1,0:T(8,128)(2,1)} %refs_1_.6, bf16[2,32,4096]{2,1,0:T(8,128)(2,1)} %refs_2_.5, bf16[128,1024]{1,0:T(8,128)(2,1)S(1)} %value.7.refs_1_.refs_0_.refs_3_), custom_call_target="tpu_custom_call" | custom-call | tf_op jit(solution)/shard_map/place_pages/pallas_call | solution.py:51
  24.6 5.9 %fetch.2 = (bf16[2048,4096]{1,0:T(8,128)(2,1)S(1)}, f32[8,128]{1,0:T(8,128)S(1)}) custom-call(bf16[4096,4096]{1,0:T(8,128)(2,1)} %refs_1_.7, bf16[128,1024]{1,0:T(8,128)(2,1)S(1)} %value.7.refs_1_.refs_0_.refs_3_), custom_call_target="tpu_custom_call" | custom-call | tf_op jit(solution)/shard_map/fetch/pallas_call | solution.py:51
  30.5 3.5 %fetch.3 = (bf16[1024,4096]{1,0:T(8,128)(2,1)S(1)}, f32[8,128]{1,0:T(8,128)S(1)}) custom-call(bf16[4096,4096]{1,0:T(8,128)(2,1)} %refs_1_.7, f32[8,128]{1,0:T(8,128)S(1)} %get-tuple-element.68.refs_1_), custom_call_target="tpu_custom_call" | custom-call | tf_op jit(solution)/shard_map/fetch/pallas_call | solution.py:51
  34.1 1.7 %collective-permute-start.4 = (bf16[2,16,4096]{2,1,0:T(8,128)(2,1)S(1)}, bf16[2,16,4096]{2,1,0:T(8,128)(2,1)S(1)}, u32[]{:S(2)}, u32[]{:S(2)}) collective-permute-start(bf16[2,16,4096]{2,1,0:T(8,128)(2,1)S(1)} %tie.7), channel_id=1, source_target_pairs={{0,4},{4,0},{8,12},{12,8},{1,5},{5,1},{9,13},{13,9},{2,6},{6,2},{1... | collective-permute-start | bytes 786440 | tf_op jit(solution)/shard_map/ppermute | solution.py:1067
  35.7 0.3 collective-permute-start.3
  36.0 0.0 collective-permute-done.2.refs_1_.refs_3_.refs_2_
  36.0 0.5 combine.2.refs_0_
  36.5 3.9 %project.4.refs_5_.refs_4_.refs_3_.refs_1_ = f32[128,4096]{1,0:T(8,128)S(1)} custom-call(bf16[128,1024]{1,0:T(8,128)(2,1)S(1)} %combine.2.refs_0_, bf16[4096,4096]{1,0:T(8,128)(2,1)} %refs_1_.7), custom_call_target="tpu_custom_call" | custom-call | tf_op jit(solution)/shard_map/project/pallas_call | solution.py:51
  40.4 0.9 %collective-permute-start.7 = (bf16[128,1024]{1,0:T(8,128)(2,1)S(1)}, bf16[128,1024]{1,0:T(8,128)(2,1)S(1)}, u32[]{:S(2)}, u32[]{:S(2)}) collective-permute-start(bf16[128,1024]{1,0:T(8,128)(2,1)S(1)} %combine.2.refs_0_), channel_id=1, source_target_pairs={{0,4},{4,0},{8,12},{12,8},{1,5},{5,1},{9,13},{13,9},{2,6},{6,2},{1... | collective-permute-start | bytes 786440 | tf_op jit(solution)/shard_map/ppermute | solution.py:1070
  41.3 0.0 collective-permute-done.5.refs_6_.refs_3_
  41.3 7.6 %collective-permute-done.4.refs_4_.refs_2_ = bf16[2,16,4096]{2,1,0:T(8,128)(2,1)S(1)} collective-permute-done((bf16[2,16,4096]{2,1,0:T(8,128)(2,1)S(1)}, bf16[2,16,4096]{2,1,0:T(8,128)(2,1)S(1)}, u32[]{:S(2)}, u32[]{:S(2)}) %collective-permute-start.4) | collective-permute-done | bytes 262176 | tf_op jit(solution)/shard_map/ppermute | solution.py:1067
  48.8 0.0 collective-permute-done.3.refs_3_
  48.9 0.5 combine.3.refs_0_
  49.3 0.9 %collective-permute-start.6 = (bf16[128,1024]{1,0:T(8,128)(2,1)S(1)}, bf16[128,1024]{1,0:T(8,128)(2,1)S(1)}, u32[]{:S(2)}, u32[]{:S(2)}) collective-permute-start(bf16[128,1024]{1,0:T(8,128)(2,1)S(1)} %combine.3.refs_0_), channel_id=1, source_target_pairs={{0,4},{4,0},{8,12},{12,8},{1,5},{5,1},{9,13},{13,9},{2,6},{6,2},{1... | collective-permute-start | bytes 786440 | tf_op jit(solution)/shard_map/ppermute | solution.py:1075
  50.2 1.9 %collective-permute-start.12 = (bf16[2,2,16,4096]{3,2,1,0:T(8,128)(2,1)S(1)}, bf16[2,2,16,4096]{3,2,1,0:T(8,128)(2,1)S(1)}, u32[]{:S(2)}, u32[]{:S(2)}) collective-permute-start(bf16[2,2,16,4096]{3,2,1,0:T(8,128)(2,1)S(1)} %tie.8), channel_id=1, source_target_pairs={{0,8},{4,12},{8,0},{12,4},{1,9},{5,13},{9,1},{13,5},{2,10},{6,14},... | collective-permute-start | bytes 1572872 | tf_op jit(solution)/shard_map/ppermute | solution.py:1072
  52.1 3.7 %collective-permute-start.13 = (bf16[2,2,16,4096]{3,2,1,0:T(8,128)(2,1)S(1)}, bf16[2,2,16,4096]{3,2,1,0:T(8,128)(2,1)S(1)}, u32[]{:S(2)}, u32[]{:S(2)}) collective-permute-start(bf16[2,2,16,4096]{3,2,1,0:T(8,128)(2,1)S(1)} %tie.9), channel_id=1, source_target_pairs={{0,12},{12,0},{1,13},{13,1},{2,14},{14,2},{3,15},{15,3},{16,28},{2... | collective-permute-start | bytes 1572872 | tf_op jit(solution)/shard_map/ppermute | solution.py:1073
  55.9 0.4 place_near.1.refs_1_
  56.2 1.1 %settle.2 = (bf16[2,64,4096]{2,1,0:T(8,128)(2,1)}, bf16[2,64,4096]{2,1,0:T(8,128)(2,1)}, f32[8,128]{1,0:T(8,128)S(1)}) custom-call(bf16[2,2,16,4096]{3,2,1,0:T(8,128)(2,1)S(1)} %get-tuple-element.73.refs_0_, bf16[2,16,4096]{2,1,0:T(8,128)(2,1)S(1)} %place_near.1.refs_1_, bf16[2,16,4096]{2,1,0:T(8,128)(2,1)S(1)} %collective-permute-done.4.refs_4_.refs_2_, ...), custom_call_target="tpu_custom_call" | custom-call | tf_op jit(solution)/shard_map/settle/pallas_call | solution.py:51
  57.4 5.8 %collective-permute-done.7.refs_1_ = bf16[128,1024]{1,0:T(8,128)(2,1)S(1)} collective-permute-done((bf16[128,1024]{1,0:T(8,128)(2,1)S(1)}, bf16[128,1024]{1,0:T(8,128)(2,1)S(1)}, u32[]{:S(2)}, u32[]{:S(2)}) %collective-permute-start.7) | collective-permute-done | bytes 262176 | tf_op jit(solution)/shard_map/ppermute | solution.py:1070
  63.1 2.4 %project.5.refs_2_ = f32[128,4096]{1,0:T(8,128)S(1)} custom-call(bf16[128,1024]{1,0:T(8,128)(2,1)S(1)} %combine.3.refs_0_, bf16[128,1024]{1,0:T(8,128)(2,1)S(1)} %collective-permute-done.7.refs_1_, bf16[2048,4096]{1,0:T(8,128)(2,1)S(1)} %get-tuple-element.72.refs_2_, f32[128,4096]{1,0:T(8,128)S(1)} %project.4.refs_5_.refs_4_.refs_3_.refs_1_, ...), custom_call_target="tpu_custom_call" | custom-call | tf_op jit(solution)/shard_map/project/pallas_call | solution.py:51
  65.5 1.0 %collective-permute-done.6.refs_0_ = bf16[128,1024]{1,0:T(8,128)(2,1)S(1)} collective-permute-done((bf16[128,1024]{1,0:T(8,128)(2,1)S(1)}, bf16[128,1024]{1,0:T(8,128)(2,1)S(1)}, u32[]{:S(2)}, u32[]{:S(2)}) %collective-permute-start.6) | collective-permute-done | bytes 262176 | tf_op jit(solution)/shard_map/ppermute | solution.py:1075
  66.5 0.8 project.7
  67.3 0.1 collective-permute-start.10
  67.4 0.8 project.6
  68.2 0.6 collective-permute-start.8
  68.8 0.2 collective-permute-done.10.refs_1_
  69.0 1.5 %collective-permute-start.11 = (bf16[32,2048]{1,0:T(8,128)(2,1)S(1)}, bf16[32,2048]{1,0:T(8,128)(2,1)S(1)}, u32[]{:S(2)}, u32[]{:S(2)}) collective-permute-start(bf16[32,2048]{1,0:T(8,128)(2,1)S(1)} %get-tuple-element.82), channel_id=1, source_target_pairs={{0,2},{1,3},{2,0},{3,1},{4,6},{5,7},{6,4},{7,5},{8,10},{9,11},{10,... | collective-permute-start | bytes 393224 | tf_op jit(solution)/shard_map/ppermute | solution.py:966
  70.5 0.0 collective-permute-done.8.refs_1_
  70.5 0.1 add_core.2
  70.6 1.0 %collective-permute-start.9 = (bf16[32,2048]{1,0:T(8,128)(2,1)S(1)}, bf16[32,2048]{1,0:T(8,128)(2,1)S(1)}, u32[]{:S(2)}, u32[]{:S(2)}) collective-permute-start(bf16[32,2048]{1,0:T(8,128)(2,1)S(1)} %get-tuple-element.78), channel_id=1, source_target_pairs={{0,2},{1,3},{2,0},{3,1},{4,6},{5,7},{6,4},{7,5},{8,10},{9,11},{10,... | collective-permute-start | bytes 393224 | tf_op jit(solution)/shard_map/ppermute | solution.py:966
  71.6 1.4 %slot_rows.1 = s32[2,64]{1,0:T(2,128)} custom-call(s32[8,128]{1,0:T(8,128)S(1)} %get-tuple-element.48.refs_0_.refs_1_, bf16[128,1152]{1,0:T(8,128)(2,1)S(1)} %value.5.refs_0_.refs_2_.refs_1_, bf16[128,1152]{1,0:T(8,128)(2,1)S(1)} %collective-permute-done.2.refs_1_.refs_3_.refs_2_, f32[32,2048]{1,0:T(8,128)S(1)} %get-tuple-element.81.refs_2_.refs_3_), custom_call_target="tpu_custom_call" | custom-call | tf_op jit(solution)/shard_map/slot_rows/pallas_call | solution.py:51
  72.9 2.5 %collective-permute-done.11.refs_3_ = bf16[32,2048]{1,0:T(8,128)(2,1)S(1)} collective-permute-done((bf16[32,2048]{1,0:T(8,128)(2,1)S(1)}, bf16[32,2048]{1,0:T(8,128)(2,1)S(1)}, u32[]{:S(2)}, u32[]{:S(2)}) %collective-permute-start.11) | collective-permute-done | bytes 131104 | tf_op jit(solution)/shard_map/ppermute | solution.py:966
  75.4 2.0 %collective-permute-done.9.refs_1_ = bf16[32,2048]{1,0:T(8,128)(2,1)S(1)} collective-permute-done((bf16[32,2048]{1,0:T(8,128)(2,1)S(1)}, bf16[32,2048]{1,0:T(8,128)(2,1)S(1)}, u32[]{:S(2)}, u32[]{:S(2)}) %collective-permute-start.9) | collective-permute-done | bytes 131104 | tf_op jit(solution)/shard_map/ppermute | solution.py:966
  77.4 0.8 finish.1
  78.2 5.1 %collective-permute-done.12.refs_0_ = bf16[2,2,16,4096]{3,2,1,0:T(8,128)(2,1)S(1)} collective-permute-done((bf16[2,2,16,4096]{3,2,1,0:T(8,128)(2,1)S(1)}, bf16[2,2,16,4096]{3,2,1,0:T(8,128)(2,1)S(1)}, u32[]{:S(2)}, u32[]{:S(2)}) %collective-permute-start.12) | collective-permute-done | bytes 524320 | tf_op jit(solution)/shard_map/ppermute | solution.py:1072
  83.2 0.0 collective-permute-done.13.refs_1_
  83.2 1.6 %settle.3 = (bf16[2,64,4096]{2,1,0:T(8,128)(2,1)}, bf16[2,64,4096]{2,1,0:T(8,128)(2,1)}, f32[8,128]{1,0:T(8,128)}) custom-call(bf16[2,2,16,4096]{3,2,1,0:T(8,128)(2,1)S(1)} %collective-permute-done.12.refs_0_, bf16[2,2,16,4096]{3,2,1,0:T(8,128)(2,1)S(1)} %collective-permute-done.13.refs_1_, ...), custom_call_target="tpu_custom_call", output_to_operand_aliasing={{0}: (2, {}), {1}: (3, {})} | custom-call | tf_op jit(solution)/shard_map/settle/pallas_call | solution.py:51
  (6 shorter events, 0.1 us)
Async XLA Ops:
  2.3 13.5 %collective-permute-start = (bf16[34,32,128]{2,1,0:T(8,128)(2,1)S(1)}, bf16[34,32,128]{2,1,0:T(8,128)(2,1)S(1)}, u32[]{:S(2)}, u32[]{:S(2)}) collective-permute-start(bf16[34,32,128]{2,1,0:T(8,128)(2,1)S(1)} %get-tuple-element.53), channel_id=1, source_target_pairs={{0,4},{4,0},{8,12},{12,8},{1,5},{5,1},{9,13},{13,9},{2,6},{6,2},{1... | collective-permute-start | bytes 835592 | tf_op jit(solution)/shard_map/ppermute | solution.py:1026
  5.4 35.9 %collective-permute-start.5 = (bf16[2,2,16,4096]{3,2,1,0:T(8,128)(2,1)S(1)}, bf16[2,2,16,4096]{3,2,1,0:T(8,128)(2,1)S(1)}, u32[]{:S(2)}, u32[]{:S(2)}) collective-permute-start(bf16[2,2,16,4096]{3,2,1,0:T(8,128)(2,1)S(1)} %get-tuple-element.47.refs_7_.refs_0_), channel_id=1, source_target_pairs={{4,8},{8,4},{5,9},{9,5},{6,10},{10,6},{7,11},{11,7},{20,24},{24,20... | collective-permute-start | bytes 1572872 | tf_op jit(solution)/shard_map/ppermute | solution.py:1027
  7.5 10.8 %collective-permute-start.1 = (bf16[33,32,128]{2,1,0:T(8,128)(2,1)S(1)}, bf16[33,32,128]{2,1,0:T(8,128)(2,1)S(1)}, u32[]{:S(2)}, u32[]{:S(2)}) collective-permute-start(bf16[33,32,128]{2,1,0:T(8,128)(2,1)S(1)} %tie.5), channel_id=1, source_target_pairs={{0,4},{4,0},{8,12},{12,8},{1,5},{5,1},{9,13},{13,9},{2,6},{6,2},{1... | collective-permute-start | bytes 811016 | tf_op jit(solution)/shard_map/ppermute | solution.py:1031
  19.1 16.9 %collective-permute-start.2 = (bf16[128,1152]{1,0:T(8,128)(2,1)S(1)}, bf16[128,1152]{1,0:T(8,128)(2,1)S(1)}, u32[]{:S(2)}, u32[]{:S(2)}) collective-permute-start(bf16[128,1152]{1,0:T(8,128)(2,1)S(1)} %value.5.refs_0_.refs_2_.refs_1_), channel_id=1, source_target_pairs={{0,8},{4,12},{8,0},{12,4},{1,9},{5,13},{9,1},{13,5},{2,10},{6,14},... | collective-permute-start | bytes 884744 | tf_op jit(solution)/shard_map/ppermute | solution.py:1066
  34.1 14.8 %collective-permute-start.4 = (bf16[2,16,4096]{2,1,0:T(8,128)(2,1)S(1)}, bf16[2,16,4096]{2,1,0:T(8,128)(2,1)S(1)}, u32[]{:S(2)}, u32[]{:S(2)}) collective-permute-start(bf16[2,16,4096]{2,1,0:T(8,128)(2,1)S(1)} %tie.7), channel_id=1, source_target_pairs={{0,4},{4,0},{8,12},{12,8},{1,5},{5,1},{9,13},{13,9},{2,6},{6,2},{1... | collective-permute-start | bytes 786440 | tf_op jit(solution)/shard_map/ppermute | solution.py:1067
  35.7 13.1 %collective-permute-start.3 = (bf16[128,1024]{1,0:T(8,128)(2,1)S(1)}, bf16[128,1024]{1,0:T(8,128)(2,1)S(1)}, u32[]{:S(2)}, u32[]{:S(2)}) collective-permute-start(bf16[128,1024]{1,0:T(8,128)(2,1)S(1)} %tie.6.refs_2_), channel_id=1, source_target_pairs={{0,8},{4,12},{8,0},{12,4},{1,9},{5,13},{9,1},{13,5},{2,10},{6,14},... | collective-permute-start | bytes 786440 | tf_op jit(solution)/shard_map/ppermute | solution.py:1066
  40.4 22.7 %collective-permute-start.7 = (bf16[128,1024]{1,0:T(8,128)(2,1)S(1)}, bf16[128,1024]{1,0:T(8,128)(2,1)S(1)}, u32[]{:S(2)}, u32[]{:S(2)}) collective-permute-start(bf16[128,1024]{1,0:T(8,128)(2,1)S(1)} %combine.2.refs_0_), channel_id=1, source_target_pairs={{0,4},{4,0},{8,12},{12,8},{1,5},{5,1},{9,13},{13,9},{2,6},{6,2},{1... | collective-permute-start | bytes 786440 | tf_op jit(solution)/shard_map/ppermute | solution.py:1070
  49.3 17.2 %collective-permute-start.6 = (bf16[128,1024]{1,0:T(8,128)(2,1)S(1)}, bf16[128,1024]{1,0:T(8,128)(2,1)S(1)}, u32[]{:S(2)}, u32[]{:S(2)}) collective-permute-start(bf16[128,1024]{1,0:T(8,128)(2,1)S(1)} %combine.3.refs_0_), channel_id=1, source_target_pairs={{0,4},{4,0},{8,12},{12,8},{1,5},{5,1},{9,13},{13,9},{2,6},{6,2},{1... | collective-permute-start | bytes 786440 | tf_op jit(solution)/shard_map/ppermute | solution.py:1075
  50.2 33.0 %collective-permute-start.12 = (bf16[2,2,16,4096]{3,2,1,0:T(8,128)(2,1)S(1)}, bf16[2,2,16,4096]{3,2,1,0:T(8,128)(2,1)S(1)}, u32[]{:S(2)}, u32[]{:S(2)}) collective-permute-start(bf16[2,2,16,4096]{3,2,1,0:T(8,128)(2,1)S(1)} %tie.8), channel_id=1, source_target_pairs={{0,8},{4,12},{8,0},{12,4},{1,9},{5,13},{9,1},{13,5},{2,10},{6,14},... | collective-permute-start | bytes 1572872 | tf_op jit(solution)/shard_map/ppermute | solution.py:1072
  52.1 31.1 %collective-permute-start.13 = (bf16[2,2,16,4096]{3,2,1,0:T(8,128)(2,1)S(1)}, bf16[2,2,16,4096]{3,2,1,0:T(8,128)(2,1)S(1)}, u32[]{:S(2)}, u32[]{:S(2)}) collective-permute-start(bf16[2,2,16,4096]{3,2,1,0:T(8,128)(2,1)S(1)} %tie.9), channel_id=1, source_target_pairs={{0,12},{12,0},{1,13},{13,1},{2,14},{14,2},{3,15},{15,3},{16,28},{2... | collective-permute-start | bytes 1572872 | tf_op jit(solution)/shard_map/ppermute | solution.py:1073
  67.3 1.6 %collective-permute-start.10 = (bf16[2,32,2048]{2,1,0:T(8,128)(2,1)S(1)}, bf16[2,32,2048]{2,1,0:T(8,128)(2,1)S(1)}, u32[]{:S(2)}, u32[]{:S(2)}) collective-permute-start(bf16[2,32,2048]{2,1,0:T(8,128)(2,1)S(1)} %get-tuple-element.80), channel_id=1, source_target_pairs={{0,1},{1,0},{2,3},{3,2},{4,5},{5,4},{6,7},{7,6},{8,9},{9,8},{10,11... | collective-permute-start | bytes 786440 | tf_op jit(solution)/shard_map/ppermute | solution.py:953
  68.2 2.3 %collective-permute-start.8 = (bf16[2,32,2048]{2,1,0:T(8,128)(2,1)S(1)}, bf16[2,32,2048]{2,1,0:T(8,128)(2,1)S(1)}, u32[]{:S(2)}, u32[]{:S(2)}) collective-permute-start(bf16[2,32,2048]{2,1,0:T(8,128)(2,1)S(1)} %get-tuple-element.76), channel_id=1, source_target_pairs={{0,1},{1,0},{2,3},{3,2},{4,5},{5,4},{6,7},{7,6},{8,9},{9,8},{10,11... | collective-permute-start | bytes 786440 | tf_op jit(solution)/shard_map/ppermute | solution.py:953
  69.0 6.4 %collective-permute-start.11 = (bf16[32,2048]{1,0:T(8,128)(2,1)S(1)}, bf16[32,2048]{1,0:T(8,128)(2,1)S(1)}, u32[]{:S(2)}, u32[]{:S(2)}) collective-permute-start(bf16[32,2048]{1,0:T(8,128)(2,1)S(1)} %get-tuple-element.82), channel_id=1, source_target_pairs={{0,2},{1,3},{2,0},{3,1},{4,6},{5,7},{6,4},{7,5},{8,10},{9,11},{10,... | collective-permute-start | bytes 393224 | tf_op jit(solution)/shard_map/ppermute | solution.py:966
  70.6 6.8 %collective-permute-start.9 = (bf16[32,2048]{1,0:T(8,128)(2,1)S(1)}, bf16[32,2048]{1,0:T(8,128)(2,1)S(1)}, u32[]{:S(2)}, u32[]{:S(2)}) collective-permute-start(bf16[32,2048]{1,0:T(8,128)(2,1)S(1)} %get-tuple-element.78), channel_id=1, source_target_pairs={{0,2},{1,3},{2,0},{3,1},{4,6},{5,7},{6,4},{7,5},{8,10},{9,11},{10,... | collective-permute-start | bytes 393224 | tf_op jit(solution)/shard_map/ppermute | solution.py:966
